TPU v7x, 32 devices: a whole 2x2x4 slice. The times are simulated.
32 devices in a mesh: batch: 8 (over z, x), seq: 4 (over y, core).
Axes of the slice: x: 2, y: 2, z: 4, core: 2. Of those that a mesh axis runs over, the one named last changes fastest.
Arguments:
- hidden_in: float32 [32, 512, 768], P('batch', 'seq'), may hold values from -6 to 6
- doc_lengths: int32 [32, 8], P('batch'), may hold values from 1 to 505, as said below
- bias_table: float32 [32, 12], replicated, may hold values from -4 to 4
- gain_attn: bfloat16 [768], P('batch'), may hold values from 0.099609375 to 1.8984375
- gain_ffn: bfloat16 [768], P('batch'), may hold values from 0.099609375 to 1.8984375
- w_query: bfloat16 [768, 768], P('batch'), may hold values from -0.0546875 to 0.0546875
- w_key: bfloat16 [768, 768], P('batch'), may hold values from -0.21875 to 0.21875
- w_value: bfloat16 [768, 768], P('batch'), may hold values from -0.21875 to 0.21875
- w_out: bfloat16 [768, 768], P('batch'), may hold values from -1.25 to 1.25
- w_in: bfloat16 [768, 3072], P('batch'), may hold values from -0.21875 to 0.21875
- w_down: bfloat16 [3072, 768], P('batch'), may hold values from -0.109375 to 0.109375
- out_grad: float32 [32, 512, 768], P('batch', 'seq'), may hold values from -6 to 6
Outputs:
- out_hidden: float32 [32, 512, 768], P('batch', 'seq')
- in_grad: float32 [32, 512, 768], P('batch', 'seq')
- table_grad: float32 [32, 12], replicated
- gain_attn_grad: float32 [768], P(('batch', 'seq'))
- gain_ffn_grad: float32 [768], P(('batch', 'seq'))
- w_query_grad: float32 [768, 768], P(('batch', 'seq'))
- w_key_grad: float32 [768, 768], P(('batch', 'seq'))
- w_value_grad: float32 [768, 768], P(('batch', 'seq'))
- w_out_grad: float32 [768, 768], P(('batch', 'seq'))
- w_in_grad: float32 [768, 3072], P(('batch', 'seq'))
- w_down_grad: float32 [3072, 768], P(('batch', 'seq'))
Inputs may be any that keep to these rules, and one draw needn't show every extreme that they name: `doc_lengths`: each row's 8 lengths are positive and sum to 512; in every aligned block of 4 rows one row holds a document of the most length.
All inputs are finite; a program needn't handle non-finite values.
Results may differ from a plain program's by a relative error of at most 0.035.
Values may be sent and summed in bfloat16 or wider, within the bound.
No kernel may reach another device: no remote copies, remote signals or barrier semaphores. Data moves between devices by JAX's collectives and lax.ppermute only.
A program may use at most 192 MiB of HBM per device.

v0:
```python
import functools

import jax
import jax.numpy as jnp
from jax import lax
from jax.experimental import pallas as pl
from jax.experimental.pallas import tpu as pltpu
from jax.sharding import PartitionSpec as P

HEADS = 12
HEAD_DIM = 64
BUCKETS = 32
TILE = 128

EPS = 1e-06
THRESHOLDS = (12, 16, 23, 32, 46, 64, 91)
HIGHEST = lax.Precision.HIGHEST
F32 = jnp.float32
BF16 = jnp.bfloat16
VMEM_LIMIT = 56 * 1024 * 1024


def bucket_of(offsets):
    distance = jnp.abs(offsets)
    stepped = jnp.full_like(distance, 8)
    for threshold in THRESHOLDS:
        stepped = stepped + (distance >= threshold).astype(jnp.int32)
    closer = jnp.where(distance < 8, distance, stepped)
    return closer + 16 * (offsets > 0).astype(jnp.int32)


def nn(left, right):
    return lax.dot_general(left, right, (((1,), (0,)), ((), ())), preferred_element_type=F32)


def nt(left, right):
    return lax.dot_general(left, right, (((1,), (1,)), ((), ())), preferred_element_type=F32)


def tn(left, right):
    return lax.dot_general(left, right, (((0,), (0,)), ((), ())), preferred_element_type=F32)


def params(**kw):
    return pltpu.CompilerParams(vmem_limit_bytes=VMEM_LIMIT, **kw)


def cost(microseconds):
    return pl.CostEstimate(flops=int(microseconds * 1e9), bytes_accessed=int(microseconds * 3.5e6), transcendentals=0)


def pack_kernel(where, hidden_ref, grad_ref, keep_ref, mate_ref, away_ref):
    for rel in range(4):
        row = where[1] ^ rel
        target = (keep_ref, mate_ref, away_ref.at[0], away_ref.at[1])[rel]
        target[0] = hidden_ref[row].astype(BF16)
        target[1] = grad_ref[row].astype(BF16)


def unpack_kernel(where, old_ref, keep_ref, mate_ref, away_ref, far_ref, new_ref):
    for rel in range(4):
        row = where[1] ^ rel
        source = (keep_ref[...], mate_ref[...], away_ref[0], far_ref[...])[rel]
        new_ref[row] = old_ref[row] + source.astype(F32)


def place_rows(where, value, keep_ref, mate_ref, away_ref, hold_ref):
    size = keep_ref.shape[0]
    hold_ref[...] = value.astype(BF16).reshape(4, size, value.shape[1])
    for rel in range(4):
        target = (keep_ref, mate_ref, away_ref.at[0], away_ref.at[1])[rel]
        target[...] = hold_ref[where[1] ^ rel]


def fill(where, pieces, out, rows_last):
    b, s = where[0], where[1]
    parts, shards = (out.shape[1], out.shape[0]) if rows_last else (out.shape[0], out.shape[1])
    for ref, flip, base in pieces:
        core = (s ^ flip) % 2
        part = (s ^ flip) if parts == 4 else core
        for i in range(ref.shape[0]):
            t = b ^ where[2 + core * shards + base + i]
            if rows_last:
                out[t, part] = ref[i]
            else:
                out[part, t] = ref[i]


def flat(ref):
    return ref[...].reshape(-1, ref.shape[-1])


def weight_kernel(pattern, rows_last, where, *refs):
    fill(where, [(ref, *entry) for ref, entry in zip(refs, pattern)], refs[-1], rows_last)


def columns_of(w_ref, start, stop):
    size = w_ref.shape[-1]
    pieces = []
    for p in range(w_ref.shape[0]):
        low, high = max(start, p * size), min(stop, (p + 1) * size)
        if low < high:
            value = w_ref[p, :, :, low - p * size : high - p * size]
            pieces.append((value.reshape(-1, high - low), low - start))
    return pieces


def times_columns(left, w_ref, start, stop):
    return jnp.concatenate([nn(left, value) for value, _ in columns_of(w_ref, start, stop)], axis=1)


def times_transposed(left, w_ref, start, stop):
    out = None
    for value, low in columns_of(w_ref, start, stop):
        term = nt(left[:, low : low + value.shape[1]], value)
        out = term if out is None else out + term
    return out


def prepare_kernel(where, lengths, table, position_ref, band_ref, segq_ref, segk_ref, perm_ref):
    s = where[1]
    shape = segq_ref.shape
    token = lax.broadcasted_iota(jnp.int32, shape, 0)
    lane = lax.broadcasted_iota(jnp.int32, shape, 1)
    segment = jnp.zeros(shape, jnp.int32)
    end = 0
    for j in range(lengths.shape[1]):
        end = end + lengths[s, j]
        segment = segment + (token >= end).astype(jnp.int32)
    same = lane == segment
    segq_ref[...] = jnp.where(same, 1.0, 0.0).astype(BF16)
    segk_ref[...] = jnp.where(same | (lane >= lengths.shape[1]), 0.0, -1e30).astype(BF16)
    offset = lax.broadcasted_iota(jnp.int32, (8, 3 * TILE), 1) - TILE
    bucket = bucket_of(offset)
    near = (TILE, 3 * TILE)
    outside = lax.broadcasted_iota(jnp.int32, near, 1) < lax.broadcasted_iota(jnp.int32, near, 0)
    for h in range(band_ref.shape[0]):
        base = jnp.zeros((8, 3 * TILE), F32)
        for i in range(BUCKETS):
            base = jnp.where(bucket == i, table[i, h], base)
        rows = pltpu.roll(jnp.broadcast_to(base[:1], near), 0, 1, stride=1, stride_axis=0)
        band_ref[h] = jnp.where(outside, table[15, h], rows)
    position = lax.broadcasted_iota(jnp.int32, perm_ref.shape, 0)
    perm_ref[...] = jnp.where(position == position_ref[...], 1.0, 0.0).astype(BF16)


def qkv_kernel(pattern, shard, where, keep_ref, mate_ref, away_ref, far_ref, perm_ref, *refs):
    count = len(pattern) if pattern else 1
    qkv_ref, first_t_ref, x_ref, glow_ref, gains_ref = refs[count : count + 5]
    w_ref = refs[count + 5] if pattern else refs[0]
    if pattern:
        fill(where, [(ref, *entry) for ref, entry in zip(refs, pattern)], w_ref, False)
    size = keep_ref.shape[1]
    width = keep_ref.shape[2]
    for rel in range(4):
        block = where[1] ^ rel
        source = (keep_ref, mate_ref, away_ref.at[0], far_ref)[rel]
        x_ref[block] = source[0]
        glow_ref[block] = source[1]
    gains = gains_of(w_ref, width, shard)
    gains_ref[...] = gains
    x = x_ref[...].reshape(4 * size, width).astype(F32)
    r1 = lax.rsqrt(jnp.mean(x * x, axis=-1, keepdims=True) + EPS)
    first = (x * r1 * gains[:1]).astype(BF16)
    for value, low in columns_of(w_ref, 0, 3 * width):
        qkv_ref[:, low : low + value.shape[1]] = nn(first, value).astype(BF16)
    first_t_ref[...] = nt(perm_ref[...], first).astype(BF16)


def gains_of(w_ref, width, shard):
    size = w_ref.shape[-1]
    spare = w_ref[4 * width // size, :, :, 4 * width % size : 4 * width % size + TILE].astype(F32)
    rows = width // TILE
    if spare.shape[0] > 1:
        together = jnp.sum(spare, axis=0)
        found = [together[k : k + 1] for k in range(2 * rows)]
    else:
        spare = spare.reshape(-1, TILE)
        row = lax.broadcasted_iota(jnp.int32, spare.shape, 0) % shard
        found = [jnp.sum(jnp.where(row == k, spare, 0.0), axis=0, keepdims=True) for k in range(2 * rows)]
    return jnp.concatenate([jnp.concatenate(found[:rows], axis=1), jnp.concatenate(found[rows:], axis=1)], axis=0)


CHUNK = 32


def attention_kernel(first_pair, q_ref, k_ref, v_ref, band_ref, table_ref, segq_ref, segk_ref, probs_ref, ctx_ref, s_ref):
    pair = pl.program_id(0) + first_pair
    length = q_ref.shape[0]
    tiles = length // TILE
    q, v = q_ref[...], v_ref[...]
    lane = lax.broadcasted_iota(jnp.int32, q.shape, 1)
    keys = jnp.concatenate([k_ref[...], segk_ref[...]], axis=1)
    halves = []
    for h in range(2):
        mine = (lane < HEAD_DIM) if h == 0 else (lane >= HEAD_DIM)
        queries = jnp.concatenate([jnp.where(mine, q, jnp.zeros_like(q)), segq_ref[...]], axis=1)
        s_ref[h] = nt(queries, keys)
    for h in range(2):
        below = table_ref[15, 2 * pair + h]
        above = table_ref[31, 2 * pair + h]
        for r in range(0, length, CHUNK):
            t = r // TILE
            parts = []
            for u in range(tiles):
                d = u - t
                part = s_ref[h, r : r + CHUNK, u * TILE : (u + 1) * TILE]
                if abs(d) <= 1:
                    part = part + band_ref[h, r - t * TILE : r - t * TILE + CHUNK, (d + 1) * TILE : (d + 2) * TILE]
                else:
                    part = part + (above if d > 0 else below)
                parts.append(part)
            s = jnp.concatenate(parts, axis=1)
            p = jnp.exp(s - jnp.max(s, axis=-1, keepdims=True))
            p = p * (1.0 / jnp.sum(p, axis=-1, keepdims=True))
            probs_ref[h, r : r + CHUNK, :] = p.astype(BF16)
        halves.append(nn(probs_ref[h], v))
    ctx_ref[...] = jnp.where(lane < HEAD_DIM, halves[0], halves[1]).astype(BF16)


def out_kernel(x_ref, ctx_a_ref, ctx_b_ref, w_ref, gains_ref, perm_ref, attn_ref, second_ref, second_t_ref):
    width = x_ref.shape[1]
    ctx = jnp.concatenate([ctx_a_ref[...], ctx_b_ref[...]], axis=1)
    attn = times_columns(ctx, w_ref, 3 * width, 4 * width)
    attn_ref[...] = attn
    middle = x_ref[...].astype(F32) + attn
    r2 = lax.rsqrt(jnp.mean(middle * middle, axis=-1, keepdims=True) + EPS)
    second = (middle * r2 * gains_ref[1:]).astype(BF16)
    second_ref[...] = second
    second_t_ref[...] = nt(perm_ref[...], second).astype(BF16)


def up_kernel(pattern, place, where, second_ref, glow_ref, *refs):
    if pattern:
        w_ref = refs[-1]

        @pl.when(pl.program_id(0) == 0)
        def _():
            fill(where, [(ref, *entry) for ref, entry in zip(refs, pattern)], w_ref, False)

        weight = w_ref[pl.program_id(0)]
        act_ref, slope_ref, keep_ref, send_ref = refs[len(pattern) : len(pattern) + 4]
        weight = weight.reshape(-1, weight.shape[-1])
    else:
        weight = flat(refs[0])
        act_ref, slope_ref, keep_ref, send_ref = refs[1:]
    up = nn(second_ref[...], weight)
    phi_cap = 0.5 * (1.0 + lax.erf(up * 0.7071067811865476))
    act = (up * phi_cap).astype(BF16)
    act_ref[...] = act
    slope = phi_cap + up * (jnp.exp(-0.5 * up * up) * 0.3989422804014327)
    slope_ref[...] = slope.astype(BF16)
    dwd = tn(act, glow_ref[...])
    if len(keep_ref.shape) == 2:
        keep_ref[...] = dwd.astype(BF16)
    else:
        rows = keep_ref.shape[-2]
        blocks = [dwd[i * rows : (i + 1) * rows].astype(BF16) for i in range(8)]
        for axis, bit in ((1, 4), (2, 2), (3, 1)):
            flip = place[axis] == 1
            blocks = [jnp.where(flip, blocks[i ^ bit], blocks[i]) for i in range(8)]
        core = place[3]
        for ref, c_rel in ((keep_ref, 0), (send_ref, 1)):
            x_outer = core == c_rel
            for i in range(2):
                for j in range(2):
                    one, other = blocks[4 * i + 2 * j + c_rel], blocks[4 * j + 2 * i + c_rel]
                    ref[i, j, 0, 0] = one if i == j else jnp.where(x_outer, one, other)


def down_kernel(pattern, where, second_t_ref, glow_ref, attn_ref, act_ref, slope_ref, win_ref, *refs):
    j = pl.program_id(0)
    win = flat(win_ref)
    count = len(pattern) if pattern else 1
    keep_ref, mate_ref, away_ref, dsec_ref, win_keep_ref, win_send_ref, acc_ref, dacc_ref, hold_ref = refs[count : count + 9]
    if pattern:
        w_ref = refs[-1]

        @pl.when(j == 0)
        def _():
            fill(where, [(ref, *entry) for ref, entry in zip(refs, pattern)], w_ref, True)

        shards = w_ref.shape[0] // 4
        wd = w_ref[pl.ds(j * shards, shards)]
        wd = wd.reshape(-1, wd.shape[-1])
    else:
        wd = flat(refs[0])
    gup = (nt(glow_ref[...], wd) * slope_ref[...].astype(F32)).astype(BF16)
    out = nn(act_ref[...], wd)
    dsec = nt(gup, win)

    @pl.when(j == 0)
    def _():
        acc_ref[...] = attn_ref[...] + out
        dacc_ref[...] = dsec

    @pl.when(j > 0)
    def _():
        acc_ref[...] += out
        dacc_ref[...] += dsec

    @pl.when(j == pl.num_programs(0) - 1)
    def _():
        place_rows(where, acc_ref[...], keep_ref, mate_ref, away_ref, hold_ref)
        dsec_ref[...] = dacc_ref[...]

    dwin = nn(second_t_ref[...], gup).astype(BF16)
    half = dwin.shape[0] // 2
    win_keep_ref[...] = dwin[:half]
    win_send_ref[...] = dwin[half:]


def mid_kernel(
    x_ref, attn_ref, gains_ref, dsec_ref, glow_ref, ctx_a_ref, ctx_b_ref, perm_ref, w_ref,
    gmd_ref, g2_ref, dctx_ref, keep_ref, send_ref,
):
    middle = x_ref[...].astype(F32) + attn_ref[...]
    r2 = lax.rsqrt(jnp.mean(middle * middle, axis=-1, keepdims=True) + EPS)
    normed = middle * r2
    dsec = dsec_ref[...]
    g2_ref[...] = jnp.sum(dsec * normed, axis=0, keepdims=True)
    scaled = dsec * gains_ref[1:]
    gmd = r2 * (scaled - normed * jnp.mean(scaled * normed, axis=-1, keepdims=True))
    gmd_ref[...] = gmd
    low = (glow_ref[...].astype(F32) + gmd).astype(BF16)
    dctx_ref[...] = times_transposed(low, w_ref, 3 * low.shape[1], 4 * low.shape[1]).astype(BF16)
    ctx_t = nt(perm_ref[...], jnp.concatenate([ctx_a_ref[...], ctx_b_ref[...]], axis=1)).astype(BF16)
    dw = nn(ctx_t, low).astype(BF16)
    half = dw.shape[0] // 2
    keep_ref[...] = dw[:half]
    send_ref[...] = dw[half:]


def back_kernel(q_ref, k_ref, v_ref, dctx_ref, ctx_ref, probs_ref, dq_ref, dk_ref, dv_ref, sums_ref, ds_ref, dp_ref, near_ref):
    length = q_ref.shape[0]
    tiles = length // TILE
    q, k, v, dctx = q_ref[...], k_ref[...], v_ref[...], dctx_ref[...]
    lane = lax.broadcasted_iota(jnp.int32, (length, TILE), 1)
    product = dctx.astype(F32) * ctx_ref[...].astype(F32)
    square = lambda axis: lax.broadcasted_iota(jnp.int32, (TILE, TILE), axis)
    turn = (square(0) + square(1) == TILE - 1).astype(F32)
    row = lax.broadcasted_iota(jnp.int32, (TILE, 3 * TILE), 0)
    column = lax.broadcasted_iota(jnp.int32, (TILE, 3 * TILE), 1)
    dqs, dk, dv = [], None, None

    def put(old, new):
        return new if old is None else old + new

    masked = []
    for h in range(2):
        mine = (lane < HEAD_DIM) if h == 0 else (lane >= HEAD_DIM)
        do = jnp.where(mine, dctx, jnp.zeros_like(dctx))
        dp_ref[h] = nt(do, v)
        masked.append((mine, do))
    for h in range(2):
        mine, do = masked[h]
        delta = jnp.sum(jnp.where(mine, product, 0.0), axis=-1, keepdims=True)
        far = [None, None]
        for start in range(0, TILE, CHUNK):
            band = [None, None, None]
            for t in range(tiles):
                rows = slice(t * TILE + start, t * TILE + start + CHUNK)
                ds = probs_ref[h, rows, :].astype(F32) * (dp_ref[h, rows, :] - delta[rows])
                ds_ref[h, rows, :] = ds.astype(BF16)
                for u in range(tiles):
                    d = u - t
                    part = ds[:, u * TILE : (u + 1) * TILE]
                    if abs(d) <= 1:
                        band[d + 1] = put(band[d + 1], part)
                    else:
                        far[int(d > 0)] = put(far[int(d > 0)], part)
            near_ref[start : start + CHUNK, :] = jnp.concatenate(band, axis=1)
        near = near_ref[...]
        outside = jnp.where(column < row, near, 0.0)
        near = jnp.where(column < row, 0.0, near)
        near = lax.dot_general(turn, near, (((1,), (0,)), ((), ())), precision=HIGHEST, preferred_element_type=F32)
        near = pltpu.roll(near, 0, 1, stride=1, stride_axis=0)
        sums_ref[0, h : h + 1, :] = jnp.sum(near, axis=0, keepdims=True)
        sums_ref[0, 2 + h : 3 + h, :] = jnp.sum(outside, axis=0, keepdims=True)
        for i in range(2):
            sums_ref[0, 4 + 2 * i + h : 5 + 2 * i + h, :TILE] = jnp.sum(far[i], axis=0, keepdims=True)
            sums_ref[0, 4 + 2 * i + h : 5 + 2 * i + h, TILE:] = jnp.zeros((1, 2 * TILE), F32)
        dqs.append(nn(ds_ref[h], k))
        dk = put(dk, tn(ds_ref[h], jnp.where(mine, q, jnp.zeros_like(q))))
        dv = put(dv, tn(probs_ref[h], do))
    dq_ref[...] = jnp.where(lane < HEAD_DIM, dqs[0], dqs[1]).astype(BF16)
    dk_ref[...] = dk.astype(BF16)
    dv_ref[...] = dv.astype(BF16)


def grad_kernel(dqa_ref, dqb_ref, dka_ref, dkb_ref, dva_ref, dvb_ref, first_t_ref, keep_ref, send_ref):
    refs = (dqa_ref, dqb_ref, dka_ref, dkb_ref, dva_ref, dvb_ref)
    dw = nn(first_t_ref[...], jnp.concatenate([ref[...] for ref in refs], axis=1)).astype(BF16)
    half = dw.shape[0] // 2
    keep_ref[...] = dw[:half]
    send_ref[...] = dw[half:]


def first_kernel(
    where, x_ref, gains_ref, dqa_ref, dqb_ref, dka_ref, dkb_ref, dva_ref, dvb_ref, w_ref, gmd_ref,
    row_keep_ref, row_mate_ref, row_away_ref, g1_ref, hold_ref,
):
    width = x_ref.shape[1]
    x = x_ref[...].astype(F32)
    r1 = lax.rsqrt(jnp.mean(x * x, axis=-1, keepdims=True) + EPS)
    normed = x * r1
    refs = (dqa_ref, dqb_ref, dka_ref, dkb_ref, dva_ref, dvb_ref)
    dfirst = times_transposed(jnp.concatenate([ref[...] for ref in refs], axis=1), w_ref, 0, 3 * width)
    g1_ref[...] = jnp.sum(dfirst * normed, axis=0, keepdims=True)
    scaled = dfirst * gains_ref[:1]
    delta = gmd_ref[...] + r1 * (scaled - normed * jnp.mean(scaled * normed, axis=-1, keepdims=True))
    place_rows(where, delta, row_keep_ref, row_mate_ref, row_away_ref, hold_ref)


def shape(dims, dtype):
    return jax.ShapeDtypeStruct(tuple(dims), dtype)


def after(value, *earlier):
    return lax.optimization_barrier((value,) + earlier)[0]


def total(*parts):
    sums = parts[0].astype(F32)
    for part in parts[1:]:
        sums = sums + part.astype(F32)
    return sums


def on_device(
    nb, ns, hidden_in, doc_lengths, bias_table, gain_attn, gain_ffn,
    w_query, w_key, w_value, w_out, w_in, w_down, out_grad,
):
    rows_dev, shard_len, width = hidden_in.shape
    length = ns * shard_len
    ff = w_in.shape[1]
    shard = w_query.shape[0]
    b, s = lax.axis_index("batch"), lax.axis_index("seq")
    y, c = s // 2, s % 2
    bits = [1 << i for i in range(1, nb.bit_length() - 1)]
    gather_order = ([1] + bits[::-1], bits[::-1] + [1])

    def masks(core):
        value = [0]
        for bit in gather_order[core]:
            value = value + [old ^ bit for old in value]
        return value

    where = jnp.concatenate([jnp.stack([b, s]), jnp.array(masks(0) + masks(1))]).astype(jnp.int32)

    def move(value, first, second=None):
        pairs = []
        for i in range(nb):
            for j in range(ns):
                bm, sm = second if second is not None and j % 2 else first
                pairs.append((i * ns + j, (i ^ bm) * ns + (j ^ sm)))
        return lax.ppermute(value, ("batch", "seq"), pairs)

    core = lambda value: move(value, (0, 1))
    other_y = lambda value: move(value, (0, 2))

    def piece(weight, parts, axis=1):
        size = weight.shape[axis] // parts
        return lax.dynamic_slice_in_dim(weight, (c if parts == 2 else s) * size, size, axis)[None]

    def step(block, i):
        return move(block, (gather_order[0][i], 0), (gather_order[1][i], 0))

    tiled = (shard // 2) % 16 == 0

    def plain(pieces, rows_last=False):
        parts = 4 if any(entry[1] > 1 for entry in pieces) else 2
        dims = pieces[0][0].shape[1:]
        full = jnp.zeros((parts, nb) + dims, BF16)
        for array, flip, base in pieces:
            part = s ^ flip if parts == 4 else (s ^ flip) % 2
            shards = b ^ jnp.where((s ^ flip) % 2 == 0, jnp.array(masks(0)), jnp.array(masks(1)))
            full = full.at[part, shards[base : base + array.shape[0]]].set(array)
        if rows_last:
            return jnp.swapaxes(full, 0, 1)
        return full.reshape(parts, 1, nb * dims[0], dims[1])

    def assemble(name, pieces, rows_last=False):
        if not tiled:
            return plain(pieces, rows_last)
        arrays = [entry[0] for entry in pieces]
        parts = 4 if any(entry[1] > 1 for entry in pieces) else 2
        return pl.pallas_call(
            functools.partial(weight_kernel, [entry[1:] for entry in pieces], rows_last),
            name=name,
            out_shape=shape(((nb, parts) if rows_last else (parts, nb)) + arrays[0].shape[1:], BF16),
            in_specs=[smem] + [vmem] * len(arrays),
            cost_estimate=cost(5),
            compiler_params=params(),
        )(where, *arrays)

    vmem = pl.BlockSpec(memory_space=pltpu.VMEM)
    smem = pl.BlockSpec(memory_space=pltpu.SMEM)
    stages = len(bits) + 1

    def grow(block, start, stop, *gates):
        for i in range(start, stop):
            block = jnp.concatenate([block, after(step(block, i), *gates)])
        return block

    per = width // (nb * ns)
    feature = jnp.arange(width)
    fb, fs, fr = feature // (per * ns), feature // per % ns, feature % per
    b_rel, s_rel = fb ^ b, fs ^ s
    x_rel, y_rel = b_rel % 2, s_rel // 2
    swapped = fs % 2 == 1
    position = (s_rel % 2) * 2 + jnp.where(swapped, y_rel, x_rel)
    position = position * 2 + jnp.where(swapped, x_rel, y_rel)
    for bit in bits:
        position = position * 2 + (b_rel & bit) // bit
    position = (position * per + fr).reshape(1, width)

    own = jnp.zeros((2, width), BF16)
    own = lax.dynamic_update_slice(own, jnp.stack([gain_attn, gain_ffn]), (0, b * shard)).reshape(-1, TILE)
    own = jnp.pad(own, ((0, shard - own.shape[0]), (0, TILE)))
    block1 = piece(jnp.concatenate([w_query, w_key, w_value, w_out, own], axis=1), 2)
    row_keep, row_mate, row_away = pl.pallas_call(
        pack_kernel,
        name="pack",
        out_shape=(
            shape((2, shard_len, width), BF16), shape((2, shard_len, width), BF16), shape((2, 2, shard_len, width), BF16),
        ),
        in_specs=[smem, vmem, vmem],
        cost_estimate=cost(3),
        compiler_params=params(),
    )(where, hidden_in, out_grad)
    row_got = other_y(row_away)
    band, seg_queries, seg_keys, perm = pl.pallas_call(
        prepare_kernel,
        name="prepare",
        out_shape=(
            shape((HEADS, TILE, 3 * TILE), F32), shape((length, TILE), BF16), shape((length, TILE), BF16),
            shape((width, width), BF16),
        ),
        in_specs=[smem, smem, smem, vmem],
        cost_estimate=cost(6),
        compiler_params=params(),
    )(where, doc_lengths, bias_table, position)
    start1 = grow(block1, 0, 1)
    low1 = grow(start1, 1, stages - 1, row_got, band)
    high1 = step(low1, stages - 1)
    row_mate, row_far = core(row_mate), core(row_got[1])
    low2 = grow(piece(after(w_in, start1), 4), 0, stages - 1)
    high1 = after(high1, low2)
    gather1 = [(low1, 0, 0), (high1, 0, nb // 2), (core(low1), 1, 0), (core(high1), 1, nb // 2)]
    high2 = step(low2, stages - 1)
    y_low2 = other_y(low2)
    block3 = piece(after(w_down, low2), 4, 0)
    gather1[0] = (after(low1, block3), 0, 0)
    row_block = shape((4, shard_len, width), BF16)
    w1_shape = shape((2, nb) + low1.shape[1:], BF16)
    pieces1 = [entry[0] for entry in gather1] if tiled else [plain(gather1)]
    outputs = pl.pallas_call(
        functools.partial(qkv_kernel, [entry[1:] for entry in gather1] if tiled else None, shard),
        name="qkv",
        out_shape=(
            shape((length, 3 * width), BF16), shape((width, length), BF16), row_block, row_block, shape((2, width), F32),
            *([w1_shape] if tiled else []),
        ),
        in_specs=[smem] + [vmem] * (5 + len(pieces1)),
        cost_estimate=cost(9),
        compiler_params=params(),
    )(where, row_keep, row_mate, row_got, row_far, perm, *pieces1)
    qkv, first_t, xb, glow, gains = outputs[:5]
    w1 = outputs[5] if tiled else pieces1[0]
    xb, glow = xb.reshape(length, width), glow.reshape(length, width)

    y_high2 = other_y(after(high2, qkv))
    mid3 = grow(block3, 0, stages - 2, qkv)

    pairs = HEADS // 4
    pair_block = lambda first: pl.BlockSpec((length, TILE), lambda p: (0, first + p))
    head_block = lambda first, *dims: pl.BlockSpec((2,) + dims, lambda p: (first + p,) + (0,) * len(dims))
    whole_block = lambda *dims: pl.BlockSpec(dims, lambda p: (0,) * len(dims))

    def attend(i, gated):
        return pl.pallas_call(
            functools.partial(attention_kernel, i * pairs),
            name="attention",
            grid=(pairs,),
            out_shape=(shape((HEADS // 2, length, length), BF16), shape((length, width // 2), BF16)),
            in_specs=[
                pair_block(i * pairs), pair_block((2 + i) * pairs), pair_block((4 + i) * pairs),
                head_block(i * pairs, TILE, 3 * TILE), smem, whole_block(length, TILE), whole_block(length, TILE),
            ],
            out_specs=(head_block(0, length, length), pair_block(0)),
            scratch_shapes=[pltpu.VMEM((2, length, length), F32)],
            cost_estimate=cost(10),
            compiler_params=params(),
        )(qkv, qkv, qkv, gated, bias_table, seg_queries, seg_keys)

    probs_a, ctx_a = attend(0, after(band, high2, mid3, y_low2))
    low3 = grow(mid3, stages - 2, stages - 1, ctx_a)
    probs_b, ctx_b = attend(1, after(band, low3, y_high2))
    high3 = after(step(low3, stages - 1), ctx_b)
    y_low3 = other_y(after(low3, y_high2))
    y_high3 = other_y(high3)
    gather3 = [
        (low3, 0, 0), (high3, 0, nb // 2), (core(low3), 1, 0), (core(high3), 1, nb // 2),
        (y_low3, 2, 0), (y_high3, 2, nb // 2), (core(y_low3), 3, 0), (core(y_high3), 3, nb // 2),
    ]

    gather2 = [
        (low2, 0, 0), (high2, 0, nb // 2), (core(low2), 1, 0), (core(high2), 1, nb // 2),
        (y_low2, 2, 0), (y_high2, 2, nb // 2),
        (core(after(y_low2, qkv)), 3, 0), (core(after(y_high2, ctx_a)), 3, nb // 2),
    ]
    attn, second, second_t = pl.pallas_call(
        out_kernel,
        name="out",
        out_shape=(shape((length, width), F32), shape((length, width), BF16), shape((width, length), BF16)),
        cost_estimate=cost(5),
        compiler_params=params(),
    )(xb, after(ctx_a, high3), ctx_b, w1, gains, perm)

    steps = 4
    part = ff // steps
    per_down = ff // (nb * ns)
    aligned = nb == 2 * steps and per_down % 16 == 0
    if aligned:

        def wd_index(j, place):
            rel = j ^ place[0]
            return 0, 0, rel % 2, rel // 2, 0, 0

        wd_block = pl.BlockSpec((2, 2, 1, 1, per_down, width), wd_index)
        wd_shape = shape((2, 2, 2, 2, per_down, width), BF16)
        wd_shapes, wd_blocks = (wd_shape, wd_shape), (wd_block, wd_block)
    else:
        wd_shapes = (shape((ff, width), BF16), shape((8, TILE), BF16))
        wd_blocks = (
            pl.BlockSpec((part, width), lambda j, place: (j, 0)),
            pl.BlockSpec((8, TILE), lambda j, place: (0, 0)),
        )
    place = jnp.stack([b // 2, b % 2, y, c]).astype(jnp.int32)
    full = lambda *dims: pl.BlockSpec(dims, lambda j, *place: (0,) * len(dims))
    half = width // 2
    column_block = lambda r: pl.BlockSpec((r, part), lambda j, *place: (0, j))
    win_shape = (4, nb) + low2.shape[1:]
    pieces2 = [entry[0] for entry in gather2] if tiled else [plain(gather2)]
    win_shape = win_shape if tiled else pieces2[0].shape
    win_block = pl.BlockSpec((1,) + win_shape[1:], lambda j, *place: (j, 0, 0, 0))
    always = lambda array: pl.BlockSpec(array.shape, lambda j, *place: (0,) * array.ndim)
    outputs = pl.pallas_call(
        functools.partial(up_kernel, [entry[1:] for entry in gather2] if tiled else None),
        name="up",
        out_shape=(
            shape((length, ff), BF16), shape((length, ff), BF16), *wd_shapes, *([shape(win_shape, BF16)] if tiled else []),
        ),
        grid_spec=pltpu.PrefetchScalarGridSpec(
            num_scalar_prefetch=1,
            grid=(steps,),
            in_specs=[smem, full(length, width), full(length, width)]
            + ([always(array) for array in pieces2] if tiled else [win_block]),
            out_specs=(
                column_block(length), column_block(length), *wd_blocks, *([full(*win_shape)] if tiled else []),
            ),
        ),
        cost_estimate=cost(10),
        compiler_params=params(),
    )(place, where, after(second, y_low3, y_high3), glow, *pieces2)
    act, slope, wd_keep, wd_send = outputs[:4]
    win = outputs[4] if tiled else pieces2[0]

    scatter_masks = [((1, 0), (0, 2)), ((0, 2), (1, 0))] + [((bit, 0), (bit, 0)) for bit in bits]

    class Scatter:
        def __init__(self, *held):
            self.held = list(held)
            self.rows = held[0].shape[0]
            self.i = 0

        def outgoing(self):
            self.sent = total(*[value[self.rows // 2 : self.rows] for value in self.held]).astype(BF16)
            return self.sent

        def send(self):
            self.got = move(self.sent, *scatter_masks[self.i])

        def take(self, *gates):
            self.i += 1
            self.rows //= 2
            self.held.append(after(self.got, *gates))

        def result(self):
            return total(*[value[: self.rows] for value in self.held])

    if not aligned:
        blocks = wd_keep.reshape(nb, ns, per_down, width)

        def order(dest):
            index = jnp.arange(nb * 2)
            digits = [(index >> (stages - i)) % 2 for i in range(stages + 1)]
            x_bit = jnp.where(dest == 0, digits[0], digits[1])
            y_bit = jnp.where(dest == 0, digits[1], digits[0])
            shards = x_bit
            for bit, digit in zip(bits, digits[2:]):
                shards = shards + bit * digit
            return blocks[shards ^ b, 2 * (y_bit ^ y) + dest]

        wd_keep, wd_send = order(c), order(1 - c)
    wd_keep, wd_send = wd_keep.reshape(ff // 2, width), wd_send.reshape(ff // 2, width)
    down = Scatter(wd_keep, core(wd_send))
    down_sent = down.outgoing()
    down.send()

    pieces3 = [entry[0] for entry in gather3] if tiled else [plain(gather3, True)]
    wd_dims = (nb, 4) + low3.shape[1:]
    wd_spec = pl.BlockSpec((nb // steps,) + wd_dims[1:], lambda j: (j, 0, 0, 0))
    row_shapes = (shape((shard_len, width), BF16),) * 2 + (shape((2, shard_len, width), BF16),)
    row_specs = (full(shard_len, width), full(shard_len, width), full(2, shard_len, width))
    hold = pltpu.VMEM((4, shard_len, width), BF16)
    out_keep, out_mate, out_away, dsec, win_keep, win_send = pl.pallas_call(
        functools.partial(down_kernel, [entry[1:] for entry in gather3] if tiled else None),
        name="down",
        grid=(steps,),
        out_shape=(*row_shapes, shape((length, width), F32), shape((half, ff), BF16), shape((half, ff), BF16)),
        in_specs=[
            smem, full(width, length), full(length, width), full(length, width), column_block(length),
            column_block(length), win_block, *([always(array) for array in pieces3] if tiled else [wd_spec]),
        ],
        out_specs=(*row_specs, full(length, width), column_block(half), column_block(half)),
        scratch_shapes=[
            pltpu.VMEM((length, width), F32), pltpu.VMEM((length, width), F32), hold,
            *([pltpu.VMEM(wd_dims, BF16)] if tiled else []),
        ],
        cost_estimate=cost(15),
        compiler_params=params(),
    )(where, second_t, glow, attn, after(act, down_sent), slope, win, *pieces3)
    win_got = core(win_send)
    out_got = other_y(out_away)

    gmd, g2, dctx, wo_keep, wo_send = pl.pallas_call(
        mid_kernel,
        name="mid",
        out_shape=(
            shape((length, width), F32), shape((1, width), F32), shape((length, width), BF16),
            shape((half, width), BF16), shape((half, width), BF16),
        ),
        cost_estimate=cost(7),
        compiler_params=params(),
    )(xb, attn, gains, dsec, glow, ctx_a, ctx_b, perm, w1)
    wo_got = core(wo_send)
    both = Scatter(
        jnp.concatenate([win_keep, wo_keep], axis=1), jnp.concatenate([after(win_got, dctx), wo_got], axis=1)
    )
    both_sent = both.outgoing()
    both.send()
    down.take(both_sent)
    down_sent = down.outgoing()
    down.send()

    def back(i, gated):
        return pl.pallas_call(
            back_kernel,
            name="back",
            grid=(pairs,),
            out_shape=(*(shape((length, width // 2), BF16),) * 3, shape((pairs, 8, 3 * TILE), F32)),
            in_specs=[
                pair_block(i * pairs), pair_block((2 + i) * pairs), pair_block((4 + i) * pairs),
                pair_block(i * pairs), pair_block(0), head_block(0, length, length),
            ],
            out_specs=(*(pair_block(0),) * 3, pl.BlockSpec((1, 8, 3 * TILE), lambda p: (p, 0, 0))),
            scratch_shapes=[
                pltpu.VMEM((2, length, length), BF16), pltpu.VMEM((2, length, length), F32), pltpu.VMEM((TILE, 3 * TILE), F32),
            ],
            cost_estimate=cost(10),
            compiler_params=params(),
        )(qkv, qkv, qkv, gated, (ctx_a, ctx_b)[i], (probs_a, probs_b)[i])

    dq_a, dk_a, dv_a, sums_a = back(0, after(dctx, down_sent, both_sent))
    down.take(dq_a)
    down_sent = down.outgoing()
    down.send()
    dq_b, dk_b, dv_b, sums_b = back(1, after(dctx, down_sent))
    both.take(dq_b)
    both_sent = both.outgoing()
    both.send()
    down.take(dq_b)
    down_sent = down.outgoing()
    down.send()

    grads = (after(dq_a, down_sent, both_sent), dq_b, dk_a, dk_b, dv_a, dv_b)
    keep, send = pl.pallas_call(
        grad_kernel,
        name="grad",
        out_shape=(shape((half, 3 * width), BF16),) * 2,
        cost_estimate=cost(5),
        compiler_params=params(),
    )(*grads, first_t)
    last_got = core(send)
    both.take(send)
    both_sent = both.outgoing()
    both.send()
    in_keep, in_mate, in_away, g1 = pl.pallas_call(
        first_kernel,
        name="first",
        out_shape=(*row_shapes, shape((1, width), F32)),
        in_specs=[smem] + [vmem] * 10,
        scratch_shapes=[hold],
        cost_estimate=cost(6),
        compiler_params=params(),
    )(where, xb, gains, after(grads[0], send, both_sent), *grads[1:], w1, gmd)
    last = Scatter(keep, after(last_got, g1))
    last_sent = last.outgoing()
    last.send()
    both.take(last_sent)
    while both.i < stages + 1:
        both.outgoing()
        both.send()
        both.take()
    op1_sent = last_sent
    in_got = other_y(after(in_away, last_sent))

    sums = jnp.concatenate([sums_a, after(sums_b, last_sent)])
    near = sums[:, :2].reshape(HEADS, 3 * TILE)
    outer = jnp.sum(sums[:, 2:], axis=-1).reshape(HEADS // 2, 3, 2)
    below, above = (outer[:, 0] + outer[:, 1]).reshape(HEADS), outer[:, 2].reshape(HEADS)
    offset_bucket = bucket_of((jnp.arange(3 * TILE) - (TILE - 1)) % (3 * TILE) - TILE)
    bucket_column = jnp.arange(BUCKETS)[:, None]
    table = jnp.dot((bucket_column == offset_bucket[None, :]).astype(F32), near.T, precision=HIGHEST)
    table = table + jnp.where(bucket_column == 15, below, 0.0) + jnp.where(bucket_column == 31, above, 0.0)
    table = jnp.pad(table.reshape(-1, TILE), ((0, 1), (0, 0)))
    small = jnp.concatenate([g1.reshape(-1, TILE), g2.reshape(-1, TILE), table])
    small_masks = [(0, 1), (0, 2), (1, 0)] + [(bit, 0) for bit in bits]

    small = small + move(after(small, last_sent), small_masks[0])
    last.take()
    last_sent = last.outgoing()
    small = small + move(after(small, last_sent), small_masks[1])
    last.send()
    for i in range(2, stages + 1):
        last.take()
        last_sent = last.outgoing()
        last.send()
        small = small + move(after(small, last_sent), small_masks[i])
    small = small + move(small, small_masks[stages + 1])
    last.take()
    down.take(last_sent)
    while down.i < stages + 1:
        down.outgoing()
        down.send()
        down.take()
    down_grad_w = down.result()
    both_sum, last_sum = both.result(), last.result()
    gain_rows_count = width // TILE
    gain_grads = small[: 2 * gain_rows_count].reshape(2, width)
    gain_grads = lax.dynamic_slice_in_dim(gain_grads, (b * ns + s) * per, per, 1)
    table = small[2 * gain_rows_count : 2 * gain_rows_count + BUCKETS * HEADS // TILE].reshape(BUCKETS, HEADS)

    def unpack(name, old, keep, mate, got):
        mate, far = core(after(mate, got)), core(got[1])
        return pl.pallas_call(
            unpack_kernel,
            name=name,
            out_shape=shape(old.shape, F32),
            in_specs=[smem] + [vmem] * 5,
            cost_estimate=cost(3),
            compiler_params=params(),
        )(where, old, keep, mate, got, far)

    out_hidden = unpack("out_rows", hidden_in, out_keep, out_mate, after(out_got, op1_sent))
    input_grad = unpack("in_rows", out_grad, in_keep, in_mate, in_got)
    return (
        out_hidden,
        input_grad,
        table,
        gain_grads[0],
        gain_grads[1],
        last_sum[:, :width],
        last_sum[:, width : 2 * width],
        last_sum[:, 2 * width :],
        both_sum[:, ff:],
        both_sum[:, :ff],
        down_grad_w,
    )


def solution(mesh):
    nb, ns = mesh.shape["batch"], mesh.shape["seq"]
    placed = (
        P("batch", "seq", None),
        P("batch", None),
        P(),
        P("batch"),
        P("batch"),
        P("batch", None),
        P("batch", None),
        P("batch", None),
        P("batch", None),
        P("batch", None),
        P("batch", None),
        P("batch", "seq", None),
    )
    both = ("batch", "seq")
    return jax.shard_map(
        functools.partial(on_device, nb, ns),
        mesh=mesh,
        in_specs=placed,
        out_specs=(
            P("batch", "seq", None),
            P("batch", "seq", None),
            P(),
            P(both),
            P(both),
            P(both, None),
            P(both, None),
            P(both, None),
            P(both, None),
            P(both, None),
            P(both, None),
        ),
        check_vma=False,
    )
```

profile of v0, /device:TPU:0, one launch (start us, length us, event | category | flops | bytes accessed | tf_op | source)
XLA Modules:
  0.0 293.9 jit_solution(12621990531252486704)
XLA Ops:
  5.4 3.1 %collective-permute-start.3 = (bf16[1,96,1664]{2,1,0:T(8,128)(2,1)S(1)}, bf16[1,96,1664]{2,1,0:T(8,128)(2,1)S(1)}, u32[]{:S(2)}, u32[]{:S(2)}) collective-permute-start(bf16[1,96,1664]{2,1,0:T(8,128)(2,1)S(1)} %dynamic-slice_bitcast_fusion), channel_id=1, source_target_pairs={{0,4},{1,17},{2,6},{3,19},{4,0},{5,21},{6,2},{7,23},{8,12},{9,25},... | collective-permute-start | bytes 958472 | tf_op jit(solution)/shard_map/ppermute | solution.py:457
  9.1 3.2 %pack.1 = (bf16[2,128,768]{2,1,0:T(8,128)(2,1)}, bf16[2,128,768]{2,1,0:T(8,128)(2,1)}, bf16[2,2,128,768]{3,2,1,0:T(8,128)(2,1)}) custom-call(s32[18]{0:T(128)} %pad_add_fusion.where, f32[4,128,768]{2,1,0:T(8,128)} %old_ref.2, f32[4,128,768]{2,1,0:T(8,128)} %old_ref.3), custom_call_target="tpu_custom_call" | custom-call | flops 3000000000 | bytes 10500000 | tf_op jit(solution)/shard_map/pack/pallas_call | solution.py:522
  12.3 1.5 collective-permute-start.1
  14.6 2.7 collective-permute-start.4
  17.9 3.6 %prepare.1 = (f32[12,128,384]{2,1,0:T(8,128)}, bf16[512,128]{1,0:T(8,128)(2,1)}, bf16[512,128]{1,0:T(8,128)(2,1)}, bf16[768,768]{1,0:T(8,128)(2,1)}) custom-call(s32[18]{0:T(128)} %pad_add_fusion.where, s32[4,8]{1,0:T(4,128)} %lengths.1, f32[32,12]{1,0:T(8,128)} %copy.36.table.table_ref, s32[1,768]{1,0:T(1,128)} %fusion.3.position_ref), custom_call_target="tpu_custom_call" | custom-call | flops 6000000000 | bytes 21000000 | tf_op jit(solution)/shard_map/prepare/pallas_call | solution.py:533
  21.5 11.0 %collective-permute-done.1.away_ref = bf16[2,2,128,768]{3,2,1,0:T(8,128)(2,1)S(1)} collective-permute-done((bf16[2,2,128,768]{3,2,1,0:T(8,128)(2,1)}, bf16[2,2,128,768]{3,2,1,0:T(8,128)(2,1)S(1)}, u32[]{:S(2)}, u32[]{:S(2)}) %collective-permute-start.1) | collective-permute-done | bytes 786464 | tf_op jit(solution)/shard_map/ppermute | solution.py:457
  33.5 1.7 collective-permute-start.7
  35.7 6.5 %collective-permute-done.5 = bf16[1,96,768]{2,1,0:T(8,128)(2,1)S(1)} collective-permute-done((bf16[1,96,768]{2,1,0:T(8,128)(2,1)S(1)}, bf16[1,96,768]{2,1,0:T(8,128)(2,1)S(1)}, u32[]{:S(2)}, u32[]{:S(2)}) %collective-permute-start.5) | collective-permute-done | bytes 147488 | tf_op jit(solution)/shard_map/ppermute | solution.py:457
  42.2 1.9 collective-permute-start.6
  44.1 13.8 %collective-permute-done.6 = bf16[2,96,768]{2,1,0:T(8,128)(2,1)S(1)} collective-permute-done((bf16[2,96,768]{2,1,0:T(8,128)(2,1)S(1)}, bf16[2,96,768]{2,1,0:T(8,128)(2,1)S(1)}, u32[]{:S(2)}, u32[]{:S(2)}) %collective-permute-start.6) | collective-permute-done | bytes 294944 | tf_op jit(solution)/shard_map/ppermute | solution.py:457
  59.4 2.0 collective-permute-start.10
  62.5 1.9 collective-permute-done.mate_ref
  64.4 1.5 collective-permute-start.12
  65.9 5.0 %collective-permute-done.10.refs_1_ = bf16[4,96,768]{2,1,0:T(8,128)(2,1)S(1)} collective-permute-done((bf16[4,96,768]{2,1,0:T(8,128)(2,1)S(1)}, bf16[4,96,768]{2,1,0:T(8,128)(2,1)S(1)}, u32[]{:S(2)}, u32[]{:S(2)}) %collective-permute-start.10) | collective-permute-done | bytes 589856 | tf_op jit(solution)/shard_map/ppermute | solution.py:457
  71.4 9.9 %qkv.1 = (bf16[512,2304]{1,0:T(8,128)(2,1)}, bf16[768,512]{1,0:T(8,128)(2,1)}, bf16[4,128,768]{2,1,0:T(8,128)(2,1)}, bf16[4,128,768]{2,1,0:T(8,128)(2,1)}, f32[2...) custom-call(s32[18]{0:T(128)} %pad_add_fusion.where, bf16[2,128,768]{2,1,0:T(8,128)(2,1)} %get-tuple-element.100.keep_ref, ...), custom_call_target="tpu_custom_call" | custom-call | flops 8999999488 | bytes 31500000 | tf_op jit(solution)/shard_map/qkv/pallas_call | solution.py:558
  82.5 3.2 %collective-permute-start.13 = (bf16[2,96,768]{2,1,0:T(8,128)(2,1)S(1)}, bf16[2,96,768]{2,1,0:T(8,128)(2,1)S(1)}, u32[]{:S(2)}, u32[]{:S(2)}) collective-permute-start(bf16[2,96,768]{2,1,0:T(8,128)(2,1)S(1)} %pad_maximum_fusion.5), channel_id=1, source_target_pairs={{0,16},{1,9},{2,18},{3,11},{4,20},{5,13},{6,22},{7,15},{8,24},{9,1... | collective-permute-start | bytes 884744 | tf_op jit(solution)/shard_map/ppermute | solution.py:457
  85.7 5.8 %attention.2 = (bf16[6,512,512]{2,1,0:T(8,128)(2,1)}, bf16[512,384]{1,0:T(8,128)(2,1)}) custom-call(bf16[512,2304]{1,0:T(8,128)(2,1)} %get-tuple-element.111.q_ref.k_ref.v_ref, bf16[512,2304]{1,0:T(8,128)(2,1)} %get-tuple-element.111.q_ref.k_ref.v_ref, bf16[512,2304]{1,0:T(8,128)(2,1)} %get-tuple-element.111.q_ref.k_ref.v_ref, ...), custom_call_target="tpu_custom_call" | custom-call | flops 10000000000 | bytes 35000000 | tf_op jit(solution)/shard_map/attention/pallas_call | solution.py:582
  91.5 1.8 collective-permute-done.13
  93.6 3.2 %collective-permute-done.15.refs_5_ = bf16[4,96,768]{2,1,0:T(8,128)(2,1)} collective-permute-done((bf16[4,96,768]{2,1,0:T(8,128)(2,1)S(1)}, bf16[4,96,768]{2,1,0:T(8,128)(2,1)}, u32[]{:S(2)}, u32[]{:S(2)}) %collective-permute-start.15) | collective-permute-done | bytes 589856 | tf_op jit(solution)/shard_map/ppermute | solution.py:457
  97.9 5.8 %attention.3 = (bf16[6,512,512]{2,1,0:T(8,128)(2,1)}, bf16[512,384]{1,0:T(8,128)(2,1)}) custom-call(bf16[512,2304]{1,0:T(8,128)(2,1)} %get-tuple-element.111.q_ref.k_ref.v_ref, bf16[512,2304]{1,0:T(8,128)(2,1)} %get-tuple-element.111.q_ref.k_ref.v_ref, bf16[512,2304]{1,0:T(8,128)(2,1)} %get-tuple-element.111.q_ref.k_ref.v_ref, ...), custom_call_target="tpu_custom_call" | custom-call | flops 10000000000 | bytes 35000000 | tf_op jit(solution)/shard_map/attention/pallas_call | solution.py:582
  104.7 8.4 %collective-permute-done.16.refs_4_ = bf16[4,96,768]{2,1,0:T(8,128)(2,1)S(1)} collective-permute-done((bf16[4,96,768]{2,1,0:T(8,128)(2,1)S(1)}, bf16[4,96,768]{2,1,0:T(8,128)(2,1)S(1)}, u32[]{:S(2)}, u32[]{:S(2)}) %collective-permute-start.16) | collective-permute-done | bytes 589856 | tf_op jit(solution)/shard_map/ppermute | solution.py:457
  113.8 6.1 %out.1 = (f32[512,768]{1,0:T(8,128)}, bf16[512,768]{1,0:T(8,128)(2,1)}, bf16[768,512]{1,0:T(8,128)(2,1)}) custom-call(bf16[512,768]{1,0:T(8,128)(2,1)} %bitcast.53, bf16[512,384]{1,0:T(8,128)(2,1)} %get-tuple-element.122.ctx_a_ref.ctx_ref, bf16[512,384]{1,0:T(8,128)(2,1)} %get-tuple-element.120.ctx_b_ref.ctx_ref, ...), custom_call_target="tpu_custom_call" | custom-call | flops 5000000000 | bytes 17500000 | tf_op jit(solution)/shard_map/out/pallas_call | solution.py:613
  119.9 4.2 %collective-permute-done.17.refs_5_ = bf16[4,96,768]{2,1,0:T(8,128)(2,1)} collective-permute-done((bf16[4,96,768]{2,1,0:T(8,128)(2,1)S(1)}, bf16[4,96,768]{2,1,0:T(8,128)(2,1)}, u32[]{:S(2)}, u32[]{:S(2)}) %collective-permute-start.17) | collective-permute-done | bytes 589856 | tf_op jit(solution)/shard_map/ppermute | solution.py:457
  124.1 14.6 %up.1 = (bf16[512,3072]{1,0:T(8,128)(2,1)}, bf16[512,3072]{1,0:T(8,128)(2,1)}, bf16[2,2,2,2,96,768]{5,4,3,2,1,0:T(8,128)(2,1)}, bf16[2,2,2,2,96,768]{5,4,3,2,1,0:T(8,128)(2,1)}, bf16[4,8,96,768]{3,2,1,0:T(8,128)(2,1)}) custom-call(s32[4]{0:T(128)} %pad_add_fusion.1.place, s32[18]{0:T(128)} %pad_add_fusion.where, ...), custom_call_target="tpu_custom_call" | custom-call | flops 10000000000 | bytes 35000000 | tf_op jit(solution)/shard_map/up/pallas_call | solution.py:649
  139.9 1.3 slice.224
  141.2 4.8 %collective-permute-done.22 = bf16[1536,768]{1,0:T(8,128)(2,1)S(1)} collective-permute-done((bf16[1536,768]{1,0:T(8,128)(2,1)}, bf16[1536,768]{1,0:T(8,128)(2,1)S(1)}, u32[]{:S(2)}, u32[]{:S(2)}) %collective-permute-start.22) | collective-permute-done | bytes 2359328 | tf_op jit(solution)/shard_map/ppermute | solution.py:457
  146.0 1.8 fusion
  149.2 20.5 %down.1 = (bf16[128,768]{1,0:T(8,128)(2,1)}, bf16[128,768]{1,0:T(8,128)(2,1)}, bf16[2,128,768]{2,1,0:T(8,128)(2,1)}, f32[512,768]{1,0:T(8,128)}, bf16[384,3072]{1,0:T(8,128)(2,1)}, /*index=5*/bf16[384,3072]{1,0:T(8,128)(2,1)}) custom-call(s32[18]{0:T(128)} %pad_add_fusion.where, bf16[768,512]{1,0:T(8,128)(2,1)} %get-tuple-element.125.second_t_ref, ...), custom_call_target="tpu_custom_call" | custom-call | flops 15000000512 | bytes 52500000 | tf_op jit(solution)/shard_map/down/pallas_call | solution.py:718
  170.6 8.3 %mid.1 = (f32[512,768]{1,0:T(8,128)}, f32[1,768]{1,0:T(1,128)}, bf16[512,768]{1,0:T(8,128)(2,1)}, bf16[384,768]{1,0:T(8,128)(2,1)}, bf16[384,768]{1,0:T(8,128)(2,1)}) custom-call(bf16[512,768]{1,0:T(8,128)(2,1)} %bitcast.54, f32[512,768]{1,0:T(8,128)} %get-tuple-element.127.attn_ref, f32[2,768]{1,0:T(2,128)} %get-tuple-element.124.gains_ref, ...), custom_call_target="tpu_custom_call" | custom-call | flops 7000000000 | bytes 24500000 | tf_op jit(solution)/shard_map/mid/pallas_call | solution.py:738
  180.5 1.4 copy-done.5
  181.9 2.2 constant_dynamic-update-slice_fusion.7
  184.1 1.4 add_convert_fusion
  186.4 2.4 add_convert_fusion.3
  189.9 1.2 collective-permute-start.33
  191.1 8.1 %back.2 = (bf16[512,384]{1,0:T(8,128)(2,1)}, bf16[512,384]{1,0:T(8,128)(2,1)}, bf16[512,384]{1,0:T(8,128)(2,1)}, f32[3,8,384]{2,1,0:T(8,128)}) custom-call(bf16[512,2304]{1,0:T(8,128)(2,1)} %get-tuple-element.111.q_ref.k_ref.v_ref, bf16[512,2304]{1,0:T(8,128)(2,1)} %get-tuple-element.111.q_ref.k_ref.v_ref, ...), custom_call_target="tpu_custom_call" | custom-call | flops 10000000000 | bytes 35000000 | tf_op jit(solution)/shard_map/back/pallas_call | solution.py:759
  199.2 5.9 %collective-permute-done.31 = bf16[384,768]{1,0:T(8,128)(2,1)S(1)} collective-permute-done((bf16[384,768]{1,0:T(8,128)(2,1)}, bf16[384,768]{1,0:T(8,128)(2,1)S(1)}, u32[]{:S(2)}, u32[]{:S(2)}) %collective-permute-start.31) | collective-permute-done | bytes 589856 | tf_op jit(solution)/shard_map/ppermute | solution.py:457
  205.2 2.2 add_convert_fusion.6
  208.5 8.2 %back.3 = (bf16[512,384]{1,0:T(8,128)(2,1)}, bf16[512,384]{1,0:T(8,128)(2,1)}, bf16[512,384]{1,0:T(8,128)(2,1)}, f32[3,8,384]{2,1,0:T(8,128)}) custom-call(bf16[512,2304]{1,0:T(8,128)(2,1)} %get-tuple-element.111.q_ref.k_ref.v_ref, bf16[512,2304]{1,0:T(8,128)(2,1)} %get-tuple-element.111.q_ref.k_ref.v_ref, ...), custom_call_target="tpu_custom_call" | custom-call | flops 10000000000 | bytes 35000000 | tf_op jit(solution)/shard_map/back/pallas_call | solution.py:759
  216.7 1.9 add_convert_fusion.9
  218.7 1.3 add_convert_fusion.2
  220.7 5.5 %grad.1 = (bf16[384,2304]{1,0:T(8,128)(2,1)}, bf16[384,2304]{1,0:T(8,128)(2,1)}) custom-call(bf16[512,384]{1,0:T(8,128)(2,1)} %get-tuple-element.168.dqa_ref, bf16[512,384]{1,0:T(8,128)(2,1)} %get-tuple-element.156.dqb_ref, bf16[512,384]{1,0:T(8,128)(2,1)} %get-tuple-element.160.dka_ref, bf16[512,384]{1,0:T(8,128)(2,1)} %get-tuple-element.161.dkb_ref, ...), custom_call_target="tpu_custom_call" | custom-call | flops 5000000000 | bytes 17500000 | tf_op jit(solution)/shard_map/grad/pallas_call | solution.py:789
  226.2 1.4 collective-permute-start.27
  227.7 2.4 collective-permute-start.52
  230.1 3.7 %collective-permute-done.35 = bf16[96,3840]{1,0:T(8,128)(2,1)} collective-permute-done((bf16[96,3840]{1,0:T(8,128)(2,1)}, bf16[96,3840]{1,0:T(8,128)(2,1)}, u32[]{:S(2)}, u32[]{:S(2)}) %collective-permute-start.35) | collective-permute-done | bytes 737312 | tf_op jit(solution)/shard_map/ppermute | solution.py:457
  233.8 1.4 add_convert_fusion.5
  235.8 7.3 %first.1 = (bf16[128,768]{1,0:T(8,128)(2,1)}, bf16[128,768]{1,0:T(8,128)(2,1)}, bf16[2,128,768]{2,1,0:T(8,128)(2,1)}, f32[1,768]{1,0:T(1,128)}) custom-call(s32[18]{0:T(128)} %pad_add_fusion.where, bf16[512,768]{1,0:T(8,128)(2,1)} %bitcast.55, f32[2,768]{1,0:T(2,128)} %get-tuple-element.124.gains_ref, bf16[512,384]{1,0:T(8,128)(2,1)} %get-tuple-element.168.dqa_ref, ...), custom_call_target="tpu_custom_call" | custom-call | flops 6000000000 | bytes 21000000 | tf_op jit(solution)/shard_map/first/pallas_call | solution.py:800
  243.8 2.6 add_convert_fusion.1
  246.7 1.3 add_convert_fusion.8
  248.0 2.0 collective-permute-start.51
  251.0 2.5 collective-permute-start.38
  254.8 2.0 collective-permute-done.51
  256.8 2.9 collective-permute-done.42
  259.7 1.4 add_convert_fusion.4
  261.2 1.2 collective-permute-start.44
  262.3 1.4 convert_add_fusion.1
  266.7 3.0 %out_rows.1 = f32[4,128,768]{2,1,0:T(8,128)} custom-call(s32[18]{0:T(128)} %pad_add_fusion.where, f32[4,128,768]{2,1,0:T(8,128)} %old_ref.2, bf16[128,768]{1,0:T(8,128)(2,1)} %get-tuple-element.139.keep_ref, bf16[128,768]{1,0:T(8,128)(2,1)} %copy-done.33, bf16[2,128,768]{2,1,0:T(8,128)(2,1)} %collective-permute-done.27.away_ref, bf16[128,768]{1,0:T(8,128)(2,1)} %copy-done.32), custom_call_target="tpu_custom_call" | custom-call | flops 3000000000 | bytes 10500000 | tf_op jit(solution)/shard_map/out_rows/pallas_call | solution.py:858
  269.7 1.4 add_convert_fusion.7
  271.1 1.6 collective-permute-start.46
  274.3 2.1 collective-permute-done.45
  278.2 1.7 collective-permute-start.47
  280.7 3.0 %in_rows.1 = f32[4,128,768]{2,1,0:T(8,128)} custom-call(s32[18]{0:T(128)} %pad_add_fusion.where, f32[4,128,768]{2,1,0:T(8,128)} %old_ref.3, bf16[128,768]{1,0:T(8,128)(2,1)} %get-tuple-element.174.keep_ref, bf16[128,768]{1,0:T(8,128)(2,1)} %copy-done.35, bf16[2,128,768]{2,1,0:T(8,128)(2,1)} %copy-done.18, bf16[128,768]{1,0:T(8,128)(2,1)} %copy-done.34), custom_call_target="tpu_custom_call" | custom-call | flops 3000000000 | bytes 10500000 | tf_op jit(solution)/shard_map/in_rows/pallas_call | solution.py:858
  283.7 1.9 collective-permute-start.49
  286.7 2.0 convert_add_fusion.2
  288.8 1.9 collective-permute-done.48
  (208 shorter events, 39.3 us)
Async XLA Ops:
  0.6 34.6 %copy-start = (bf16[96,3072]{1,0:T(8,128)(2,1)S(1)}, bf16[96,3072]{1,0:T(8,128)(2,1)}, u32[]{:S(2)}) copy-start(bf16[96,3072]{1,0:T(8,128)(2,1)} %param.22) | copy-start | bytes 1769476
  5.4 9.1 %collective-permute-start.3 = (bf16[1,96,1664]{2,1,0:T(8,128)(2,1)S(1)}, bf16[1,96,1664]{2,1,0:T(8,128)(2,1)S(1)}, u32[]{:S(2)}, u32[]{:S(2)}) collective-permute-start(bf16[1,96,1664]{2,1,0:T(8,128)(2,1)S(1)} %dynamic-slice_bitcast_fusion), channel_id=1, source_target_pairs={{0,4},{1,17},{2,6},{3,19},{4,0},{5,21},{6,2},{7,23},{8,12},{9,25},... | collective-permute-start | bytes 958472 | tf_op jit(solution)/shard_map/ppermute | solution.py:457
  12.3 20.2 %collective-permute-start.1 = (bf16[2,2,128,768]{3,2,1,0:T(8,128)(2,1)}, bf16[2,2,128,768]{3,2,1,0:T(8,128)(2,1)S(1)}, u32[]{:S(2)}, u32[]{:S(2)}) collective-permute-start(bf16[2,2,128,768]{3,2,1,0:T(8,128)(2,1)} %get-tuple-element.102), channel_id=1, source_target_pairs={{0,2},{1,3},{2,0},{3,1},{4,6},{5,7},{6,4},{7,5},{8,10},{9,11},{10,... | collective-permute-start | bytes 2359304 | tf_op jit(solution)/shard_map/ppermute | solution.py:457
  14.6 18.2 %collective-permute-start.4 = (bf16[2,96,1664]{2,1,0:T(8,128)(2,1)S(1)}, bf16[2,96,1664]{2,1,0:T(8,128)(2,1)S(1)}, u32[]{:S(2)}, u32[]{:S(2)}) collective-permute-start(bf16[2,96,1664]{2,1,0:T(8,128)(2,1)S(1)} %pad_maximum_fusion.1), channel_id=1, source_target_pairs={{0,16},{1,9},{2,18},{3,11},{4,20},{5,13},{6,22},{7,15},{8,24},{9,1... | collective-permute-start | bytes 1916936 | tf_op jit(solution)/shard_map/ppermute | solution.py:457
  33.5 37.9 %copy-start.7 = (bf16[4,96,1664]{2,1,0:T(8,128)(2,1)}, bf16[4,96,1664]{2,1,0:T(8,128)(2,1)S(1)}, u32[]{:S(2)}) copy-start(bf16[4,96,1664]{2,1,0:T(8,128)(2,1)S(1)} %pad_maximum_fusion.refs_0_) | copy-start | bytes 3833860
  33.5 25.3 %collective-permute-start.7 = (bf16[4,96,1664]{2,1,0:T(8,128)(2,1)S(1)}, bf16[4,96,1664]{2,1,0:T(8,128)(2,1)}, u32[]{:S(2)}, u32[]{:S(2)}) collective-permute-start(bf16[4,96,1664]{2,1,0:T(8,128)(2,1)S(1)} %pad_maximum_fusion.refs_0_), channel_id=1, source_target_pairs={{0,8},{1,5},{2,10},{3,7},{4,12},{5,1},{6,14},{7,3},{8,0},{9,13},{1... | collective-permute-start | bytes 3833864 | tf_op jit(solution)/shard_map/ppermute | solution.py:457
  35.3 26.1 %copy-start.16 = (bf16[2,2,128,768]{3,2,1,0:T(8,128)(2,1)S(1)}, bf16[2,2,128,768]{3,2,1,0:T(8,128)(2,1)}, u32[]{:S(2)}) copy-start(bf16[2,2,128,768]{3,2,1,0:T(8,128)(2,1)} %copy-done.15) | copy-start | bytes 2359300
  35.3 6.9 %collective-permute-start.5 = (bf16[1,96,768]{2,1,0:T(8,128)(2,1)S(1)}, bf16[1,96,768]{2,1,0:T(8,128)(2,1)S(1)}, u32[]{:S(2)}, u32[]{:S(2)}) collective-permute-start(bf16[1,96,768]{2,1,0:T(8,128)(2,1)S(1)} %dynamic-slice_bitcast_fusion.2), channel_id=1, source_target_pairs={{0,4},{1,17},{2,6},{3,19},{4,0},{5,21},{6,2},{7,23},{8,12},{9,25},... | collective-permute-start | bytes 442376 | tf_op jit(solution)/shard_map/ppermute | solution.py:457
  42.2 15.8 %collective-permute-start.6 = (bf16[2,96,768]{2,1,0:T(8,128)(2,1)S(1)}, bf16[2,96,768]{2,1,0:T(8,128)(2,1)S(1)}, u32[]{:S(2)}, u32[]{:S(2)}) collective-permute-start(bf16[2,96,768]{2,1,0:T(8,128)(2,1)S(1)} %pad_maximum_fusion.4), channel_id=1, source_target_pairs={{0,16},{1,9},{2,18},{3,11},{4,20},{5,13},{6,22},{7,15},{8,24},{9,1... | collective-permute-start | bytes 884744 | tf_op jit(solution)/shard_map/ppermute | solution.py:457
  58.0 23.3 %copy-start.9 = (bf16[4,96,768]{2,1,0:T(8,128)(2,1)}, bf16[4,96,768]{2,1,0:T(8,128)(2,1)S(1)}, u32[]{:S(2)}) copy-start(bf16[4,96,768]{2,1,0:T(8,128)(2,1)S(1)} %pad_maximum_fusion.2.refs_0_) | copy-start | bytes 1769476
  58.0 12.8 %collective-permute-start.8 = (bf16[4,96,1664]{2,1,0:T(8,128)(2,1)S(1)}, bf16[4,96,1664]{2,1,0:T(8,128)(2,1)}, u32[]{:S(2)}, u32[]{:S(2)}) collective-permute-start(bf16[4,96,1664]{2,1,0:T(8,128)(2,1)S(1)} %pad_maximum_fusion.refs_0_), channel_id=1, source_target_pairs={{0,1},{1,0},{2,3},{3,2},{4,5},{5,4},{6,7},{7,6},{8,9},{9,8},{10,11... | collective-permute-start | bytes 3833864 | tf_op jit(solution)/shard_map/ppermute | solution.py:457
  58.9 12.5 %collective-permute-start.9 = (bf16[4,96,1664]{2,1,0:T(8,128)(2,1)}, bf16[4,96,1664]{2,1,0:T(8,128)(2,1)}, u32[]{:S(2)}, u32[]{:S(2)}) collective-permute-start(bf16[4,96,1664]{2,1,0:T(8,128)(2,1)} %collective-permute-done.7.refs_1_), channel_id=1, source_target_pairs={{0,1},{1,0},{2,3},{3,2},{4,5},{5,4},{6,7},{7,6},{8,9},{9,8},{10,11... | collective-permute-start | bytes 3833864 | tf_op jit(solution)/shard_map/ppermute | solution.py:457
  58.9 5.5 %collective-permute-start = (bf16[2,128,768]{2,1,0:T(8,128)(2,1)}, bf16[2,128,768]{2,1,0:T(8,128)(2,1)}, u32[]{:S(2)}, u32[]{:S(2)}) collective-permute-start(bf16[2,128,768]{2,1,0:T(8,128)(2,1)} %get-tuple-element.101), channel_id=1, source_target_pairs={{0,1},{1,0},{2,3},{3,2},{4,5},{5,4},{6,7},{7,6},{8,9},{9,8},{10,11... | collective-permute-start | bytes 1179656 | tf_op jit(solution)/shard_map/ppermute | solution.py:457
  59.4 11.5 %collective-permute-start.10 = (bf16[4,96,768]{2,1,0:T(8,128)(2,1)S(1)}, bf16[4,96,768]{2,1,0:T(8,128)(2,1)S(1)}, u32[]{:S(2)}, u32[]{:S(2)}) collective-permute-start(bf16[4,96,768]{2,1,0:T(8,128)(2,1)S(1)} %pad_maximum_fusion.2.refs_0_), channel_id=1, source_target_pairs={{0,8},{1,5},{2,10},{3,7},{4,12},{5,1},{6,14},{7,3},{8,0},{9,13},{1... | collective-permute-start | bytes 1769480 | tf_op jit(solution)/shard_map/ppermute | solution.py:457
  61.5 2.9 collective-permute-start.2
  64.4 18.1 %collective-permute-start.11 = (bf16[1,96,768]{2,1,0:T(8,128)(2,1)S(1)}, bf16[1,96,768]{2,1,0:T(8,128)(2,1)S(1)}, u32[]{:S(2)}, u32[]{:S(2)}) collective-permute-start(bf16[1,96,768]{2,1,0:T(8,128)(2,1)S(1)} %dynamic-slice_bitcast_fusion.1), channel_id=1, source_target_pairs={{0,4},{1,17},{2,6},{3,19},{4,0},{5,21},{6,2},{7,23},{8,12},{9,25},... | collective-permute-start | bytes 442376 | tf_op jit(solution)/shard_map/ppermute | solution.py:457
  64.4 21.3 %collective-permute-start.12 = (bf16[4,96,768]{2,1,0:T(8,128)(2,1)S(1)}, bf16[4,96,768]{2,1,0:T(8,128)(2,1)}, u32[]{:S(2)}, u32[]{:S(2)}) collective-permute-start(bf16[4,96,768]{2,1,0:T(8,128)(2,1)S(1)} %pad_maximum_fusion.2.refs_0_), channel_id=1, source_target_pairs={{0,2},{1,3},{2,0},{3,1},{4,6},{5,7},{6,4},{7,5},{8,10},{9,11},{10,... | collective-permute-start | bytes 1769480 | tf_op jit(solution)/shard_map/ppermute | solution.py:457
  70.9 53.2 %collective-permute-start.18 = (bf16[4,96,768]{2,1,0:T(8,128)(2,1)S(1)}, bf16[4,96,768]{2,1,0:T(8,128)(2,1)}, u32[]{:S(2)}, u32[]{:S(2)}) collective-permute-start(bf16[4,96,768]{2,1,0:T(8,128)(2,1)S(1)} %pad_maximum_fusion.2.refs_0_), channel_id=1, source_target_pairs={{0,1},{1,0},{2,3},{3,2},{4,5},{5,4},{6,7},{7,6},{8,9},{9,8},{10,11... | collective-permute-start | bytes 1769480 | tf_op jit(solution)/shard_map/ppermute | solution.py:457
  70.9 53.2 %collective-permute-start.19 = (bf16[4,96,768]{2,1,0:T(8,128)(2,1)S(1)}, bf16[4,96,768]{2,1,0:T(8,128)(2,1)}, u32[]{:S(2)}, u32[]{:S(2)}) collective-permute-start(bf16[4,96,768]{2,1,0:T(8,128)(2,1)S(1)} %collective-permute-done.10.refs_1_), channel_id=1, source_target_pairs={{0,1},{1,0},{2,3},{3,2},{4,5},{5,4},{6,7},{7,6},{8,9},{9,8},{10,11... | collective-permute-start | bytes 1769480 | tf_op jit(solution)/shard_map/ppermute | solution.py:457
  81.3 15.5 %collective-permute-start.15 = (bf16[4,96,768]{2,1,0:T(8,128)(2,1)S(1)}, bf16[4,96,768]{2,1,0:T(8,128)(2,1)}, u32[]{:S(2)}, u32[]{:S(2)}) collective-permute-start(bf16[4,96,768]{2,1,0:T(8,128)(2,1)S(1)} %collective-permute-done.10.refs_1_), channel_id=1, source_target_pairs={{0,2},{1,3},{2,0},{3,1},{4,6},{5,7},{6,4},{7,5},{8,10},{9,11},{10,... | collective-permute-start | bytes 1769480 | tf_op jit(solution)/shard_map/ppermute | solution.py:457
  82.5 10.8 %collective-permute-start.13 = (bf16[2,96,768]{2,1,0:T(8,128)(2,1)S(1)}, bf16[2,96,768]{2,1,0:T(8,128)(2,1)S(1)}, u32[]{:S(2)}, u32[]{:S(2)}) collective-permute-start(bf16[2,96,768]{2,1,0:T(8,128)(2,1)S(1)} %pad_maximum_fusion.5), channel_id=1, source_target_pairs={{0,16},{1,9},{2,18},{3,11},{4,20},{5,13},{6,22},{7,15},{8,24},{9,1... | collective-permute-start | bytes 884744 | tf_op jit(solution)/shard_map/ppermute | solution.py:457
  93.3 45.4 %copy-start.10 = (bf16[4,96,768]{2,1,0:T(8,128)(2,1)}, bf16[4,96,768]{2,1,0:T(8,128)(2,1)S(1)}, u32[]{:S(2)}) copy-start(bf16[4,96,768]{2,1,0:T(8,128)(2,1)S(1)} %pad_maximum_fusion.3.refs_0_) | copy-start | bytes 1769476
  93.4 10.3 %collective-permute-start.14 = (bf16[4,96,768]{2,1,0:T(8,128)(2,1)S(1)}, bf16[4,96,768]{2,1,0:T(8,128)(2,1)S(1)}, u32[]{:S(2)}, u32[]{:S(2)}) collective-permute-start(bf16[4,96,768]{2,1,0:T(8,128)(2,1)S(1)} %pad_maximum_fusion.3.refs_0_), channel_id=1, source_target_pairs={{0,8},{1,5},{2,10},{3,7},{4,12},{5,1},{6,14},{7,3},{8,0},{9,13},{1... | collective-permute-start | bytes 1769480 | tf_op jit(solution)/shard_map/ppermute | solution.py:457
  96.8 16.3 %collective-permute-start.16 = (bf16[4,96,768]{2,1,0:T(8,128)(2,1)S(1)}, bf16[4,96,768]{2,1,0:T(8,128)(2,1)S(1)}, u32[]{:S(2)}, u32[]{:S(2)}) collective-permute-start(bf16[4,96,768]{2,1,0:T(8,128)(2,1)S(1)} %pad_maximum_fusion.3.refs_0_), channel_id=1, source_target_pairs={{0,2},{1,3},{2,0},{3,1},{4,6},{5,7},{6,4},{7,5},{8,10},{9,11},{10,... | collective-permute-start | bytes 1769480 | tf_op jit(solution)/shard_map/ppermute | solution.py:457
  103.7 35.6 %copy-start.25 = (bf16[4,96,768]{2,1,0:T(8,128)(2,1)}, bf16[4,96,768]{2,1,0:T(8,128)(2,1)S(1)}, u32[]{:S(2)}) copy-start(bf16[4,96,768]{2,1,0:T(8,128)(2,1)S(1)} %collective-permute-done.14.refs_1_) | copy-start | bytes 1769476
  103.7 20.3 %collective-permute-start.17 = (bf16[4,96,768]{2,1,0:T(8,128)(2,1)S(1)}, bf16[4,96,768]{2,1,0:T(8,128)(2,1)}, u32[]{:S(2)}, u32[]{:S(2)}) collective-permute-start(bf16[4,96,768]{2,1,0:T(8,128)(2,1)S(1)} %collective-permute-done.14.refs_1_), channel_id=1, source_target_pairs={{0,2},{1,3},{2,0},{3,1},{4,6},{5,7},{6,4},{7,5},{8,10},{9,11},{10,... | collective-permute-start | bytes 1769480 | tf_op jit(solution)/shard_map/ppermute | solution.py:457
  104.7 19.3 %collective-permute-start.20 = (bf16[4,96,768]{2,1,0:T(8,128)(2,1)}, bf16[4,96,768]{2,1,0:T(8,128)(2,1)}, u32[]{:S(2)}, u32[]{:S(2)}) collective-permute-start(bf16[4,96,768]{2,1,0:T(8,128)(2,1)} %collective-permute-done.12.refs_4_), channel_id=1, source_target_pairs={{0,1},{1,0},{2,3},{3,2},{4,5},{5,4},{6,7},{7,6},{8,9},{9,8},{10,11... | collective-permute-start | bytes 1769480 | tf_op jit(solution)/shard_map/ppermute | solution.py:457
  113.1 26.3 %copy-start.26 = (bf16[4,96,768]{2,1,0:T(8,128)(2,1)}, bf16[4,96,768]{2,1,0:T(8,128)(2,1)S(1)}, u32[]{:S(2)}) copy-start(bf16[4,96,768]{2,1,0:T(8,128)(2,1)S(1)} %collective-permute-done.16.refs_4_) | copy-start | bytes 1769476
  113.1 11.0 %collective-permute-start.21 = (bf16[4,96,768]{2,1,0:T(8,128)(2,1)}, bf16[4,96,768]{2,1,0:T(8,128)(2,1)}, u32[]{:S(2)}, u32[]{:S(2)}) collective-permute-start(bf16[4,96,768]{2,1,0:T(8,128)(2,1)} %collective-permute-done.15.refs_5_), channel_id=1, source_target_pairs={{0,1},{1,0},{2,3},{3,2},{4,5},{5,4},{6,7},{7,6},{8,9},{9,8},{10,11... | collective-permute-start | bytes 1769480 | tf_op jit(solution)/shard_map/ppermute | solution.py:457
  138.7 7.3 %collective-permute-start.22 = (bf16[1536,768]{1,0:T(8,128)(2,1)}, bf16[1536,768]{1,0:T(8,128)(2,1)S(1)}, u32[]{:S(2)}, u32[]{:S(2)}) collective-permute-start(bf16[1536,768]{1,0:T(8,128)(2,1)} %bitcast.50), channel_id=1, source_target_pairs={{0,1},{1,0},{2,3},{3,2},{4,5},{5,4},{6,7},{7,6},{8,9},{9,8},{10,11... | collective-permute-start | bytes 7077896 | tf_op jit(solution)/shard_map/ppermute | solution.py:457
  138.8 9.0 %collective-permute-start.23 = (bf16[4,96,768]{2,1,0:T(8,128)(2,1)S(1)}, bf16[4,96,768]{2,1,0:T(8,128)(2,1)S(1)}, u32[]{:S(2)}, u32[]{:S(2)}) collective-permute-start(bf16[4,96,768]{2,1,0:T(8,128)(2,1)S(1)} %pad_maximum_fusion.3.refs_0_), channel_id=1, source_target_pairs={{0,1},{1,0},{2,3},{3,2},{4,5},{5,4},{6,7},{7,6},{8,9},{9,8},{10,11... | collective-permute-start | bytes 1769480 | tf_op jit(solution)/shard_map/ppermute | solution.py:457
  139.3 8.5 %collective-permute-start.24 = (bf16[4,96,768]{2,1,0:T(8,128)(2,1)S(1)}, bf16[4,96,768]{2,1,0:T(8,128)(2,1)S(1)}, u32[]{:S(2)}, u32[]{:S(2)}) collective-permute-start(bf16[4,96,768]{2,1,0:T(8,128)(2,1)S(1)} %collective-permute-done.14.refs_1_), channel_id=1, source_target_pairs={{0,1},{1,0},{2,3},{3,2},{4,5},{5,4},{6,7},{7,6},{8,9},{9,8},{10,11... | collective-permute-start | bytes 1769480 | tf_op jit(solution)/shard_map/ppermute | solution.py:457
  139.4 8.4 %collective-permute-start.25 = (bf16[4,96,768]{2,1,0:T(8,128)(2,1)S(1)}, bf16[4,96,768]{2,1,0:T(8,128)(2,1)S(1)}, u32[]{:S(2)}, u32[]{:S(2)}) collective-permute-start(bf16[4,96,768]{2,1,0:T(8,128)(2,1)S(1)} %collective-permute-done.16.refs_4_), channel_id=1, source_target_pairs={{0,1},{1,0},{2,3},{3,2},{4,5},{5,4},{6,7},{7,6},{8,9},{9,8},{10,11... | collective-permute-start | bytes 1769480 | tf_op jit(solution)/shard_map/ppermute | solution.py:457
  139.8 8.0 %collective-permute-start.26 = (bf16[4,96,768]{2,1,0:T(8,128)(2,1)}, bf16[4,96,768]{2,1,0:T(8,128)(2,1)S(1)}, u32[]{:S(2)}, u32[]{:S(2)}) collective-permute-start(bf16[4,96,768]{2,1,0:T(8,128)(2,1)} %collective-permute-done.17.refs_5_), channel_id=1, source_target_pairs={{0,1},{1,0},{2,3},{3,2},{4,5},{5,4},{6,7},{7,6},{8,9},{9,8},{10,11... | collective-permute-start | bytes 1769480 | tf_op jit(solution)/shard_map/ppermute | solution.py:457
  169.6 10.8 %collective-permute-start.29 = (bf16[384,3072]{1,0:T(8,128)(2,1)}, bf16[384,3072]{1,0:T(8,128)(2,1)S(1)}, u32[]{:S(2)}, u32[]{:S(2)}) collective-permute-start(bf16[384,3072]{1,0:T(8,128)(2,1)} %get-tuple-element.146), channel_id=1, source_target_pairs={{0,1},{1,0},{2,3},{3,2},{4,5},{5,4},{6,7},{7,6},{8,9},{9,8},{10,11... | collective-permute-start | bytes 7077896 | tf_op jit(solution)/shard_map/ppermute | solution.py:457
  169.8 16.5 %collective-permute-start.28 = (bf16[768,768]{1,0:T(8,128)(2,1)}, bf16[768,768]{1,0:T(8,128)(2,1)}, u32[]{:S(2)}, u32[]{:S(2)}) collective-permute-start(bf16[768,768]{1,0:T(8,128)(2,1)} %fusion), channel_id=1, source_target_pairs={{0,4},{1,3},{2,6},{3,1},{4,0},{5,7},{6,2},{7,5},{8,12},{9,11},{10,... | collective-permute-start | bytes 3538952 | tf_op jit(solution)/shard_map/ppermute | solution.py:457
  178.9 5.1 %collective-permute-start.30 = (bf16[384,768]{1,0:T(8,128)(2,1)}, bf16[384,768]{1,0:T(8,128)(2,1)S(1)}, u32[]{:S(2)}, u32[]{:S(2)}) collective-permute-start(bf16[384,768]{1,0:T(8,128)(2,1)} %get-tuple-element.148), channel_id=1, source_target_pairs={{0,1},{1,0},{2,3},{3,2},{4,5},{5,4},{6,7},{7,6},{8,9},{9,8},{10,11... | collective-permute-start | bytes 1769480 | tf_op jit(solution)/shard_map/ppermute | solution.py:457
  180.4 38.2 %copy-start.2 = (bf16[384,3840]{1,0:T(8,128)(2,1)}, bf16[384,3840]{1,0:T(8,128)(2,1)S(1)}, u32[]{:S(2)}) copy-start(bf16[384,3840]{1,0:T(8,128)(2,1)S(1)} %constant_dynamic-update-slice_fusion.4) | copy-start | bytes 8847364
  188.8 16.4 %collective-permute-start.31 = (bf16[384,768]{1,0:T(8,128)(2,1)}, bf16[384,768]{1,0:T(8,128)(2,1)S(1)}, u32[]{:S(2)}, u32[]{:S(2)}) collective-permute-start(bf16[384,768]{1,0:T(8,128)(2,1)} %add_convert_fusion.3), channel_id=1, source_target_pairs={{0,2},{1,5},{2,0},{3,7},{4,6},{5,1},{6,4},{7,3},{8,10},{9,13},{10,... | collective-permute-start | bytes 1769480 | tf_op jit(solution)/shard_map/ppermute | solution.py:457
  189.9 28.8 %collective-permute-start.33 = (bf16[192,3840]{1,0:T(8,128)(2,1)}, bf16[192,3840]{1,0:T(8,128)(2,1)S(1)}, u32[]{:S(2)}, u32[]{:S(2)}) collective-permute-start(bf16[192,3840]{1,0:T(8,128)(2,1)} %add_convert_fusion), channel_id=1, source_target_pairs={{0,4},{1,3},{2,6},{3,1},{4,0},{5,7},{6,2},{7,5},{8,12},{9,11},{10,... | collective-permute-start | bytes 4423688 | tf_op jit(solution)/shard_map/ppermute | solution.py:457
  205.2 11.5 %copy-start.8 = (bf16[384,768]{1,0:T(8,128)(2,1)}, bf16[384,768]{1,0:T(8,128)(2,1)S(1)}, u32[]{:S(2)}) copy-start(bf16[384,768]{1,0:T(8,128)(2,1)S(1)} %collective-permute-done.31) | copy-start | bytes 1769476
  207.4 9.3 %collective-permute-start.32 = (bf16[192,768]{1,0:T(8,128)(2,1)}, bf16[192,768]{1,0:T(8,128)(2,1)S(1)}, u32[]{:S(2)}, u32[]{:S(2)}) collective-permute-start(bf16[192,768]{1,0:T(8,128)(2,1)} %add_convert_fusion.6), channel_id=1, source_target_pairs={{0,8},{1,9},{2,10},{3,11},{4,12},{5,13},{6,14},{7,15},{8,0},{9,1},... | collective-permute-start | bytes 884744 | tf_op jit(solution)/shard_map/ppermute | solution.py:457
  220.0 13.8 %collective-permute-start.35 = (bf16[96,3840]{1,0:T(8,128)(2,1)}, bf16[96,3840]{1,0:T(8,128)(2,1)}, u32[]{:S(2)}, u32[]{:S(2)}) collective-permute-start(bf16[96,3840]{1,0:T(8,128)(2,1)} %add_convert_fusion.2), channel_id=1, source_target_pairs={{0,2},{1,5},{2,0},{3,7},{4,6},{5,1},{6,4},{7,3},{8,10},{9,13},{10,... | collective-permute-start | bytes 2211848 | tf_op jit(solution)/shard_map/ppermute | solution.py:457
  226.2 17.6 %collective-permute-start.34 = (bf16[384,2304]{1,0:T(8,128)(2,1)}, bf16[384,2304]{1,0:T(8,128)(2,1)}, u32[]{:S(2)}, u32[]{:S(2)}) collective-permute-start(bf16[384,2304]{1,0:T(8,128)(2,1)} %get-tuple-element.166), channel_id=1, source_target_pairs={{0,1},{1,0},{2,3},{3,2},{4,5},{5,4},{6,7},{7,6},{8,9},{9,8},{10,11... | collective-permute-start | bytes 5308424 | tf_op jit(solution)/shard_map/ppermute | solution.py:457
  226.2 24.8 %collective-permute-start.27 = (bf16[2,128,768]{2,1,0:T(8,128)(2,1)}, bf16[2,128,768]{2,1,0:T(8,128)(2,1)}, u32[]{:S(2)}, u32[]{:S(2)}) collective-permute-start(bf16[2,128,768]{2,1,0:T(8,128)(2,1)} %get-tuple-element.141), channel_id=1, source_target_pairs={{0,2},{1,3},{2,0},{3,1},{4,6},{5,7},{6,4},{7,5},{8,10},{9,11},{10,... | collective-permute-start | bytes 1179656 | tf_op jit(solution)/shard_map/ppermute | solution.py:457
  227.7 58.0 %collective-permute-start.52 = (bf16[96,768]{1,0:T(8,128)(2,1)}, bf16[96,768]{1,0:T(8,128)(2,1)}, u32[]{:S(2)}, u32[]{:S(2)}) collective-permute-start(bf16[96,768]{1,0:T(8,128)(2,1)} %add_convert_fusion.9), channel_id=1, source_target_pairs={{0,16},{1,17},{2,18},{3,19},{4,20},{5,21},{6,22},{7,23},{8,24},{9,... | collective-permute-start | bytes 442376 | tf_op jit(solution)/shard_map/ppermute | solution.py:457
  235.2 11.5 %collective-permute-start.50 = (bf16[48,3840]{1,0:T(8,128)(2,1)S(1)}, bf16[48,3840]{1,0:T(8,128)(2,1)}, u32[]{:S(2)}, u32[]{:S(2)}) collective-permute-start(bf16[48,3840]{1,0:T(8,128)(2,1)S(1)} %add_convert_fusion.5), channel_id=1, source_target_pairs={{0,8},{1,9},{2,10},{3,11},{4,12},{5,13},{6,14},{7,15},{8,0},{9,1},... | collective-permute-start | bytes 1105928 | tf_op jit(solution)/shard_map/ppermute | solution.py:457
  246.3 13.4 %collective-permute-start.42 = (bf16[192,2304]{1,0:T(8,128)(2,1)}, bf16[192,2304]{1,0:T(8,128)(2,1)}, u32[]{:S(2)}, u32[]{:S(2)}) collective-permute-start(bf16[192,2304]{1,0:T(8,128)(2,1)} %add_convert_fusion.1), channel_id=1, source_target_pairs={{0,4},{1,3},{2,6},{3,1},{4,0},{5,7},{6,2},{7,5},{8,12},{9,11},{10,... | collective-permute-start | bytes 2654216 | tf_op jit(solution)/shard_map/ppermute | solution.py:457
  248.0 8.8 %collective-permute-start.51 = (bf16[24,3840]{1,0:T(8,128)(2,1)S(1)}, bf16[24,3840]{1,0:T(8,128)(2,1)S(1)}, u32[]{:S(2)}, u32[]{:S(2)}) collective-permute-start(bf16[24,3840]{1,0:T(8,128)(2,1)S(1)} %add_convert_fusion.8), channel_id=1, source_target_pairs={{0,16},{1,17},{2,18},{3,19},{4,20},{5,21},{6,22},{7,23},{8,24},{9,... | collective-permute-start | bytes 552968 | tf_op jit(solution)/shard_map/ppermute | solution.py:457
  250.9 3.6 %collective-permute-start.41 = (f32[16,128]{1,0:T(8,128)S(1)}, f32[16,128]{1,0:T(8,128)S(1)}, u32[]{:S(2)}, u32[]{:S(2)}) collective-permute-start(f32[16,128]{1,0:T(8,128)S(1)} %select_maximum_fusion), channel_id=1, source_target_pairs={{0,1},{1,0},{2,3},{3,2},{4,5},{5,4},{6,7},{7,6},{8,9},{9,8},{10,11... | collective-permute-start | bytes 24584 | tf_op jit(solution)/shard_map/ppermute | solution.py:457
  251.0 22.7 %collective-permute-start.38 = (bf16[2,128,768]{2,1,0:T(8,128)(2,1)}, bf16[2,128,768]{2,1,0:T(8,128)(2,1)S(1)}, u32[]{:S(2)}, u32[]{:S(2)}) collective-permute-start(bf16[2,128,768]{2,1,0:T(8,128)(2,1)} %get-tuple-element.177), channel_id=1, source_target_pairs={{0,2},{1,3},{2,0},{3,1},{4,6},{5,7},{6,4},{7,5},{8,10},{9,11},{10,... | collective-permute-start | bytes 1179656 | tf_op jit(solution)/shard_map/ppermute | solution.py:457
  254.5 10.6 %collective-permute-start.37 = (bf16[128,768]{1,0:T(8,128)(2,1)S(1)}, bf16[128,768]{1,0:T(8,128)(2,1)S(1)}, u32[]{:S(2)}, u32[]{:S(2)}) collective-permute-start(bf16[128,768]{1,0:T(8,128)(2,1)S(1)} %slice_bitcast_fusion.2), channel_id=1, source_target_pairs={{0,1},{1,0},{2,3},{3,2},{4,5},{5,4},{6,7},{7,6},{8,9},{9,8},{10,11... | collective-permute-start | bytes 589832 | tf_op jit(solution)/shard_map/ppermute | solution.py:457
  256.8 9.2 %collective-permute-start.36 = (bf16[128,768]{1,0:T(8,128)(2,1)}, bf16[128,768]{1,0:T(8,128)(2,1)S(1)}, u32[]{:S(2)}, u32[]{:S(2)}) collective-permute-start(bf16[128,768]{1,0:T(8,128)(2,1)} %get-tuple-element.173), channel_id=1, source_target_pairs={{0,1},{1,0},{2,3},{3,2},{4,5},{5,4},{6,7},{7,6},{8,9},{9,8},{10,11... | collective-permute-start | bytes 589832 | tf_op jit(solution)/shard_map/ppermute | solution.py:457
  261.2 8.6 %collective-permute-start.44 = (bf16[96,2304]{1,0:T(8,128)(2,1)S(1)}, bf16[96,2304]{1,0:T(8,128)(2,1)S(1)}, u32[]{:S(2)}, u32[]{:S(2)}) collective-permute-start(bf16[96,2304]{1,0:T(8,128)(2,1)S(1)} %add_convert_fusion.4), channel_id=1, source_target_pairs={{0,2},{1,5},{2,0},{3,7},{4,6},{5,1},{6,4},{7,3},{8,10},{9,13},{10,... | collective-permute-start | bytes 1327112 | tf_op jit(solution)/shard_map/ppermute | solution.py:457
  265.1 4.6 %collective-permute-start.43 = (f32[16,128]{1,0:T(8,128)S(1)}, f32[16,128]{1,0:T(8,128)S(1)}, u32[]{:S(2)}, u32[]{:S(2)}) collective-permute-start(f32[16,128]{1,0:T(8,128)S(1)} %fusion.18), channel_id=1, source_target_pairs={{0,2},{1,3},{2,0},{3,1},{4,6},{5,7},{6,4},{7,5},{8,10},{9,11},{10,... | collective-permute-start | bytes 24584 | tf_op jit(solution)/shard_map/ppermute | solution.py:457
  269.7 14.0 %copy-start.12 = (bf16[96,2304]{1,0:T(8,128)(2,1)}, bf16[96,2304]{1,0:T(8,128)(2,1)S(1)}, u32[]{:S(2)}) copy-start(bf16[96,2304]{1,0:T(8,128)(2,1)S(1)} %collective-permute-done.44) | copy-start | bytes 1327108
  271.1 6.0 %collective-permute-start.46 = (bf16[48,2304]{1,0:T(8,128)(2,1)S(1)}, bf16[48,2304]{1,0:T(8,128)(2,1)S(1)}, u32[]{:S(2)}, u32[]{:S(2)}) collective-permute-start(bf16[48,2304]{1,0:T(8,128)(2,1)S(1)} %add_convert_fusion.7), channel_id=1, source_target_pairs={{0,8},{1,9},{2,10},{3,11},{4,12},{5,13},{6,14},{7,15},{8,0},{9,1},... | collective-permute-start | bytes 663560 | tf_op jit(solution)/shard_map/ppermute | solution.py:457
  272.8 3.7 %collective-permute-start.45 = (f32[16,128]{1,0:T(8,128)S(1)}, f32[16,128]{1,0:T(8,128)S(1)}, u32[]{:S(2)}, u32[]{:S(2)}) collective-permute-start(f32[16,128]{1,0:T(8,128)S(1)} %add.464), channel_id=1, source_target_pairs={{0,4},{1,5},{2,6},{3,7},{4,0},{5,1},{6,2},{7,3},{8,12},{9,13},{10,... | collective-permute-start | bytes 24584 | tf_op jit(solution)/shard_map/ppermute | solution.py:457
  273.7 6.2 %collective-permute-start.40 = (bf16[128,768]{1,0:T(8,128)(2,1)S(1)}, bf16[128,768]{1,0:T(8,128)(2,1)S(1)}, u32[]{:S(2)}, u32[]{:S(2)}) collective-permute-start(bf16[128,768]{1,0:T(8,128)(2,1)S(1)} %slice_bitcast_fusion.1), channel_id=1, source_target_pairs={{0,1},{1,0},{2,3},{3,2},{4,5},{5,4},{6,7},{7,6},{8,9},{9,8},{10,11... | collective-permute-start | bytes 589832 | tf_op jit(solution)/shard_map/ppermute | solution.py:457
  273.8 6.1 %collective-permute-start.39 = (bf16[128,768]{1,0:T(8,128)(2,1)S(1)}, bf16[128,768]{1,0:T(8,128)(2,1)S(1)}, u32[]{:S(2)}, u32[]{:S(2)}) collective-permute-start(bf16[128,768]{1,0:T(8,128)(2,1)S(1)} %copy-done.31), channel_id=1, source_target_pairs={{0,1},{1,0},{2,3},{3,2},{4,5},{5,4},{6,7},{7,6},{8,9},{9,8},{10,11... | collective-permute-start | bytes 589832 | tf_op jit(solution)/shard_map/ppermute | solution.py:457
  278.2 7.4 %collective-permute-start.47 = (f32[16,128]{1,0:T(8,128)S(1)}, f32[16,128]{1,0:T(8,128)S(1)}, u32[]{:S(2)}, u32[]{:S(2)}) collective-permute-start(f32[16,128]{1,0:T(8,128)S(1)} %add.468), channel_id=1, source_target_pairs={{0,8},{1,9},{2,10},{3,11},{4,12},{5,13},{6,14},{7,15},{8,0},{9,1},... | collective-permute-start | bytes 24584 | tf_op jit(solution)/shard_map/ppermute | solution.py:457
  280.7 13.2 %copy-start.1 = (bf16[96,3072]{1,0:T(8,128)(2,1)S(1)}, bf16[96,3072]{1,0:T(8,128)(2,1)}, u32[]{:S(2)}) copy-start(bf16[96,3072]{1,0:T(8,128)(2,1)} %param.22) | copy-start | bytes 1769476
  283.7 8.3 %collective-permute-start.49 = (bf16[24,2304]{1,0:T(8,128)(2,1)S(1)}, bf16[24,2304]{1,0:T(8,128)(2,1)S(1)}, u32[]{:S(2)}, u32[]{:S(2)}) collective-permute-start(bf16[24,2304]{1,0:T(8,128)(2,1)S(1)} %add_convert_fusion.10), channel_id=1, source_target_pairs={{0,16},{1,17},{2,18},{3,19},{4,20},{5,21},{6,22},{7,23},{8,24},{9,... | collective-permute-start | bytes 331784 | tf_op jit(solution)/shard_map/ppermute | solution.py:457
  285.7 5.0 %collective-permute-start.48 = (f32[16,128]{1,0:T(8,128)S(1)}, f32[16,128]{1,0:T(8,128)S(1)}, u32[]{:S(2)}, u32[]{:S(2)}) collective-permute-start(f32[16,128]{1,0:T(8,128)S(1)} %add.473), channel_id=1, source_target_pairs={{0,16},{1,17},{2,18},{3,19},{4,20},{5,21},{6,22},{7,23},{8,24},{9,... | collective-permute-start | bytes 24584 | tf_op jit(solution)/shard_map/ppermute | solution.py:457
  (25 other events, 99.1 us)
where the time goes:
time: 295 us; the launch traced here: 294 us
  Pallas kernels  113 us (38%)
  waiting for transfers between devices  81.8 us (28%)
  starting transfers between devices  48.7 us (17%)
  other arithmetic  28.8 us (10%)
  local copies, waits for them, and re-layouts  20.2 us (7%)
    ppermute x53, waiting for transfers between devices, move(): return lax.ppermute(value, ('batch', 'seq'), pairs)  81.8 us
    ppermute x53, starting transfers between devices, move(): return lax.ppermute(value, ('batch', 'seq'), pairs)  48.7 us
    pallas_call x1, Pallas kernels, on_device(): pl.pallas_call(functools.partial(down_kernel, [entry[1:] for entry in gat...  20.5 us
    convert_element_type x12, other arithmetic, outgoing(): total(*[value[self.rows // 2:self.rows] for value in self.held])  20.3 us
    pallas_call x2, Pallas kernels, back(): pl.pallas_call(back_kernel, name='back', grid=(pairs,), out_shape=(*(shap...  16.3 us
    pallas_call x1, Pallas kernels, on_device(): pl.pallas_call(functools.partial(up_kernel, [entry[1:] for entry in gathe...  14.6 us
    unnamed x81, local copies, waits for them, and re-layouts  13.2 us
    pallas_call x2, Pallas kernels, attend(): pl.pallas_call(functools.partial(attention_kernel, i * pairs), name='atte...  11.6 us
  transfers between devices with their start and end apart: 53, of which 20 were waited for; matrix products, arithmetic and copies ran while one was open for 11% of the time, Pallas kernels for 26%

commit v1 on v0

--- a/solution.py
+++ b/solution.py
@@ -49,12 +49,17 @@
     return pl.CostEstimate(flops=int(microseconds * 1e9), bytes_accessed=int(microseconds * 3.5e6), transcendentals=0)
 
 
-def pack_kernel(where, hidden_ref, grad_ref, keep_ref, mate_ref, away_ref):
+def pack_kernel(where, hidden_ref, grad_ref, *refs):
+    for source, (keep_ref, mate_ref, away_ref) in ((hidden_ref, refs[:3]), (grad_ref, refs[3:])):
+        for rel in range(4):
+            target = (keep_ref, mate_ref, away_ref.at[0], away_ref.at[1])[rel]
+            target[...] = source[where[1] ^ rel].astype(BF16)
+
+
+def row_of(where, refs, out):
     for rel in range(4):
-        row = where[1] ^ rel
-        target = (keep_ref, mate_ref, away_ref.at[0], away_ref.at[1])[rel]
-        target[0] = hidden_ref[row].astype(BF16)
-        target[1] = grad_ref[row].astype(BF16)
+        source = (refs[0], refs[1], refs[2].at[0], refs[3])[rel]
+        out[where[1] ^ rel] = source[...]
 
 
 def unpack_kernel(where, old_ref, keep_ref, mate_ref, away_ref, far_ref, new_ref):
@@ -72,26 +77,42 @@
         target[...] = hold_ref[where[1] ^ rel]
 
 
-def fill(where, pieces, out, rows_last):
+def fill(where, pattern, refs, out, rows_last):
     b, s = where[0], where[1]
     parts, shards = (out.shape[1], out.shape[0]) if rows_last else (out.shape[0], out.shape[1])
-    for ref, flip, base in pieces:
+    size = out.shape[2] if rows_last else out.shape[3]
+    rows = out.shape[2]
+    for p in range(parts):
+        if rows_last:
+            out[b, p] = refs[0][p * size : (p + 1) * size, :]
+        else:
+            out[p, b] = refs[0][:, p * size : (p + 1) * size]
+    for ref, (flip, base) in zip(refs[1:], pattern):
         core = (s ^ flip) % 2
         part = (s ^ flip) if parts == 4 else core
         for i in range(ref.shape[0]):
             t = b ^ where[2 + core * shards + base + i]
             if rows_last:
-                out[t, part] = ref[i]
+                out[t, part] = ref[i, :rows, :]
             else:
-                out[part, t] = ref[i]
+                out[part, t] = ref[i, :rows, :]
+
+
+def fill_rows(where, pattern, refs, out, first):
+    b, s = where[0], where[1]
+    shard = refs[0].shape[0]
+    shards = out.shape[0] // shard
+    quarter = shard // 4
+    out[pl.ds(pl.multiple_of(b * shard, 8), shard), :] = refs[0][...].astype(F32)
+    for ref, (flip, base) in zip(refs[1:], pattern):
+        for i in range(ref.shape[0]):
+            t = b ^ where[2 + (s ^ flip) % 2 * shards + base + i]
+            low = pl.multiple_of(t * shard + (s ^ flip) * quarter, 8)
+            out[pl.ds(low, quarter), :] = ref[i, first : first + quarter, :].astype(F32)
 
 
 def flat(ref):
     return ref[...].reshape(-1, ref.shape[-1])
-
-
-def weight_kernel(pattern, rows_last, where, *refs):
-    fill(where, [(ref, *entry) for ref, entry in zip(refs, pattern)], refs[-1], rows_last)
 
 
 def columns_of(w_ref, start, stop):
@@ -145,18 +166,13 @@
 
 
 def qkv_kernel(pattern, shard, where, keep_ref, mate_ref, away_ref, far_ref, perm_ref, *refs):
-    count = len(pattern) if pattern else 1
-    qkv_ref, first_t_ref, x_ref, glow_ref, gains_ref = refs[count : count + 5]
-    w_ref = refs[count + 5] if pattern else refs[0]
+    count = len(pattern) + 1 if pattern else 1
+    qkv_ref, first_t_ref, x_ref, gains_ref = refs[count : count + 4]
+    w_ref = refs[count + 4] if pattern else refs[0]
     if pattern:
-        fill(where, [(ref, *entry) for ref, entry in zip(refs, pattern)], w_ref, False)
-    size = keep_ref.shape[1]
-    width = keep_ref.shape[2]
-    for rel in range(4):
-        block = where[1] ^ rel
-        source = (keep_ref, mate_ref, away_ref.at[0], far_ref)[rel]
-        x_ref[block] = source[0]
-        glow_ref[block] = source[1]
+        fill(where, pattern, refs[:count], w_ref, False)
+    size, width = keep_ref.shape
+    row_of(where, (keep_ref, mate_ref, away_ref, far_ref), x_ref)
     gains = gains_of(w_ref, width, shard)
     gains_ref[...] = gains
     x = x_ref[...].reshape(4 * size, width).astype(F32)
@@ -169,7 +185,7 @@
 
 def gains_of(w_ref, width, shard):
     size = w_ref.shape[-1]
-    spare = w_ref[4 * width // size, :, :, 4 * width % size : 4 * width % size + TILE].astype(F32)
+    spare = w_ref[3 * width // size, :, :, 3 * width % size : 3 * width % size + TILE].astype(F32)
     rows = width // TILE
     if spare.shape[0] > 1:
         together = jnp.sum(spare, axis=0)
@@ -218,10 +234,17 @@
     ctx_ref[...] = jnp.where(lane < HEAD_DIM, halves[0], halves[1]).astype(BF16)
 
 
-def out_kernel(x_ref, ctx_a_ref, ctx_b_ref, w_ref, gains_ref, perm_ref, attn_ref, second_ref, second_t_ref):
-    width = x_ref.shape[1]
+def out_kernel(pattern, where, x_ref, ctx_a_ref, ctx_b_ref, gains_ref, perm_ref, *refs):
+    count = len(pattern) + 1 if pattern else 1
+    attn_ref, second_ref, second_t_ref = refs[count : count + 3]
+    if pattern:
+        w_ref, hold_ref = refs[count + 3 : count + 5]
+        fill_rows(where, pattern, refs[:count], hold_ref, refs[1].shape[1] - refs[0].shape[0] // 4)
+        w_ref[...] = hold_ref[...].astype(BF16)
+    else:
+        w_ref = refs[0]
     ctx = jnp.concatenate([ctx_a_ref[...], ctx_b_ref[...]], axis=1)
-    attn = times_columns(ctx, w_ref, 3 * width, 4 * width)
+    attn = nn(ctx, w_ref[...])
     attn_ref[...] = attn
     middle = x_ref[...].astype(F32) + attn
     r2 = lax.rsqrt(jnp.mean(middle * middle, axis=-1, keepdims=True) + EPS)
@@ -230,37 +253,44 @@
     second_t_ref[...] = nt(perm_ref[...], second).astype(BF16)
 
 
-def up_kernel(pattern, place, where, second_ref, glow_ref, *refs):
+def up_kernel(pattern, place, where, second_ref, keep_ref, mate_ref, away_ref, far_ref, *refs):
+    glow_ref = refs[-1]
+    refs = refs[:-1]
+
+    @pl.when(pl.program_id(0) == 0)
+    def _():
+        row_of(where, (keep_ref, mate_ref, away_ref, far_ref), glow_ref)
+
     if pattern:
         w_ref = refs[-1]
 
         @pl.when(pl.program_id(0) == 0)
         def _():
-            fill(where, [(ref, *entry) for ref, entry in zip(refs, pattern)], w_ref, False)
+            fill(where, pattern, refs[: len(pattern) + 1], w_ref, False)
 
         weight = w_ref[pl.program_id(0)]
-        act_ref, slope_ref, keep_ref, send_ref = refs[len(pattern) : len(pattern) + 4]
+        act_ref, slope_ref, wd_keep_ref, wd_send_ref = refs[len(pattern) + 1 : len(pattern) + 5]
         weight = weight.reshape(-1, weight.shape[-1])
     else:
         weight = flat(refs[0])
-        act_ref, slope_ref, keep_ref, send_ref = refs[1:]
+        act_ref, slope_ref, wd_keep_ref, wd_send_ref = refs[1:]
     up = nn(second_ref[...], weight)
     phi_cap = 0.5 * (1.0 + lax.erf(up * 0.7071067811865476))
     act = (up * phi_cap).astype(BF16)
     act_ref[...] = act
     slope = phi_cap + up * (jnp.exp(-0.5 * up * up) * 0.3989422804014327)
     slope_ref[...] = slope.astype(BF16)
-    dwd = tn(act, glow_ref[...])
-    if len(keep_ref.shape) == 2:
-        keep_ref[...] = dwd.astype(BF16)
+    dwd = tn(act, flat(glow_ref))
+    if len(wd_keep_ref.shape) == 2:
+        wd_keep_ref[...] = dwd.astype(BF16)
     else:
-        rows = keep_ref.shape[-2]
+        rows = wd_keep_ref.shape[-2]
         blocks = [dwd[i * rows : (i + 1) * rows].astype(BF16) for i in range(8)]
         for axis, bit in ((1, 4), (2, 2), (3, 1)):
             flip = place[axis] == 1
             blocks = [jnp.where(flip, blocks[i ^ bit], blocks[i]) for i in range(8)]
         core = place[3]
-        for ref, c_rel in ((keep_ref, 0), (send_ref, 1)):
+        for ref, c_rel in ((wd_keep_ref, 0), (wd_send_ref, 1)):
             x_outer = core == c_rel
             for i in range(2):
                 for j in range(2):
@@ -271,14 +301,14 @@
 def down_kernel(pattern, where, second_t_ref, glow_ref, attn_ref, act_ref, slope_ref, win_ref, *refs):
     j = pl.program_id(0)
     win = flat(win_ref)
-    count = len(pattern) if pattern else 1
+    count = len(pattern) + 1 if pattern else 1
     keep_ref, mate_ref, away_ref, dsec_ref, win_keep_ref, win_send_ref, acc_ref, dacc_ref, hold_ref = refs[count : count + 9]
     if pattern:
         w_ref = refs[-1]
 
         @pl.when(j == 0)
         def _():
-            fill(where, [(ref, *entry) for ref, entry in zip(refs, pattern)], w_ref, True)
+            fill(where, pattern, refs[:count], w_ref, True)
 
         shards = w_ref.shape[0] // 4
         wd = w_ref[pl.ds(j * shards, shards)]
@@ -323,7 +353,7 @@
     gmd = r2 * (scaled - normed * jnp.mean(scaled * normed, axis=-1, keepdims=True))
     gmd_ref[...] = gmd
     low = (glow_ref[...].astype(F32) + gmd).astype(BF16)
-    dctx_ref[...] = times_transposed(low, w_ref, 3 * low.shape[1], 4 * low.shape[1]).astype(BF16)
+    dctx_ref[...] = nt(low, w_ref[...]).astype(BF16)
     ctx_t = nt(perm_ref[...], jnp.concatenate([ctx_a_ref[...], ctx_b_ref[...]], axis=1)).astype(BF16)
     dw = nn(ctx_t, low).astype(BF16)
     half = dw.shape[0] // 2
@@ -398,7 +428,7 @@
 
 def first_kernel(
     where, x_ref, gains_ref, dqa_ref, dqb_ref, dka_ref, dkb_ref, dva_ref, dvb_ref, w_ref, gmd_ref,
-    row_keep_ref, row_mate_ref, row_away_ref, g1_ref, hold_ref,
+    g2_ref, sums_a_ref, sums_b_ref, row_keep_ref, row_mate_ref, row_away_ref, small_ref, hold_ref,
 ):
     width = x_ref.shape[1]
     x = x_ref[...].astype(F32)
@@ -406,7 +436,27 @@
     normed = x * r1
     refs = (dqa_ref, dqb_ref, dka_ref, dkb_ref, dva_ref, dvb_ref)
     dfirst = times_transposed(jnp.concatenate([ref[...] for ref in refs], axis=1), w_ref, 0, 3 * width)
-    g1_ref[...] = jnp.sum(dfirst * normed, axis=0, keepdims=True)
+    lines = width // TILE
+    for i, gain_grad in enumerate((jnp.sum(dfirst * normed, axis=0, keepdims=True), g2_ref[...])):
+        for k in range(lines):
+            small_ref[i * lines + k : i * lines + k + 1, :] = gain_grad[:, k * TILE : (k + 1) * TILE]
+    picked = [[], [], []]
+    for ref in (sums_a_ref, sums_b_ref):
+        for p in range(ref.shape[0]):
+            picked[0].append(ref[p, 0:2])
+            picked[1].append(ref[p, 2:4] + ref[p, 4:6])
+            picked[2].append(ref[p, 6:8])
+    near, below, above = (jnp.concatenate(part, axis=0) for part in picked)
+    square = (3 * TILE, TILE)
+    offset = lax.broadcasted_iota(jnp.int32, square, 0) - (TILE - 1)
+    offset = jnp.where(offset < 0, offset + 3 * TILE, offset) - TILE
+    bucket = lax.broadcasted_iota(jnp.int32, square, 1)
+    choice = (bucket_of(offset) == bucket).astype(F32)
+    table = lax.dot_general(near, choice, (((1,), (0,)), ((), ())), precision=HIGHEST, preferred_element_type=F32)
+    lane = lax.broadcasted_iota(jnp.int32, table.shape, 1)
+    table = table + jnp.where(lane == 15, jnp.sum(below, axis=-1, keepdims=True), 0.0)
+    table = table + jnp.where(lane == 31, jnp.sum(above, axis=-1, keepdims=True), 0.0)
+    small_ref[2 * lines : 2 * lines + HEADS, :] = table
     scaled = dfirst * gains_ref[:1]
     delta = gmd_ref[...] + r1 * (scaled - normed * jnp.mean(scaled * normed, axis=-1, keepdims=True))
     place_rows(where, delta, row_keep_ref, row_mate_ref, row_away_ref, hold_ref)
@@ -468,40 +518,34 @@
 
     tiled = (shard // 2) % 16 == 0
 
-    def plain(pieces, rows_last=False):
+    def plain(local, pieces, axis=1, low=0, high=None):
         parts = 4 if any(entry[1] > 1 for entry in pieces) else 2
-        dims = pieces[0][0].shape[1:]
-        full = jnp.zeros((parts, nb) + dims, BF16)
+        own = jnp.stack(jnp.split(local, parts, axis))
+        full = jnp.zeros((parts, nb) + own.shape[1:], BF16).at[:, b].set(own)
         for array, flip, base in pieces:
             part = s ^ flip if parts == 4 else (s ^ flip) % 2
             shards = b ^ jnp.where((s ^ flip) % 2 == 0, jnp.array(masks(0)), jnp.array(masks(1)))
-            full = full.at[part, shards[base : base + array.shape[0]]].set(array)
-        if rows_last:
+            full = full.at[part, shards[base : base + array.shape[0]]].set(array[:, low:high])
+        if axis == 0:
             return jnp.swapaxes(full, 0, 1)
-        return full.reshape(parts, 1, nb * dims[0], dims[1])
-
-    def assemble(name, pieces, rows_last=False):
-        if not tiled:
-            return plain(pieces, rows_last)
-        arrays = [entry[0] for entry in pieces]
-        parts = 4 if any(entry[1] > 1 for entry in pieces) else 2
-        return pl.pallas_call(
-            functools.partial(weight_kernel, [entry[1:] for entry in pieces], rows_last),
-            name=name,
-            out_shape=shape(((nb, parts) if rows_last else (parts, nb)) + arrays[0].shape[1:], BF16),
-            in_specs=[smem] + [vmem] * len(arrays),
-            cost_estimate=cost(5),
-            compiler_params=params(),
-        )(where, *arrays)
+        return full.reshape(parts, 1, -1, own.shape[2])
+
+    class Gather:
+        def __init__(self, block):
+            self.block, self.brought = block, []
+
+        def start(self):
+            self.brought.append(step(self.block, len(self.brought)))
+            return self.brought[-1]
+
+        def grow(self, *gates):
+            self.brought[-1] = after(self.brought[-1], *gates) if gates else self.brought[-1]
+            self.block = jnp.concatenate([self.block, self.brought[-1]])
+            return self.block
 
     vmem = pl.BlockSpec(memory_space=pltpu.VMEM)
     smem = pl.BlockSpec(memory_space=pltpu.SMEM)
     stages = len(bits) + 1
-
-    def grow(block, start, stop, *gates):
-        for i in range(start, stop):
-            block = jnp.concatenate([block, after(step(block, i), *gates)])
-        return block
 
     per = width // (nb * ns)
     feature = jnp.arange(width)
@@ -518,13 +562,14 @@
     own = jnp.zeros((2, width), BF16)
     own = lax.dynamic_update_slice(own, jnp.stack([gain_attn, gain_ffn]), (0, b * shard)).reshape(-1, TILE)
     own = jnp.pad(own, ((0, shard - own.shape[0]), (0, TILE)))
-    block1 = piece(jnp.concatenate([w_query, w_key, w_value, w_out, own], axis=1), 2)
-    row_keep, row_mate, row_away = pl.pallas_call(
+    local1 = jnp.concatenate([w_query, w_key, w_value, own], axis=1)
+    one = Gather(piece(local1, 4))
+    one.start()
+    row_shapes = (shape((shard_len, width), BF16),) * 2 + (shape((2, shard_len, width), BF16),)
+    row_keep, row_mate, row_away, grad_keep, grad_mate, grad_away = pl.pallas_call(
         pack_kernel,
         name="pack",
-        out_shape=(
-            shape((2, shard_len, width), BF16), shape((2, shard_len, width), BF16), shape((2, 2, shard_len, width), BF16),
-        ),
+        out_shape=row_shapes * 2,
         in_specs=[smem, vmem, vmem],
         cost_estimate=cost(3),
         compiler_params=params(),
@@ -541,37 +586,61 @@
         cost_estimate=cost(6),
         compiler_params=params(),
     )(where, doc_lengths, bias_table, position)
-    start1 = grow(block1, 0, 1)
-    low1 = grow(start1, 1, stages - 1, row_got, band)
-    high1 = step(low1, stages - 1)
+    def tagged(arrays, flip):
+        return [(array, flip, 1 << i) for i, array in enumerate(arrays)]
+
+    y_one = [other_y(one.brought[0])]
+    while len(one.brought) < stages - 1:
+        one.grow()
+        one.start()
+        if len(one.brought) < stages - 1:
+            y_one.append(other_y(one.brought[-1]))
+    one.grow(band, row_got, *y_one)
+    one.start()
+    y_one.append(other_y(one.brought[-2]))
+    core_one = [core(array) for array in one.brought[:-1]]
+    two = Gather(jnp.concatenate([piece(after(w_in, one.block), 4), piece(w_out, 4, 0)], axis=1))
+    two.start()
+    one.brought[-1] = after(one.brought[-1], *y_one, *core_one)
+    core_one.append(core(one.brought[-1]))
+    y_one.append(after(other_y(one.brought[-1]), two.brought[0]))
     row_mate, row_far = core(row_mate), core(row_got[1])
-    low2 = grow(piece(after(w_in, start1), 4), 0, stages - 1)
-    high1 = after(high1, low2)
-    gather1 = [(low1, 0, 0), (high1, 0, nb // 2), (core(low1), 1, 0), (core(high1), 1, nb // 2)]
-    high2 = step(low2, stages - 1)
-    y_low2 = other_y(low2)
-    block3 = piece(after(w_down, low2), 4, 0)
-    gather1[0] = (after(low1, block3), 0, 0)
+    while len(two.brought) < stages - 1:
+        two.grow()
+        two.start()
+    two.grow()
+    y_two = [other_y(after(array, y_one[-1])) for array in two.brought]
+    two.start()
+    three = Gather(piece(after(w_down, two.block), 2, 0))
+    three.start()
+    gather1 = tagged(one.brought, 0) + tagged(core_one, 1) + tagged(y_one, 2) + tagged([core(array) for array in y_one], 3)
+    part = ff // 4
+
     row_block = shape((4, shard_len, width), BF16)
-    w1_shape = shape((2, nb) + low1.shape[1:], BF16)
-    pieces1 = [entry[0] for entry in gather1] if tiled else [plain(gather1)]
+    w1_shape = shape((4, nb) + one.block.shape[1:], BF16)
+    pieces1 = [local1] + [entry[0] for entry in gather1] if tiled else [plain(local1, gather1)]
     outputs = pl.pallas_call(
         functools.partial(qkv_kernel, [entry[1:] for entry in gather1] if tiled else None, shard),
         name="qkv",
         out_shape=(
-            shape((length, 3 * width), BF16), shape((width, length), BF16), row_block, row_block, shape((2, width), F32),
+            shape((length, 3 * width), BF16), shape((width, length), BF16), row_block, shape((2, width), F32),
             *([w1_shape] if tiled else []),
         ),
         in_specs=[smem] + [vmem] * (5 + len(pieces1)),
         cost_estimate=cost(9),
         compiler_params=params(),
-    )(where, row_keep, row_mate, row_got, row_far, perm, *pieces1)
-    qkv, first_t, xb, glow, gains = outputs[:5]
-    w1 = outputs[5] if tiled else pieces1[0]
-    xb, glow = xb.reshape(length, width), glow.reshape(length, width)
-
-    y_high2 = other_y(after(high2, qkv))
-    mid3 = grow(block3, 0, stages - 2, qkv)
+    )(where, row_keep, row_mate, row_got, row_far, perm, after(pieces1[0], two.block, three.block), *pieces1[1:])
+    qkv, first_t, xb, gains = outputs[:4]
+    w1 = outputs[4] if tiled else pieces1[0]
+    xb = xb.reshape(length, width)
+
+    two.brought[-1] = after(two.brought[-1], qkv)
+    y_two.append(other_y(two.brought[-1]))
+    grad_got = other_y(after(grad_away, two.brought[-1]))
+    while len(three.brought) < stages - 2:
+        three.grow(qkv)
+        three.start()
+    three.grow(qkv)
 
     pairs = HEADS // 4
     pair_block = lambda first: pl.BlockSpec((length, TILE), lambda p: (0, first + p))
@@ -594,32 +663,38 @@
             compiler_params=params(),
         )(qkv, qkv, qkv, gated, bias_table, seg_queries, seg_keys)
 
-    probs_a, ctx_a = attend(0, after(band, high2, mid3, y_low2))
-    low3 = grow(mid3, stages - 2, stages - 1, ctx_a)
-    probs_b, ctx_b = attend(1, after(band, low3, y_high2))
-    high3 = after(step(low3, stages - 1), ctx_b)
-    y_low3 = other_y(after(low3, y_high2))
-    y_high3 = other_y(high3)
-    gather3 = [
-        (low3, 0, 0), (high3, 0, nb // 2), (core(low3), 1, 0), (core(high3), 1, nb // 2),
-        (y_low3, 2, 0), (y_high3, 2, nb // 2), (core(y_low3), 3, 0), (core(y_high3), 3, nb // 2),
-    ]
-
-    gather2 = [
-        (low2, 0, 0), (high2, 0, nb // 2), (core(low2), 1, 0), (core(high2), 1, nb // 2),
-        (y_low2, 2, 0), (y_high2, 2, nb // 2),
-        (core(after(y_low2, qkv)), 3, 0), (core(after(y_high2, ctx_a)), 3, nb // 2),
-    ]
-    attn, second, second_t = pl.pallas_call(
-        out_kernel,
+    probs_a, ctx_a = attend(0, after(band, two.brought[-1], three.block, *y_two[:-1]))
+    probs_b, ctx_b = attend(1, after(band, ctx_a))
+    three.start()
+    three.grow(ctx_b)
+    y_two_core = [core(after(array, ctx_b)) for array in y_two]
+    gather2 = tagged(two.brought, 0) + tagged([core(array) for array in two.brought], 1) + tagged(y_two, 2) + tagged(y_two_core, 3)
+    pattern2 = [entry[1:] for entry in gather2]
+    arrays2 = [entry[0] for entry in gather2]
+    if tiled:
+        wo_pieces = [w_out] + arrays2
+    else:
+        wo_pieces = [plain(w_out, gather2, 0, shard).reshape(width, width)]
+    outputs = pl.pallas_call(
+        functools.partial(out_kernel, pattern2 if tiled else None),
         name="out",
-        out_shape=(shape((length, width), F32), shape((length, width), BF16), shape((width, length), BF16)),
-        cost_estimate=cost(5),
+        out_shape=(
+            shape((length, width), F32), shape((length, width), BF16), shape((width, length), BF16),
+            *([shape((width, width), BF16)] if tiled else []),
+        ),
+        in_specs=[smem] + [vmem] * (5 + len(wo_pieces)),
+        scratch_shapes=[pltpu.VMEM((width, width), F32)] if tiled else [],
+        cost_estimate=cost(6),
         compiler_params=params(),
-    )(xb, after(ctx_a, high3), ctx_b, w1, gains, perm)
+    )(where, xb, after(ctx_a, three.block), ctx_b, gains, perm, *wo_pieces)
+    attn, second, second_t = outputs[:3]
+    wo = outputs[3] if tiled else wo_pieces[0]
+    high3 = three.start()
+    grad_got = after(grad_got, second)
+    grad_mate, grad_far = core(after(grad_mate, ctx_b)), core(grad_got[1])
+    gather3 = tagged(three.brought, 0) + tagged([core(array) for array in three.brought], 1)
 
     steps = 4
-    part = ff // steps
     per_down = ff // (nb * ns)
     aligned = nb == 2 * steps and per_down % 16 == 0
     if aligned:
@@ -639,44 +714,49 @@
         )
     place = jnp.stack([b // 2, b % 2, y, c]).astype(jnp.int32)
     full = lambda *dims: pl.BlockSpec(dims, lambda j, *place: (0,) * len(dims))
+    row_specs = (full(shard_len, width), full(shard_len, width), full(2, shard_len, width))
     half = width // 2
     column_block = lambda r: pl.BlockSpec((r, part), lambda j, *place: (0, j))
-    win_shape = (4, nb) + low2.shape[1:]
-    pieces2 = [entry[0] for entry in gather2] if tiled else [plain(gather2)]
+    win_shape = (4, nb, shard, part)
+    pieces2 = [w_in] + arrays2 if tiled else [plain(w_in, gather2, 1, 0, shard)]
     win_shape = win_shape if tiled else pieces2[0].shape
     win_block = pl.BlockSpec((1,) + win_shape[1:], lambda j, *place: (j, 0, 0, 0))
     always = lambda array: pl.BlockSpec(array.shape, lambda j, *place: (0,) * array.ndim)
     outputs = pl.pallas_call(
-        functools.partial(up_kernel, [entry[1:] for entry in gather2] if tiled else None),
+        functools.partial(up_kernel, pattern2 if tiled else None),
         name="up",
         out_shape=(
-            shape((length, ff), BF16), shape((length, ff), BF16), *wd_shapes, *([shape(win_shape, BF16)] if tiled else []),
+            shape((length, ff), BF16), shape((length, ff), BF16), *wd_shapes, *([shape(win_shape, BF16)] if tiled else []), row_block,
         ),
         grid_spec=pltpu.PrefetchScalarGridSpec(
             num_scalar_prefetch=1,
             grid=(steps,),
-            in_specs=[smem, full(length, width), full(length, width)]
+            in_specs=[smem, full(length, width), *row_specs[:2], row_specs[2], row_specs[0]]
             + ([always(array) for array in pieces2] if tiled else [win_block]),
             out_specs=(
-                column_block(length), column_block(length), *wd_blocks, *([full(*win_shape)] if tiled else []),
+                column_block(length), column_block(length), *wd_blocks, *([full(*win_shape)] if tiled else []), full(*row_block.shape),
             ),
         ),
         cost_estimate=cost(10),
         compiler_params=params(),
-    )(place, where, after(second, y_low3, y_high3), glow, *pieces2)
+    )(place, where, second, grad_keep, grad_mate, grad_got, grad_far, *pieces2)
     act, slope, wd_keep, wd_send = outputs[:4]
     win = outputs[4] if tiled else pieces2[0]
+    glow = outputs[-1].reshape(length, width)
 
     scatter_masks = [((1, 0), (0, 2)), ((0, 2), (1, 0))] + [((bit, 0), (bit, 0)) for bit in bits]
 
     class Scatter:
         def __init__(self, *held):
-            self.held = list(held)
-            self.rows = held[0].shape[0]
+            self.held = [value if isinstance(value, tuple) else (value,) for value in held]
+            self.rows = self.held[0][0].shape[0]
+            self.widths = [value.shape[1] for value in self.held[0]]
             self.i = 0
 
         def outgoing(self):
-            self.sent = total(*[value[self.rows // 2 : self.rows] for value in self.held]).astype(BF16)
+            rows = slice(self.rows // 2, self.rows)
+            groups = [total(*[value[rows] for value in group]).astype(BF16) for group in zip(*self.held)]
+            self.sent = groups[0] if len(groups) == 1 else jnp.concatenate(groups, axis=1)
             return self.sent
 
         def send(self):
@@ -685,10 +765,13 @@
         def take(self, *gates):
             self.i += 1
             self.rows //= 2
-            self.held.append(after(self.got, *gates))
+            got = after(self.got, *gates)
+            starts = [sum(self.widths[:k]) for k in range(len(self.widths))]
+            self.held.append(tuple(got[:, low : low + size] for low, size in zip(starts, self.widths)))
 
         def result(self):
-            return total(*[value[: self.rows] for value in self.held])
+            groups = [total(*[value[: self.rows] for value in group]) for group in zip(*self.held)]
+            return groups[0] if len(groups) == 1 else groups
 
     if not aligned:
         blocks = wd_keep.reshape(nb, ns, per_down, width)
@@ -705,15 +788,13 @@
 
         wd_keep, wd_send = order(c), order(1 - c)
     wd_keep, wd_send = wd_keep.reshape(ff // 2, width), wd_send.reshape(ff // 2, width)
-    down = Scatter(wd_keep, core(wd_send))
+    down = Scatter(wd_keep, core(after(wd_send, high3)))
     down_sent = down.outgoing()
     down.send()
 
-    pieces3 = [entry[0] for entry in gather3] if tiled else [plain(gather3, True)]
-    wd_dims = (nb, 4) + low3.shape[1:]
+    pieces3 = [w_down] + [entry[0] for entry in gather3] if tiled else [plain(w_down, gather3, 0)]
+    wd_dims = (nb, 2) + three.block.shape[1:]
     wd_spec = pl.BlockSpec((nb // steps,) + wd_dims[1:], lambda j: (j, 0, 0, 0))
-    row_shapes = (shape((shard_len, width), BF16),) * 2 + (shape((2, shard_len, width), BF16),)
-    row_specs = (full(shard_len, width), full(shard_len, width), full(2, shard_len, width))
     hold = pltpu.VMEM((4, shard_len, width), BF16)
     out_keep, out_mate, out_away, dsec, win_keep, win_send = pl.pallas_call(
         functools.partial(down_kernel, [entry[1:] for entry in gather3] if tiled else None),
@@ -733,6 +814,9 @@
         compiler_params=params(),
     )(where, second_t, glow, attn, after(act, down_sent), slope, win, *pieces3)
     win_got = core(win_send)
+    down.take(dsec)
+    down_sent = down.outgoing()
+    down.send()
     out_got = other_y(out_away)
 
     gmd, g2, dctx, wo_keep, wo_send = pl.pallas_call(
@@ -744,14 +828,12 @@
         ),
         cost_estimate=cost(7),
         compiler_params=params(),
-    )(xb, attn, gains, dsec, glow, ctx_a, ctx_b, perm, w1)
+    )(xb, attn, gains, after(dsec, down_sent), glow, ctx_a, ctx_b, perm, wo)
     wo_got = core(wo_send)
-    both = Scatter(
-        jnp.concatenate([win_keep, wo_keep], axis=1), jnp.concatenate([after(win_got, dctx), wo_got], axis=1)
-    )
+    both = Scatter((win_keep, wo_keep), (after(win_got, dctx), wo_got))
     both_sent = both.outgoing()
     both.send()
-    down.take(both_sent)
+    down.take(dctx)
     down_sent = down.outgoing()
     down.send()
 
@@ -781,11 +863,8 @@
     both.take(dq_b)
     both_sent = both.outgoing()
     both.send()
-    down.take(dq_b)
-    down_sent = down.outgoing()
-    down.send()
-
-    grads = (after(dq_a, down_sent, both_sent), dq_b, dk_a, dk_b, dv_a, dv_b)
+
+    grads = (after(dq_a, both_sent), dq_b, dk_a, dk_b, dv_a, dv_b)
     keep, send = pl.pallas_call(
         grad_kernel,
         name="grad",
@@ -797,61 +876,33 @@
     both.take(send)
     both_sent = both.outgoing()
     both.send()
-    in_keep, in_mate, in_away, g1 = pl.pallas_call(
+    last = Scatter(keep, after(last_got, both_sent))
+    last_sent = last.outgoing()
+    last.send()
+    small_lines = 2 * width // TILE
+    in_keep, in_mate, in_away, small = pl.pallas_call(
         first_kernel,
         name="first",
-        out_shape=(*row_shapes, shape((1, width), F32)),
-        in_specs=[smem] + [vmem] * 10,
+        out_shape=(*row_shapes, shape((small_lines + HEADS, TILE), F32)),
+        in_specs=[smem] + [vmem] * 13,
         scratch_shapes=[hold],
-        cost_estimate=cost(6),
+        cost_estimate=cost(7),
         compiler_params=params(),
-    )(where, xb, gains, after(grads[0], send, both_sent), *grads[1:], w1, gmd)
-    last = Scatter(keep, after(last_got, g1))
+    )(where, xb, gains, after(grads[0], last_sent), *grads[1:], w1, gmd, g2, sums_a, sums_b)
+    last.got = after(last.got, both.got)
+    in_got = other_y(after(in_away, last.got))
+    small = after(small, last.got)
+    last.take()
     last_sent = last.outgoing()
     last.send()
+    op2_sent = last_sent
     both.take(last_sent)
-    while both.i < stages + 1:
+    while both.i < stages:
         both.outgoing()
         both.send()
         both.take()
-    op1_sent = last_sent
-    in_got = other_y(after(in_away, last_sent))
-
-    sums = jnp.concatenate([sums_a, after(sums_b, last_sent)])
-    near = sums[:, :2].reshape(HEADS, 3 * TILE)
-    outer = jnp.sum(sums[:, 2:], axis=-1).reshape(HEADS // 2, 3, 2)
-    below, above = (outer[:, 0] + outer[:, 1]).reshape(HEADS), outer[:, 2].reshape(HEADS)
-    offset_bucket = bucket_of((jnp.arange(3 * TILE) - (TILE - 1)) % (3 * TILE) - TILE)
-    bucket_column = jnp.arange(BUCKETS)[:, None]
-    table = jnp.dot((bucket_column == offset_bucket[None, :]).astype(F32), near.T, precision=HIGHEST)
-    table = table + jnp.where(bucket_column == 15, below, 0.0) + jnp.where(bucket_column == 31, above, 0.0)
-    table = jnp.pad(table.reshape(-1, TILE), ((0, 1), (0, 0)))
-    small = jnp.concatenate([g1.reshape(-1, TILE), g2.reshape(-1, TILE), table])
-    small_masks = [(0, 1), (0, 2), (1, 0)] + [(bit, 0) for bit in bits]
-
-    small = small + move(after(small, last_sent), small_masks[0])
-    last.take()
-    last_sent = last.outgoing()
-    small = small + move(after(small, last_sent), small_masks[1])
-    last.send()
-    for i in range(2, stages + 1):
-        last.take()
-        last_sent = last.outgoing()
-        last.send()
-        small = small + move(after(small, last_sent), small_masks[i])
-    small = small + move(small, small_masks[stages + 1])
-    last.take()
-    down.take(last_sent)
-    while down.i < stages + 1:
-        down.outgoing()
-        down.send()
-        down.take()
-    down_grad_w = down.result()
-    both_sum, last_sum = both.result(), last.result()
-    gain_rows_count = width // TILE
-    gain_grads = small[: 2 * gain_rows_count].reshape(2, width)
-    gain_grads = lax.dynamic_slice_in_dim(gain_grads, (b * ns + s) * per, per, 1)
-    table = small[2 * gain_rows_count : 2 * gain_rows_count + BUCKETS * HEADS // TILE].reshape(BUCKETS, HEADS)
+    both.outgoing()
+    both.send()
 
     def unpack(name, old, keep, mate, got):
         mate, far = core(after(mate, got)), core(got[1])
@@ -864,8 +915,37 @@
             compiler_params=params(),
         )(where, old, keep, mate, got, far)
 
-    out_hidden = unpack("out_rows", hidden_in, out_keep, out_mate, after(out_got, op1_sent))
-    input_grad = unpack("in_rows", out_grad, in_keep, in_mate, in_got)
+    out_hidden = unpack("out_rows", hidden_in, out_keep, out_mate, after(out_got, op2_sent))
+    small = small + move(small, (0, 1))
+    small = small + move(after(small, op2_sent), (1, 0))
+    last.take(out_hidden, small)
+    last.outgoing()
+    last.send()
+    both.take(last.sent)
+    down.take(last.sent)
+    while down.i < stages + 1:
+        down.outgoing()
+        down.send()
+        down.take()
+    input_grad = unpack("in_rows", out_grad, in_keep, in_mate, after(in_got, last.sent))
+    for bit in bits[:-1]:
+        small = small + move(after(small, last.sent), (bit, 0))
+    small = small + move(small, (0, 2))
+    last.take(input_grad, small)
+    last_sent = last.outgoing()
+    last.send()
+    small = small + move(after(small, last_sent), (bits[-1], 0))
+    last.take()
+    while last.i < stages + 1:
+        last.outgoing()
+        last.send()
+        last.take()
+    down_grad_w = down.result()
+    both_sum, last_sum = both.result(), last.result()
+    gain_grads = small[:small_lines].reshape(2, width)
+    gain_grads = lax.dynamic_slice_in_dim(gain_grads, (b * ns + s) * per, per, 1)
+    table = small[small_lines:, :BUCKETS].T
+
     return (
         out_hidden,
         input_grad,
@@ -875,8 +955,8 @@
         last_sum[:, :width],
         last_sum[:, width : 2 * width],
         last_sum[:, 2 * width :],
-        both_sum[:, ff:],
-        both_sum[:, :ff],
+        both_sum[1],
+        both_sum[0],
         down_grad_w,
     )
 

time: 295 us -> 269 us (0.912)
  waiting for transfers between devices: 81.8 us -> 69.2 us
  starting transfers between devices: 48.7 us -> 39.1 us
  local copies, waits for them, and re-layouts: 20.2 us -> 10.6 us
  other arithmetic: 28.8 us -> 35.4 us
    ppermute x53 -> x63, waiting for transfers between devices: 81.8 us -> 69.2 us  [move(): return lax.ppermute(value, ('batch', 'seq'), pairs)]
    ppermute x53 -> x63, starting transfers between devices: 48.7 us -> 39.1 us  [move(): return lax.ppermute(value, ('batch', 'seq'), pairs)]
    unnamed x81 -> x109, local copies, waits for them, and re-layouts: 13.2 us -> 5.36 us
    concatenate x7 -> x12, other arithmetic: 0.41 us -> 5.62 us  [the longest x4 3.16 us: outgoing(): jnp.concatenate(groups, axis=1)]
    add x3 -> x4, other arithmetic: 4.55 us -> 6.38 us  [total(): sums = sums + part.astype(F32)]
    convert_element_type x12 -> x16, other arithmetic: 20.3 us -> 20.2 us  [outgoing(): total(*[value[rows] for value in group]).astype(BF16)]
  transfers between devices with their start and end apart: 53 -> 63, of which waited for: 20 -> 26; matrix products, arithmetic and copies ran while one was open for 11% -> 12% of each run, Pallas kernels for 26% -> 42%
where the time goes in v1:
time: 269 us; the launch traced here: 268 us
  Pallas kernels  112 us (42%)
  waiting for transfers between devices  69.2 us (26%)
  starting transfers between devices  39.1 us (15%)
  other arithmetic  35.4 us (13%)
  local copies, waits for them, and re-layouts  10.6 us (4%)
    ppermute x63, waiting for transfers between devices, move(): return lax.ppermute(value, ('batch', 'seq'), pairs)  69.2 us
    ppermute x63, starting transfers between devices, move(): return lax.ppermute(value, ('batch', 'seq'), pairs)  39.1 us
    pallas_call x1, Pallas kernels, on_device(): pl.pallas_call(functools.partial(down_kernel, [entry[1:] for entry in gat...  20.3 us
    convert_element_type x16, other arithmetic, outgoing(): total(*[value[rows] for value in group]).astype(BF16)  20.2 us
    pallas_call x2, Pallas kernels, back(): pl.pallas_call(back_kernel, name='back', grid=(pairs,), out_shape=(*(shap...  16.3 us
    pallas_call x1, Pallas kernels, on_device(): pl.pallas_call(functools.partial(up_kernel, pattern2 if tiled else None),...  15 us
    pallas_call x2, Pallas kernels, attend(): pl.pallas_call(functools.partial(attention_kernel, i * pairs), name='atte...  11.8 us
    pallas_call x1, Pallas kernels, on_device(): pl.pallas_call(functools.partial(qkv_kernel, [entry[1:] for entry in gath...  9.07 us
  transfers between devices with their start and end apart: 63, of which 26 were waited for; matrix products, arithmetic and copies ran while one was open for 12% of the time, Pallas kernels for 42%

profile of v1, /device:TPU:0, one launch (start us, length us, event | category | flops | bytes accessed | tf_op | source)
XLA Modules:
  0.0 267.6 jit_solution(9007008317206894973)
XLA Ops:
  1.5 1.1 fusion.2.refs_0_
  2.7 3.1 %collective-permute-start.3 = (bf16[1,96,640]{2,1,0:T(8,128)(2,1)S(1)}, bf16[1,96,640]{2,1,0:T(8,128)(2,1)S(1)}, u32[]{:S(2)}, u32[]{:S(2)}) collective-permute-start(bf16[1,96,640]{2,1,0:T(8,128)(2,1)S(1)} %dynamic-slice_bitcast_fusion.2), channel_id=1, source_target_pairs={{0,4},{1,17},{2,6},{3,19},{4,0},{5,21},{6,2},{7,23},{8,12},{9,25},... | collective-permute-start | bytes 368648 | tf_op jit(solution)/shard_map/ppermute | solution.py:507
  5.8 1.3 pad_add_fusion.where
  7.1 3.2 %pack.1 = (bf16[128,768]{1,0:T(8,128)(2,1)}, bf16[128,768]{1,0:T(8,128)(2,1)}, bf16[2,128,768]{2,1,0:T(8,128)(2,1)}, bf16[128,768]{1,0:T(8,128)(2,1)}, bf16[128,...) custom-call(s32[18]{0:T(128)} %pad_add_fusion.where, f32[4,128,768]{2,1,0:T(8,128)} %old_ref.2, f32[4,128,768]{2,1,0:T(8,128)} %old_ref.3), custom_call_target="tpu_custom_call" | custom-call | flops 3000000000 | bytes 10500000 | tf_op jit(solution)/shard_map/pack/pallas_call | solution.py:569
  10.3 1.5 collective-permute-start.1
  13.2 2.7 collective-permute-start.4
  16.4 3.7 %prepare.1 = (f32[12,128,384]{2,1,0:T(8,128)}, bf16[512,128]{1,0:T(8,128)(2,1)}, bf16[512,128]{1,0:T(8,128)(2,1)}, bf16[768,768]{1,0:T(8,128)(2,1)}) custom-call(s32[18]{0:T(128)} %pad_add_fusion.where, s32[4,8]{1,0:T(4,128)} %lengths.1, f32[32,12]{1,0:T(8,128)} %copy.24.table.table_ref, s32[1,768]{1,0:T(1,128)} %fusion.3.position_ref), custom_call_target="tpu_custom_call" | custom-call | flops 6000000000 | bytes 21000000 | tf_op jit(solution)/shard_map/prepare/pallas_call | solution.py:578
  20.0 4.8 %collective-permute-done.5.refs_7_ = bf16[1,96,640]{2,1,0:T(8,128)(2,1)} collective-permute-done((bf16[1,96,640]{2,1,0:T(8,128)(2,1)S(1)}, bf16[1,96,640]{2,1,0:T(8,128)(2,1)}, u32[]{:S(2)}, u32[]{:S(2)}) %collective-permute-start.5) | collective-permute-done | bytes 122912 | tf_op jit(solution)/shard_map/ppermute | solution.py:507
  24.9 1.7 collective-permute-start.8
  26.6 1.5 collective-permute-start.9
  30.1 5.0 %collective-permute-done.9.refs_8_ = bf16[2,96,640]{2,1,0:T(8,128)(2,1)} collective-permute-done((bf16[2,96,640]{2,1,0:T(8,128)(2,1)S(1)}, bf16[2,96,640]{2,1,0:T(8,128)(2,1)}, u32[]{:S(2)}, u32[]{:S(2)}) %collective-permute-start.9) | collective-permute-done | bytes 245792 | tf_op jit(solution)/shard_map/ppermute | solution.py:507
  35.1 1.5 collective-permute-start.13
  37.0 5.3 %collective-permute-done.6.refs_1_ = bf16[1,120,768]{2,1,0:T(8,128)(2,1)S(1)} collective-permute-done((bf16[1,120,768]{2,1,0:T(8,128)(2,1)S(1)}, bf16[1,120,768]{2,1,0:T(8,128)(2,1)S(1)}, u32[]{:S(2)}, u32[]{:S(2)}) %collective-permute-start.6) | collective-permute-done | bytes 184352 | tf_op jit(solution)/shard_map/ppermute | solution.py:507
  43.3 4.7 %collective-permute-done.13.refs_9_ = bf16[4,96,640]{2,1,0:T(8,128)(2,1)} collective-permute-done((bf16[4,96,640]{2,1,0:T(8,128)(2,1)S(1)}, bf16[4,96,640]{2,1,0:T(8,128)(2,1)}, u32[]{:S(2)}, u32[]{:S(2)}) %collective-permute-start.13) | collective-permute-done | bytes 491552 | tf_op jit(solution)/shard_map/ppermute | solution.py:507
  48.7 1.7 collective-permute-done.mate_ref
  50.5 4.2 %collective-permute-done.7.refs_2_ = bf16[2,120,768]{2,1,0:T(8,128)(2,1)} collective-permute-done((bf16[2,120,768]{2,1,0:T(8,128)(2,1)S(1)}, bf16[2,120,768]{2,1,0:T(8,128)(2,1)}, u32[]{:S(2)}, u32[]{:S(2)}) %collective-permute-start.7) | collective-permute-done | bytes 368672 | tf_op jit(solution)/shard_map/ppermute | solution.py:507
  57.0 1.5 collective-permute-start.20
  58.5 9.1 %qkv.1 = (bf16[512,2304]{1,0:T(8,128)(2,1)}, bf16[768,512]{1,0:T(8,128)(2,1)}, bf16[4,128,768]{2,1,0:T(8,128)(2,1)}, f32[2,768]{1,0:T(2,128)}, bf16[4,8,96,640]{3,2,1,0:T(8,128)(2,1)}) custom-call(s32[18]{0:T(128)} %pad_add_fusion.where, bf16[128,768]{1,0:T(8,128)(2,1)} %get-tuple-element.114.keep_ref, bf16[128,768]{1,0:T(8,128)(2,1)} %copy-done.43, ...), custom_call_target="tpu_custom_call" | custom-call | flops 8999999488 | bytes 31500000 | tf_op jit(solution)/shard_map/qkv/pallas_call | solution.py:622
  67.6 3.4 %collective-permute-done.17.refs_3_ = bf16[4,120,768]{2,1,0:T(8,128)(2,1)S(1)} collective-permute-done((bf16[4,120,768]{2,1,0:T(8,128)(2,1)S(1)}, bf16[4,120,768]{2,1,0:T(8,128)(2,1)S(1)}, u32[]{:S(2)}, u32[]{:S(2)}) %collective-permute-start.17) | collective-permute-done | bytes 737312 | tf_op jit(solution)/shard_map/ppermute | solution.py:507
  71.7 6.0 %attention.2 = (bf16[6,512,512]{2,1,0:T(8,128)(2,1)}, bf16[512,384]{1,0:T(8,128)(2,1)}) custom-call(bf16[512,2304]{1,0:T(8,128)(2,1)} %get-tuple-element.126.q_ref.k_ref.v_ref, bf16[512,2304]{1,0:T(8,128)(2,1)} %get-tuple-element.126.q_ref.k_ref.v_ref, bf16[512,2304]{1,0:T(8,128)(2,1)} %get-tuple-element.126.q_ref.k_ref.v_ref, ...), custom_call_target="tpu_custom_call" | custom-call | flops 10000000000 | bytes 35000000 | tf_op jit(solution)/shard_map/attention/pallas_call | solution.py:651
  77.6 5.9 %attention.3 = (bf16[6,512,512]{2,1,0:T(8,128)(2,1)}, bf16[512,384]{1,0:T(8,128)(2,1)}) custom-call(bf16[512,2304]{1,0:T(8,128)(2,1)} %get-tuple-element.126.q_ref.k_ref.v_ref, bf16[512,2304]{1,0:T(8,128)(2,1)} %get-tuple-element.126.q_ref.k_ref.v_ref, bf16[512,2304]{1,0:T(8,128)(2,1)} %get-tuple-element.126.q_ref.k_ref.v_ref, ...), custom_call_target="tpu_custom_call" | custom-call | flops 10000000000 | bytes 35000000 | tf_op jit(solution)/shard_map/attention/pallas_call | solution.py:651
  83.5 5.2 %collective-permute-done.25.refs_9_ = bf16[4,120,768]{2,1,0:T(8,128)(2,1)S(1)} collective-permute-done((bf16[4,120,768]{2,1,0:T(8,128)(2,1)S(1)}, bf16[4,120,768]{2,1,0:T(8,128)(2,1)S(1)}, u32[]{:S(2)}, u32[]{:S(2)}) %collective-permute-start.25) | collective-permute-done | bytes 737312 | tf_op jit(solution)/shard_map/ppermute | solution.py:507
  89.3 2.2 collective-permute-done.22.refs_4_
  94.9 6.4 %out.1 = (f32[512,768]{1,0:T(8,128)}, bf16[512,768]{1,0:T(8,128)(2,1)}, bf16[768,512]{1,0:T(8,128)(2,1)}, bf16[768,768]{1,0:T(8,128)(2,1)}) custom-call(s32[18]{0:T(128)} %pad_add_fusion.where, bf16[512,768]{1,0:T(8,128)(2,1)} %bitcast.44, bf16[512,384]{1,0:T(8,128)(2,1)} %get-tuple-element.138.ctx_a_ref.ctx_ref, ...), custom_call_target="tpu_custom_call" | custom-call | flops 6000000000 | bytes 21000000 | tf_op jit(solution)/shard_map/out/pallas_call | solution.py:678
  101.4 2.1 collective-permute-done.30.away_ref
  105.7 15.0 %up.1 = (bf16[512,3072]{1,0:T(8,128)(2,1)}, bf16[512,3072]{1,0:T(8,128)(2,1)}, bf16[2,2,2,2,96,768]{5,4,3,2,1,0:T(8,128)(2,1)}, bf16[2,2,2,2,96,768]{5,4,3,2,1,0...) custom-call(s32[4]{0:T(128)} %pad_add_fusion.1.place, s32[18]{0:T(128)} %pad_add_fusion.where, ...), custom_call_target="tpu_custom_call" | custom-call | flops 10000000000 | bytes 35000000 | tf_op jit(solution)/shard_map/up/pallas_call | solution.py:725
  121.8 1.3 slice.294
  123.2 2.4 collective-permute-done.33
  126.3 1.5 collective-permute-done.34.refs_4_
  129.5 20.3 %down.1 = (bf16[128,768]{1,0:T(8,128)(2,1)}, bf16[128,768]{1,0:T(8,128)(2,1)}, bf16[2,128,768]{2,1,0:T(8,128)(2,1)}, f32[512,768]{1,0:T(8,128)}, bf16[384,3072]{1,0:T(8,128)(2,1)}, /*index=5*/bf16[384,3072]{1,0:T(8,128)(2,1)}) custom-call(s32[18]{0:T(128)} %pad_add_fusion.where, bf16[768,512]{1,0:T(8,128)(2,1)} %get-tuple-element.143.second_t_ref, ...), custom_call_target="tpu_custom_call" | custom-call | flops 15000000512 | bytes 52500000 | tf_op jit(solution)/shard_map/down/pallas_call | solution.py:799
  150.1 2.5 add_convert_fusion.3
  153.1 7.0 %mid.1 = (f32[512,768]{1,0:T(8,128)}, f32[1,768]{1,0:T(1,128)}, bf16[512,768]{1,0:T(8,128)(2,1)}, bf16[384,768]{1,0:T(8,128)(2,1)}, bf16[384,768]{1,0:T(8,128)(2,1)}) custom-call(bf16[512,768]{1,0:T(8,128)(2,1)} %bitcast.45, f32[512,768]{1,0:T(8,128)} %get-tuple-element.152.attn_ref, f32[2,768]{1,0:T(2,128)} %get-tuple-element.139.gains_ref, ...), custom_call_target="tpu_custom_call" | custom-call | flops 7000000000 | bytes 24500000 | tf_op jit(solution)/shard_map/mid/pallas_call | solution.py:822
  160.1 2.6 collective-permute-done.39
  162.7 2.1 add_convert_fusion.7
  164.8 1.2 add_convert_fusion.6
  166.5 1.5 pad_maximum_fusion
  168.4 8.2 %back.2 = (bf16[512,384]{1,0:T(8,128)(2,1)}, bf16[512,384]{1,0:T(8,128)(2,1)}, bf16[512,384]{1,0:T(8,128)(2,1)}, f32[3,8,384]{2,1,0:T(8,128)}) custom-call(bf16[512,2304]{1,0:T(8,128)(2,1)} %get-tuple-element.126.q_ref.k_ref.v_ref, bf16[512,2304]{1,0:T(8,128)(2,1)} %get-tuple-element.126.q_ref.k_ref.v_ref, ...), custom_call_target="tpu_custom_call" | custom-call | flops 10000000000 | bytes 35000000 | tf_op jit(solution)/shard_map/back/pallas_call | solution.py:841
  176.6 1.8 add_convert_fusion.11
  178.4 8.2 %back.3 = (bf16[512,384]{1,0:T(8,128)(2,1)}, bf16[512,384]{1,0:T(8,128)(2,1)}, bf16[512,384]{1,0:T(8,128)(2,1)}, f32[3,8,384]{2,1,0:T(8,128)}) custom-call(bf16[512,2304]{1,0:T(8,128)(2,1)} %get-tuple-element.126.q_ref.k_ref.v_ref, bf16[512,2304]{1,0:T(8,128)(2,1)} %get-tuple-element.126.q_ref.k_ref.v_ref, ...), custom_call_target="tpu_custom_call" | custom-call | flops 10000000000 | bytes 35000000 | tf_op jit(solution)/shard_map/back/pallas_call | solution.py:841
  187.6 1.3 add_convert_fusion.2
  191.4 5.6 %grad.1 = (bf16[384,2304]{1,0:T(8,128)(2,1)}, bf16[384,2304]{1,0:T(8,128)(2,1)}) custom-call(bf16[512,384]{1,0:T(8,128)(2,1)} %get-tuple-element.195.dqa_ref, bf16[512,384]{1,0:T(8,128)(2,1)} %get-tuple-element.180.dqb_ref, bf16[512,384]{1,0:T(8,128)(2,1)} %get-tuple-element.183.dka_ref, bf16[512,384]{1,0:T(8,128)(2,1)} %get-tuple-element.184.dkb_ref, ...), custom_call_target="tpu_custom_call" | custom-call | flops 5000000000 | bytes 17500000 | tf_op jit(solution)/shard_map/grad/pallas_call | solution.py:868
  197.0 5.5 %collective-permute-done.45 = bf16[96,3840]{1,0:T(8,128)(2,1)S(1)} collective-permute-done((bf16[96,3840]{1,0:T(8,128)(2,1)}, bf16[96,3840]{1,0:T(8,128)(2,1)S(1)}, u32[]{:S(2)}, u32[]{:S(2)}) %collective-permute-start.45) | collective-permute-done | bytes 737312 | tf_op jit(solution)/shard_map/ppermute | solution.py:507
  202.5 1.2 add_convert_fusion.13
  203.8 1.1 add_convert_fusion.5
  205.7 1.3 add_convert_fusion.1
  208.3 2.0 collective-permute-start.62
  211.0 7.5 %first.1 = (bf16[128,768]{1,0:T(8,128)(2,1)}, bf16[128,768]{1,0:T(8,128)(2,1)}, bf16[2,128,768]{2,1,0:T(8,128)(2,1)}, f32[24,128]{1,0:T(8,128)}) custom-call(s32[18]{0:T(128)} %pad_add_fusion.where, bf16[512,768]{1,0:T(8,128)(2,1)} %bitcast.46, f32[2,768]{1,0:T(2,128)} %get-tuple-element.139.gains_ref, bf16[512,384]{1,0:T(8,128)(2,1)} %get-tuple-element.195.dqa_ref, ...), custom_call_target="tpu_custom_call" | custom-call | flops 7000000000 | bytes 24500000 | tf_op jit(solution)/shard_map/first/pallas_call | solution.py:883
  218.4 2.4 collective-permute-done.47
  221.3 1.3 add_convert_fusion.4
  222.7 1.1 collective-permute-start.51
  223.8 1.3 add_convert_fusion.9
  225.1 1.8 collective-permute-start.49
  228.3 3.3 %collective-permute-done.53 = f32[24,128]{1,0:T(8,128)S(1)} collective-permute-done((f32[24,128]{1,0:T(8,128)S(1)}, f32[24,128]{1,0:T(8,128)S(1)}, u32[]{:S(2)}, u32[]{:S(2)}) %collective-permute-start.53) | collective-permute-done | bytes 12320 | tf_op jit(solution)/shard_map/ppermute | solution.py:507
  234.4 3.0 %out_rows.1 = f32[4,128,768]{2,1,0:T(8,128)} custom-call(s32[18]{0:T(128)} %pad_add_fusion.where, f32[4,128,768]{2,1,0:T(8,128)} %old_ref.2, bf16[128,768]{1,0:T(8,128)(2,1)} %get-tuple-element.160.keep_ref, bf16[128,768]{1,0:T(8,128)(2,1)} %copy-done.47, bf16[2,128,768]{2,1,0:T(8,128)(2,1)} %copy-done.19, bf16[128,768]{1,0:T(8,128)(2,1)} %copy-done.46), custom_call_target="tpu_custom_call" | custom-call | flops 3000000000 | bytes 10500000 | tf_op jit(solution)/shard_map/out_rows/pallas_call | solution.py:909
  237.4 1.3 add_convert_fusion.8
  238.7 1.7 collective-permute-start.58
  240.4 3.1 %collective-permute-done.61 = bf16[24,3840]{1,0:T(8,128)(2,1)S(1)} collective-permute-done((bf16[24,3840]{1,0:T(8,128)(2,1)S(1)}, bf16[24,3840]{1,0:T(8,128)(2,1)S(1)}, u32[]{:S(2)}, u32[]{:S(2)}) %collective-permute-start.61) | collective-permute-done | bytes 184352 | tf_op jit(solution)/shard_map/ppermute | solution.py:507
  243.5 1.9 convert_add_fusion.2
  246.0 3.1 %collective-permute-done.56 = f32[24,128]{1,0:T(8,128)S(1)} collective-permute-done((f32[24,128]{1,0:T(8,128)S(1)}, f32[24,128]{1,0:T(8,128)S(1)}, u32[]{:S(2)}, u32[]{:S(2)}) %collective-permute-start.56) | collective-permute-done | bytes 12320 | tf_op jit(solution)/shard_map/ppermute | solution.py:507
  250.1 2.0 convert_add_fusion.1
  253.6 3.0 %in_rows.1 = f32[4,128,768]{2,1,0:T(8,128)} custom-call(s32[18]{0:T(128)} %pad_add_fusion.where, f32[4,128,768]{2,1,0:T(8,128)} %old_ref.3, bf16[128,768]{1,0:T(8,128)(2,1)} %get-tuple-element.201.keep_ref, bf16[128,768]{1,0:T(8,128)(2,1)} %copy-done.49, bf16[2,128,768]{2,1,0:T(8,128)(2,1)} %copy-done.20, bf16[128,768]{1,0:T(8,128)(2,1)} %copy-done.48), custom_call_target="tpu_custom_call" | custom-call | flops 3000000000 | bytes 10500000 | tf_op jit(solution)/shard_map/in_rows/pallas_call | solution.py:909
  258.7 1.5 convert_add_fusion.4
  260.1 1.9 collective-permute-start.60
  263.6 2.2 collective-permute-done.60
  (245 shorter events, 40.5 us)
Async XLA Ops:
  2.7 10.5 %collective-permute-start.3 = (bf16[1,96,640]{2,1,0:T(8,128)(2,1)S(1)}, bf16[1,96,640]{2,1,0:T(8,128)(2,1)S(1)}, u32[]{:S(2)}, u32[]{:S(2)}) collective-permute-start(bf16[1,96,640]{2,1,0:T(8,128)(2,1)S(1)} %dynamic-slice_bitcast_fusion.2), channel_id=1, source_target_pairs={{0,4},{1,17},{2,6},{3,19},{4,0},{5,21},{6,2},{7,23},{8,12},{9,25},... | collective-permute-start | bytes 368648 | tf_op jit(solution)/shard_map/ppermute | solution.py:507
  10.3 14.5 %collective-permute-start.1 = (bf16[2,128,768]{2,1,0:T(8,128)(2,1)}, bf16[2,128,768]{2,1,0:T(8,128)(2,1)S(1)}, u32[]{:S(2)}, u32[]{:S(2)}) collective-permute-start(bf16[2,128,768]{2,1,0:T(8,128)(2,1)} %get-tuple-element.116), channel_id=1, source_target_pairs={{0,2},{1,3},{2,0},{3,1},{4,6},{5,7},{6,4},{7,5},{8,10},{9,11},{10,... | collective-permute-start | bytes 1179656 | tf_op jit(solution)/shard_map/ppermute | solution.py:507
  13.2 11.6 %collective-permute-start.4 = (bf16[2,96,640]{2,1,0:T(8,128)(2,1)S(1)}, bf16[2,96,640]{2,1,0:T(8,128)(2,1)S(1)}, u32[]{:S(2)}, u32[]{:S(2)}) collective-permute-start(bf16[2,96,640]{2,1,0:T(8,128)(2,1)S(1)} %pad_maximum_fusion.8), channel_id=1, source_target_pairs={{0,16},{1,9},{2,18},{3,11},{4,20},{5,13},{6,22},{7,15},{8,24},{9,1... | collective-permute-start | bytes 737288 | tf_op jit(solution)/shard_map/ppermute | solution.py:507
  15.9 8.9 %collective-permute-start.5 = (bf16[1,96,640]{2,1,0:T(8,128)(2,1)S(1)}, bf16[1,96,640]{2,1,0:T(8,128)(2,1)}, u32[]{:S(2)}, u32[]{:S(2)}) collective-permute-start(bf16[1,96,640]{2,1,0:T(8,128)(2,1)S(1)} %collective-permute-done.3.refs_1_), channel_id=1, source_target_pairs={{0,2},{1,3},{2,0},{3,1},{4,6},{5,7},{6,4},{7,5},{8,10},{9,11},{10,... | collective-permute-start | bytes 368648 | tf_op jit(solution)/shard_map/ppermute | solution.py:507
  24.9 10.2 %collective-permute-start.8 = (bf16[4,96,640]{2,1,0:T(8,128)(2,1)S(1)}, bf16[4,96,640]{2,1,0:T(8,128)(2,1)S(1)}, u32[]{:S(2)}, u32[]{:S(2)}) collective-permute-start(bf16[4,96,640]{2,1,0:T(8,128)(2,1)S(1)} %pad_maximum_fusion.5), channel_id=1, source_target_pairs={{0,8},{1,5},{2,10},{3,7},{4,12},{5,1},{6,14},{7,3},{8,0},{9,13},{1... | collective-permute-start | bytes 1474568 | tf_op jit(solution)/shard_map/ppermute | solution.py:507
  26.6 3.5 %collective-permute-start.11 = (bf16[2,96,640]{2,1,0:T(8,128)(2,1)S(1)}, bf16[2,96,640]{2,1,0:T(8,128)(2,1)S(1)}, u32[]{:S(2)}, u32[]{:S(2)}) collective-permute-start(bf16[2,96,640]{2,1,0:T(8,128)(2,1)S(1)} %collective-permute-done.4.refs_2_), channel_id=1, source_target_pairs={{0,1},{1,0},{2,3},{3,2},{4,5},{5,4},{6,7},{7,6},{8,9},{9,8},{10,11... | collective-permute-start | bytes 737288 | tf_op jit(solution)/shard_map/ppermute | solution.py:507
  26.6 8.5 %collective-permute-start.9 = (bf16[2,96,640]{2,1,0:T(8,128)(2,1)S(1)}, bf16[2,96,640]{2,1,0:T(8,128)(2,1)}, u32[]{:S(2)}, u32[]{:S(2)}) collective-permute-start(bf16[2,96,640]{2,1,0:T(8,128)(2,1)S(1)} %collective-permute-done.4.refs_2_), channel_id=1, source_target_pairs={{0,2},{1,3},{2,0},{3,1},{4,6},{5,7},{6,4},{7,5},{8,10},{9,11},{10,... | collective-permute-start | bytes 737288 | tf_op jit(solution)/shard_map/ppermute | solution.py:507
  28.2 1.9 collective-permute-start.10
  35.1 13.0 %collective-permute-start.13 = (bf16[4,96,640]{2,1,0:T(8,128)(2,1)S(1)}, bf16[4,96,640]{2,1,0:T(8,128)(2,1)}, u32[]{:S(2)}, u32[]{:S(2)}) collective-permute-start(bf16[4,96,640]{2,1,0:T(8,128)(2,1)S(1)} %collective-permute-done.8.refs_3_), channel_id=1, source_target_pairs={{0,2},{1,3},{2,0},{3,1},{4,6},{5,7},{6,4},{7,5},{8,10},{9,11},{10,... | collective-permute-start | bytes 1474568 | tf_op jit(solution)/shard_map/ppermute | solution.py:507
  36.7 5.6 %collective-permute-start.6 = (bf16[1,120,768]{2,1,0:T(8,128)(2,1)S(1)}, bf16[1,120,768]{2,1,0:T(8,128)(2,1)S(1)}, u32[]{:S(2)}, u32[]{:S(2)}) collective-permute-start(bf16[1,120,768]{2,1,0:T(8,128)(2,1)S(1)} %pad_maximum_fusion.9), channel_id=1, source_target_pairs={{0,4},{1,17},{2,6},{3,19},{4,0},{5,21},{6,2},{7,23},{8,12},{9,25},... | collective-permute-start | bytes 552968 | tf_op jit(solution)/shard_map/ppermute | solution.py:507
  42.3 12.5 %collective-permute-start.7 = (bf16[2,120,768]{2,1,0:T(8,128)(2,1)S(1)}, bf16[2,120,768]{2,1,0:T(8,128)(2,1)}, u32[]{:S(2)}, u32[]{:S(2)}) collective-permute-start(bf16[2,120,768]{2,1,0:T(8,128)(2,1)S(1)} %pad_maximum_fusion.6), channel_id=1, source_target_pairs={{0,16},{1,9},{2,18},{3,11},{4,20},{5,13},{6,22},{7,15},{8,24},{9,1... | collective-permute-start | bytes 1105928 | tf_op jit(solution)/shard_map/ppermute | solution.py:507
  42.7 14.3 %collective-permute-start.12 = (bf16[4,96,640]{2,1,0:T(8,128)(2,1)S(1)}, bf16[4,96,640]{2,1,0:T(8,128)(2,1)}, u32[]{:S(2)}, u32[]{:S(2)}) collective-permute-start(bf16[4,96,640]{2,1,0:T(8,128)(2,1)S(1)} %collective-permute-done.8.refs_3_), channel_id=1, source_target_pairs={{0,1},{1,0},{2,3},{3,2},{4,5},{5,4},{6,7},{7,6},{8,9},{9,8},{10,11... | collective-permute-start | bytes 1474568 | tf_op jit(solution)/shard_map/ppermute | solution.py:507
  48.1 10.4 %collective-permute-start.16 = (bf16[4,96,640]{2,1,0:T(8,128)(2,1)}, bf16[4,96,640]{2,1,0:T(8,128)(2,1)}, u32[]{:S(2)}, u32[]{:S(2)}) collective-permute-start(bf16[4,96,640]{2,1,0:T(8,128)(2,1)} %collective-permute-done.13.refs_9_), channel_id=1, source_target_pairs={{0,1},{1,0},{2,3},{3,2},{4,5},{5,4},{6,7},{7,6},{8,9},{9,8},{10,11... | collective-permute-start | bytes 1474568 | tf_op jit(solution)/shard_map/ppermute | solution.py:507
  48.1 2.3 collective-permute-start
  48.6 7.3 %collective-permute-start.14 = (bf16[1,96,640]{2,1,0:T(8,128)(2,1)}, bf16[1,96,640]{2,1,0:T(8,128)(2,1)S(1)}, u32[]{:S(2)}, u32[]{:S(2)}) collective-permute-start(bf16[1,96,640]{2,1,0:T(8,128)(2,1)} %collective-permute-done.5.refs_7_), channel_id=1, source_target_pairs={{0,1},{1,0},{2,3},{3,2},{4,5},{5,4},{6,7},{7,6},{8,9},{9,8},{10,11... | collective-permute-start | bytes 368648 | tf_op jit(solution)/shard_map/ppermute | solution.py:507
  50.4 5.9 %collective-permute-start.2 = (bf16[128,768]{1,0:T(8,128)(2,1)S(1)}, bf16[128,768]{1,0:T(8,128)(2,1)S(1)}, u32[]{:S(2)}, u32[]{:S(2)}) collective-permute-start(bf16[128,768]{1,0:T(8,128)(2,1)S(1)} %slice_bitcast_fusion), channel_id=1, source_target_pairs={{0,1},{1,0},{2,3},{3,2},{4,5},{5,4},{6,7},{7,6},{8,9},{9,8},{10,11... | collective-permute-start | bytes 589832 | tf_op jit(solution)/shard_map/ppermute | solution.py:507
  54.8 1.7 collective-permute-start.15
  55.9 15.6 %collective-permute-start.18 = (bf16[1,192,768]{2,1,0:T(8,128)(2,1)S(1)}, bf16[1,192,768]{2,1,0:T(8,128)(2,1)S(1)}, u32[]{:S(2)}, u32[]{:S(2)}) collective-permute-start(bf16[1,192,768]{2,1,0:T(8,128)(2,1)S(1)} %dynamic-slice_bitcast_fusion), channel_id=1, source_target_pairs={{0,4},{1,17},{2,6},{3,19},{4,0},{5,21},{6,2},{7,23},{8,12},{9,25},... | collective-permute-start | bytes 884744 | tf_op jit(solution)/shard_map/ppermute | solution.py:507
  56.3 14.6 %collective-permute-start.17 = (bf16[4,120,768]{2,1,0:T(8,128)(2,1)S(1)}, bf16[4,120,768]{2,1,0:T(8,128)(2,1)S(1)}, u32[]{:S(2)}, u32[]{:S(2)}) collective-permute-start(bf16[4,120,768]{2,1,0:T(8,128)(2,1)S(1)} %pad_maximum_fusion.2), channel_id=1, source_target_pairs={{0,8},{1,5},{2,10},{3,7},{4,12},{5,1},{6,14},{7,3},{8,0},{9,13},{1... | collective-permute-start | bytes 2211848 | tf_op jit(solution)/shard_map/ppermute | solution.py:507
  56.5 15.2 %collective-permute-start.19 = (bf16[1,120,768]{2,1,0:T(8,128)(2,1)S(1)}, bf16[1,120,768]{2,1,0:T(8,128)(2,1)S(1)}, u32[]{:S(2)}, u32[]{:S(2)}) collective-permute-start(bf16[1,120,768]{2,1,0:T(8,128)(2,1)S(1)} %collective-permute-done.6.refs_1_), channel_id=1, source_target_pairs={{0,2},{1,3},{2,0},{3,1},{4,6},{5,7},{6,4},{7,5},{8,10},{9,11},{10,... | collective-permute-start | bytes 552968 | tf_op jit(solution)/shard_map/ppermute | solution.py:507
  57.0 14.7 %collective-permute-start.20 = (bf16[2,120,768]{2,1,0:T(8,128)(2,1)}, bf16[2,120,768]{2,1,0:T(8,128)(2,1)S(1)}, u32[]{:S(2)}, u32[]{:S(2)}) collective-permute-start(bf16[2,120,768]{2,1,0:T(8,128)(2,1)} %collective-permute-done.7.refs_2_), channel_id=1, source_target_pairs={{0,2},{1,3},{2,0},{3,1},{4,6},{5,7},{6,4},{7,5},{8,10},{9,11},{10,... | collective-permute-start | bytes 1105928 | tf_op jit(solution)/shard_map/ppermute | solution.py:507
  71.0 17.8 %collective-permute-start.25 = (bf16[4,120,768]{2,1,0:T(8,128)(2,1)S(1)}, bf16[4,120,768]{2,1,0:T(8,128)(2,1)S(1)}, u32[]{:S(2)}, u32[]{:S(2)}) collective-permute-start(bf16[4,120,768]{2,1,0:T(8,128)(2,1)S(1)} %collective-permute-done.17.refs_3_), channel_id=1, source_target_pairs={{0,2},{1,3},{2,0},{3,1},{4,6},{5,7},{6,4},{7,5},{8,10},{9,11},{10,... | collective-permute-start | bytes 2211848 | tf_op jit(solution)/shard_map/ppermute | solution.py:507
  71.5 22.3 %collective-permute-start.24 = (bf16[4,120,768]{2,1,0:T(8,128)(2,1)S(1)}, bf16[4,120,768]{2,1,0:T(8,128)(2,1)S(1)}, u32[]{:S(2)}, u32[]{:S(2)}) collective-permute-start(bf16[4,120,768]{2,1,0:T(8,128)(2,1)S(1)} %collective-permute-done.17.refs_3_), channel_id=1, source_target_pairs={{0,1},{1,0},{2,3},{3,2},{4,5},{5,4},{6,7},{7,6},{8,9},{9,8},{10,11... | collective-permute-start | bytes 2211848 | tf_op jit(solution)/shard_map/ppermute | solution.py:507
  71.5 50.0 %copy-start.4 = (bf16[1,192,768]{2,1,0:T(8,128)(2,1)}, bf16[1,192,768]{2,1,0:T(8,128)(2,1)S(1)}, u32[]{:S(2)}) copy-start(bf16[1,192,768]{2,1,0:T(8,128)(2,1)S(1)} %collective-permute-done.18.refs_1_) | copy-start | bytes 884740
  71.6 20.1 %collective-permute-start.21 = (bf16[2,192,768]{2,1,0:T(8,128)(2,1)S(1)}, bf16[2,192,768]{2,1,0:T(8,128)(2,1)S(1)}, u32[]{:S(2)}, u32[]{:S(2)}) collective-permute-start(bf16[2,192,768]{2,1,0:T(8,128)(2,1)S(1)} %pad_maximum_fusion.4), channel_id=1, source_target_pairs={{0,16},{1,9},{2,18},{3,11},{4,20},{5,13},{6,22},{7,15},{8,24},{9,1... | collective-permute-start | bytes 1769480 | tf_op jit(solution)/shard_map/ppermute | solution.py:507
  88.8 5.0 %collective-permute-start.28 = (bf16[4,120,768]{2,1,0:T(8,128)(2,1)S(1)}, bf16[4,120,768]{2,1,0:T(8,128)(2,1)S(1)}, u32[]{:S(2)}, u32[]{:S(2)}) collective-permute-start(bf16[4,120,768]{2,1,0:T(8,128)(2,1)S(1)} %collective-permute-done.25.refs_9_), channel_id=1, source_target_pairs={{0,1},{1,0},{2,3},{3,2},{4,5},{5,4},{6,7},{7,6},{8,9},{9,8},{10,11... | collective-permute-start | bytes 2211848 | tf_op jit(solution)/shard_map/ppermute | solution.py:507
  88.8 2.7 %collective-permute-start.22 = (bf16[1,120,768]{2,1,0:T(8,128)(2,1)S(1)}, bf16[1,120,768]{2,1,0:T(8,128)(2,1)S(1)}, u32[]{:S(2)}, u32[]{:S(2)}) collective-permute-start(bf16[1,120,768]{2,1,0:T(8,128)(2,1)S(1)} %collective-permute-done.6.refs_1_), channel_id=1, source_target_pairs={{0,1},{1,0},{2,3},{3,2},{4,5},{5,4},{6,7},{7,6},{8,9},{9,8},{10,11... | collective-permute-start | bytes 552968 | tf_op jit(solution)/shard_map/ppermute | solution.py:507
  89.3 2.9 %collective-permute-start.23 = (bf16[2,120,768]{2,1,0:T(8,128)(2,1)}, bf16[2,120,768]{2,1,0:T(8,128)(2,1)S(1)}, u32[]{:S(2)}, u32[]{:S(2)}) collective-permute-start(bf16[2,120,768]{2,1,0:T(8,128)(2,1)} %collective-permute-done.7.refs_2_), channel_id=1, source_target_pairs={{0,1},{1,0},{2,3},{3,2},{4,5},{5,4},{6,7},{7,6},{8,9},{9,8},{10,11... | collective-permute-start | bytes 1105928 | tf_op jit(solution)/shard_map/ppermute | solution.py:507
  91.5 2.2 collective-permute-start.27
  91.6 1.9 collective-permute-start.26
  92.2 11.2 %collective-permute-start.30 = (bf16[2,128,768]{2,1,0:T(8,128)(2,1)S(1)}, bf16[2,128,768]{2,1,0:T(8,128)(2,1)S(1)}, u32[]{:S(2)}, u32[]{:S(2)}) collective-permute-start(bf16[2,128,768]{2,1,0:T(8,128)(2,1)S(1)} %copy-done.30), channel_id=1, source_target_pairs={{0,2},{1,3},{2,0},{3,1},{4,6},{5,7},{6,4},{7,5},{8,10},{9,11},{10,... | collective-permute-start | bytes 1179656 | tf_op jit(solution)/shard_map/ppermute | solution.py:507
  93.6 10.6 %collective-permute-start.29 = (bf16[128,768]{1,0:T(8,128)(2,1)S(1)}, bf16[128,768]{1,0:T(8,128)(2,1)S(1)}, u32[]{:S(2)}, u32[]{:S(2)}) collective-permute-start(bf16[128,768]{1,0:T(8,128)(2,1)S(1)} %copy-done.38), channel_id=1, source_target_pairs={{0,1},{1,0},{2,3},{3,2},{4,5},{5,4},{6,7},{7,6},{8,9},{9,8},{10,11... | collective-permute-start | bytes 589832 | tf_op jit(solution)/shard_map/ppermute | solution.py:507
  93.7 27.0 %collective-permute-start.32 = (bf16[4,192,768]{2,1,0:T(8,128)(2,1)S(1)}, bf16[4,192,768]{2,1,0:T(8,128)(2,1)}, u32[]{:S(2)}, u32[]{:S(2)}) collective-permute-start(bf16[4,192,768]{2,1,0:T(8,128)(2,1)S(1)} %pad_maximum_fusion.1), channel_id=1, source_target_pairs={{0,8},{1,5},{2,10},{3,7},{4,12},{5,1},{6,14},{7,3},{8,0},{9,13},{1... | collective-permute-start | bytes 3538952 | tf_op jit(solution)/shard_map/ppermute | solution.py:507
  103.5 1.5 collective-permute-start.31
  120.7 4.8 %collective-permute-start.33 = (bf16[1536,768]{1,0:T(8,128)(2,1)}, bf16[1536,768]{1,0:T(8,128)(2,1)S(1)}, u32[]{:S(2)}, u32[]{:S(2)}) collective-permute-start(bf16[1536,768]{1,0:T(8,128)(2,1)} %bitcast.41), channel_id=1, source_target_pairs={{0,1},{1,0},{2,3},{3,2},{4,5},{5,4},{6,7},{7,6},{8,9},{9,8},{10,11... | collective-permute-start | bytes 7077896 | tf_op jit(solution)/shard_map/ppermute | solution.py:507
  120.9 7.6 %collective-permute-start.36 = (bf16[4,192,768]{2,1,0:T(8,128)(2,1)}, bf16[4,192,768]{2,1,0:T(8,128)(2,1)S(1)}, u32[]{:S(2)}, u32[]{:S(2)}) collective-permute-start(bf16[4,192,768]{2,1,0:T(8,128)(2,1)} %collective-permute-done.32.refs_3_), channel_id=1, source_target_pairs={{0,1},{1,0},{2,3},{3,2},{4,5},{5,4},{6,7},{7,6},{8,9},{9,8},{10,11... | collective-permute-start | bytes 3538952 | tf_op jit(solution)/shard_map/ppermute | solution.py:507
  121.3 6.6 %collective-permute-start.35 = (bf16[2,192,768]{2,1,0:T(8,128)(2,1)S(1)}, bf16[2,192,768]{2,1,0:T(8,128)(2,1)S(1)}, u32[]{:S(2)}, u32[]{:S(2)}) collective-permute-start(bf16[2,192,768]{2,1,0:T(8,128)(2,1)S(1)} %collective-permute-done.21.refs_2_), channel_id=1, source_target_pairs={{0,1},{1,0},{2,3},{3,2},{4,5},{5,4},{6,7},{7,6},{8,9},{9,8},{10,11... | collective-permute-start | bytes 1769480 | tf_op jit(solution)/shard_map/ppermute | solution.py:507
  121.5 6.4 %collective-permute-start.34 = (bf16[1,192,768]{2,1,0:T(8,128)(2,1)S(1)}, bf16[1,192,768]{2,1,0:T(8,128)(2,1)S(1)}, u32[]{:S(2)}, u32[]{:S(2)}) collective-permute-start(bf16[1,192,768]{2,1,0:T(8,128)(2,1)S(1)} %collective-permute-done.18.refs_1_), channel_id=1, source_target_pairs={{0,1},{1,0},{2,3},{3,2},{4,5},{5,4},{6,7},{7,6},{8,9},{9,8},{10,11... | collective-permute-start | bytes 884744 | tf_op jit(solution)/shard_map/ppermute | solution.py:507
  125.9 24.2 %collective-permute-start.38 = (bf16[768,768]{1,0:T(8,128)(2,1)S(1)}, bf16[768,768]{1,0:T(8,128)(2,1)S(1)}, u32[]{:S(2)}, u32[]{:S(2)}) collective-permute-start(bf16[768,768]{1,0:T(8,128)(2,1)S(1)} %fusion), channel_id=1, source_target_pairs={{0,4},{1,3},{2,6},{3,1},{4,0},{5,7},{6,2},{7,5},{8,12},{9,11},{10,... | collective-permute-start | bytes 3538952 | tf_op jit(solution)/shard_map/ppermute | solution.py:507
  149.9 16.2 %collective-permute-start.40 = (bf16[384,3072]{1,0:T(8,128)(2,1)}, bf16[384,3072]{1,0:T(8,128)(2,1)S(1)}, u32[]{:S(2)}, u32[]{:S(2)}) collective-permute-start(bf16[384,3072]{1,0:T(8,128)(2,1)} %get-tuple-element.170), channel_id=1, source_target_pairs={{0,1},{1,0},{2,3},{3,2},{4,5},{5,4},{6,7},{7,6},{8,9},{9,8},{10,11... | collective-permute-start | bytes 7077896 | tf_op jit(solution)/shard_map/ppermute | solution.py:507
  152.6 10.1 %collective-permute-start.39 = (bf16[384,768]{1,0:T(8,128)(2,1)}, bf16[384,768]{1,0:T(8,128)(2,1)S(1)}, u32[]{:S(2)}, u32[]{:S(2)}) collective-permute-start(bf16[384,768]{1,0:T(8,128)(2,1)} %add_convert_fusion.3), channel_id=1, source_target_pairs={{0,2},{1,5},{2,0},{3,7},{4,6},{5,1},{6,4},{7,3},{8,10},{9,13},{10,... | collective-permute-start | bytes 1769480 | tf_op jit(solution)/shard_map/ppermute | solution.py:507
  160.1 4.7 %collective-permute-start.41 = (bf16[384,768]{1,0:T(8,128)(2,1)}, bf16[384,768]{1,0:T(8,128)(2,1)S(1)}, u32[]{:S(2)}, u32[]{:S(2)}) collective-permute-start(bf16[384,768]{1,0:T(8,128)(2,1)} %get-tuple-element.173), channel_id=1, source_target_pairs={{0,1},{1,0},{2,3},{3,2},{4,5},{5,4},{6,7},{7,6},{8,9},{9,8},{10,11... | collective-permute-start | bytes 1769480 | tf_op jit(solution)/shard_map/ppermute | solution.py:507
  164.8 11.8 %collective-permute-start.43 = (bf16[192,768]{1,0:T(8,128)(2,1)}, bf16[192,768]{1,0:T(8,128)(2,1)}, u32[]{:S(2)}, u32[]{:S(2)}) collective-permute-start(bf16[192,768]{1,0:T(8,128)(2,1)} %add_convert_fusion.7), channel_id=1, source_target_pairs={{0,8},{1,9},{2,10},{3,11},{4,12},{5,13},{6,14},{7,15},{8,0},{9,1},... | collective-permute-start | bytes 884744 | tf_op jit(solution)/shard_map/ppermute | solution.py:507
  167.9 19.7 %collective-permute-start.42 = (bf16[192,3840]{1,0:T(8,128)(2,1)}, bf16[192,3840]{1,0:T(8,128)(2,1)}, u32[]{:S(2)}, u32[]{:S(2)}) collective-permute-start(bf16[192,3840]{1,0:T(8,128)(2,1)} %pad_maximum_fusion), channel_id=1, source_target_pairs={{0,4},{1,3},{2,6},{3,1},{4,0},{5,7},{6,2},{7,5},{8,12},{9,11},{10,... | collective-permute-start | bytes 4423688 | tf_op jit(solution)/shard_map/ppermute | solution.py:507
  190.9 11.7 %collective-permute-start.45 = (bf16[96,3840]{1,0:T(8,128)(2,1)}, bf16[96,3840]{1,0:T(8,128)(2,1)S(1)}, u32[]{:S(2)}, u32[]{:S(2)}) collective-permute-start(bf16[96,3840]{1,0:T(8,128)(2,1)} %pad_maximum_fusion.3), channel_id=1, source_target_pairs={{0,2},{1,5},{2,0},{3,7},{4,6},{5,1},{6,4},{7,3},{8,10},{9,13},{10,... | collective-permute-start | bytes 2211848 | tf_op jit(solution)/shard_map/ppermute | solution.py:507
  197.0 8.7 %collective-permute-start.44 = (bf16[384,2304]{1,0:T(8,128)(2,1)}, bf16[384,2304]{1,0:T(8,128)(2,1)S(1)}, u32[]{:S(2)}, u32[]{:S(2)}) collective-permute-start(bf16[384,2304]{1,0:T(8,128)(2,1)} %get-tuple-element.189), channel_id=1, source_target_pairs={{0,1},{1,0},{2,3},{3,2},{4,5},{5,4},{6,7},{7,6},{8,9},{9,8},{10,11... | collective-permute-start | bytes 5308424 | tf_op jit(solution)/shard_map/ppermute | solution.py:507
  207.2 13.6 %collective-permute-start.46 = (bf16[192,2304]{1,0:T(8,128)(2,1)}, bf16[192,2304]{1,0:T(8,128)(2,1)S(1)}, u32[]{:S(2)}, u32[]{:S(2)}) collective-permute-start(bf16[192,2304]{1,0:T(8,128)(2,1)} %add_convert_fusion.1), channel_id=1, source_target_pairs={{0,4},{1,3},{2,6},{3,1},{4,0},{5,7},{6,2},{7,5},{8,12},{9,11},{10,... | collective-permute-start | bytes 2654216 | tf_op jit(solution)/shard_map/ppermute | solution.py:507
  207.7 16.1 %collective-permute-start.37 = (bf16[2,128,768]{2,1,0:T(8,128)(2,1)}, bf16[2,128,768]{2,1,0:T(8,128)(2,1)S(1)}, u32[]{:S(2)}, u32[]{:S(2)}) collective-permute-start(bf16[2,128,768]{2,1,0:T(8,128)(2,1)} %get-tuple-element.162), channel_id=1, source_target_pairs={{0,2},{1,3},{2,0},{3,1},{4,6},{5,7},{6,4},{7,5},{8,10},{9,11},{10,... | collective-permute-start | bytes 1179656 | tf_op jit(solution)/shard_map/ppermute | solution.py:507
  208.3 37.1 %collective-permute-start.62 = (bf16[96,768]{1,0:T(8,128)(2,1)}, bf16[96,768]{1,0:T(8,128)(2,1)S(1)}, u32[]{:S(2)}, u32[]{:S(2)}) collective-permute-start(bf16[96,768]{1,0:T(8,128)(2,1)} %add_convert_fusion.11), channel_id=1, source_target_pairs={{0,16},{1,17},{2,18},{3,19},{4,20},{5,21},{6,22},{7,23},{8,24},{9,... | collective-permute-start | bytes 442376 | tf_op jit(solution)/shard_map/ppermute | solution.py:507
  210.3 10.5 %collective-permute-start.47 = (bf16[48,3840]{1,0:T(8,128)(2,1)}, bf16[48,3840]{1,0:T(8,128)(2,1)S(1)}, u32[]{:S(2)}, u32[]{:S(2)}) collective-permute-start(bf16[48,3840]{1,0:T(8,128)(2,1)} %pad_maximum_fusion.7), channel_id=1, source_target_pairs={{0,8},{1,9},{2,10},{3,11},{4,12},{5,13},{6,14},{7,15},{8,0},{9,1},... | collective-permute-start | bytes 1105928 | tf_op jit(solution)/shard_map/ppermute | solution.py:507
  220.8 7.0 %collective-permute-start.52 = (f32[24,128]{1,0:T(8,128)}, f32[24,128]{1,0:T(8,128)S(1)}, u32[]{:S(2)}, u32[]{:S(2)}) collective-permute-start(f32[24,128]{1,0:T(8,128)} %get-tuple-element.206), channel_id=1, source_target_pairs={{0,1},{1,0},{2,3},{3,2},{4,5},{5,4},{6,7},{7,6},{8,9},{9,8},{10,11... | collective-permute-start | bytes 36872 | tf_op jit(solution)/shard_map/ppermute | solution.py:507
  222.7 14.7 %collective-permute-start.51 = (bf16[96,2304]{1,0:T(8,128)(2,1)S(1)}, bf16[96,2304]{1,0:T(8,128)(2,1)S(1)}, u32[]{:S(2)}, u32[]{:S(2)}) collective-permute-start(bf16[96,2304]{1,0:T(8,128)(2,1)S(1)} %add_convert_fusion.4), channel_id=1, source_target_pairs={{0,2},{1,5},{2,0},{3,7},{4,6},{5,1},{6,4},{7,3},{8,10},{9,13},{10,... | collective-permute-start | bytes 1327112 | tf_op jit(solution)/shard_map/ppermute | solution.py:507
  225.1 7.6 %collective-permute-start.49 = (bf16[128,768]{1,0:T(8,128)(2,1)S(1)}, bf16[128,768]{1,0:T(8,128)(2,1)S(1)}, u32[]{:S(2)}, u32[]{:S(2)}) collective-permute-start(bf16[128,768]{1,0:T(8,128)(2,1)S(1)} %slice_bitcast_fusion.2), channel_id=1, source_target_pairs={{0,1},{1,0},{2,3},{3,2},{4,5},{5,4},{6,7},{7,6},{8,9},{9,8},{10,11... | collective-permute-start | bytes 589832 | tf_op jit(solution)/shard_map/ppermute | solution.py:507
  226.9 6.8 %collective-permute-start.48 = (bf16[128,768]{1,0:T(8,128)(2,1)S(1)}, bf16[128,768]{1,0:T(8,128)(2,1)S(1)}, u32[]{:S(2)}, u32[]{:S(2)}) collective-permute-start(bf16[128,768]{1,0:T(8,128)(2,1)S(1)} %copy-done.39), channel_id=1, source_target_pairs={{0,1},{1,0},{2,3},{3,2},{4,5},{5,4},{6,7},{7,6},{8,9},{9,8},{10,11... | collective-permute-start | bytes 589832 | tf_op jit(solution)/shard_map/ppermute | solution.py:507
  227.9 3.8 %collective-permute-start.53 = (f32[24,128]{1,0:T(8,128)S(1)}, f32[24,128]{1,0:T(8,128)S(1)}, u32[]{:S(2)}, u32[]{:S(2)}) collective-permute-start(f32[24,128]{1,0:T(8,128)S(1)} %add.424), channel_id=1, source_target_pairs={{0,4},{1,5},{2,6},{3,7},{4,0},{5,1},{6,2},{7,3},{8,12},{9,13},{10,... | collective-permute-start | bytes 36872 | tf_op jit(solution)/shard_map/ppermute | solution.py:507
  231.7 13.7 %collective-permute-start.50 = (bf16[2,128,768]{2,1,0:T(8,128)(2,1)S(1)}, bf16[2,128,768]{2,1,0:T(8,128)(2,1)S(1)}, u32[]{:S(2)}, u32[]{:S(2)}) collective-permute-start(bf16[2,128,768]{2,1,0:T(8,128)(2,1)S(1)} %copy-done.31), channel_id=1, source_target_pairs={{0,2},{1,3},{2,0},{3,1},{4,6},{5,7},{6,4},{7,5},{8,10},{9,11},{10,... | collective-permute-start | bytes 1179656 | tf_op jit(solution)/shard_map/ppermute | solution.py:507
  232.7 10.8 %collective-permute-start.61 = (bf16[24,3840]{1,0:T(8,128)(2,1)S(1)}, bf16[24,3840]{1,0:T(8,128)(2,1)S(1)}, u32[]{:S(2)}, u32[]{:S(2)}) collective-permute-start(bf16[24,3840]{1,0:T(8,128)(2,1)S(1)} %pad_maximum_fusion.10), channel_id=1, source_target_pairs={{0,16},{1,17},{2,18},{3,19},{4,20},{5,21},{6,22},{7,23},{8,24},{9,... | collective-permute-start | bytes 552968 | tf_op jit(solution)/shard_map/ppermute | solution.py:507
  238.7 17.8 %collective-permute-start.58 = (bf16[48,2304]{1,0:T(8,128)(2,1)S(1)}, bf16[48,2304]{1,0:T(8,128)(2,1)S(1)}, u32[]{:S(2)}, u32[]{:S(2)}) collective-permute-start(bf16[48,2304]{1,0:T(8,128)(2,1)S(1)} %add_convert_fusion.8), channel_id=1, source_target_pairs={{0,8},{1,9},{2,10},{3,11},{4,12},{5,13},{6,14},{7,15},{8,0},{9,1},... | collective-permute-start | bytes 663560 | tf_op jit(solution)/shard_map/ppermute | solution.py:507
  245.4 3.7 %collective-permute-start.56 = (f32[24,128]{1,0:T(8,128)S(1)}, f32[24,128]{1,0:T(8,128)S(1)}, u32[]{:S(2)}, u32[]{:S(2)}) collective-permute-start(f32[24,128]{1,0:T(8,128)S(1)} %add.425), channel_id=1, source_target_pairs={{0,8},{1,9},{2,10},{3,11},{4,12},{5,13},{6,14},{7,15},{8,0},{9,1},... | collective-permute-start | bytes 36872 | tf_op jit(solution)/shard_map/ppermute | solution.py:507
  245.4 7.4 %collective-permute-start.55 = (bf16[128,768]{1,0:T(8,128)(2,1)S(1)}, bf16[128,768]{1,0:T(8,128)(2,1)S(1)}, u32[]{:S(2)}, u32[]{:S(2)}) collective-permute-start(bf16[128,768]{1,0:T(8,128)(2,1)S(1)} %slice_bitcast_fusion.1), channel_id=1, source_target_pairs={{0,1},{1,0},{2,3},{3,2},{4,5},{5,4},{6,7},{7,6},{8,9},{9,8},{10,11... | collective-permute-start | bytes 589832 | tf_op jit(solution)/shard_map/ppermute | solution.py:507
  245.5 7.3 %collective-permute-start.54 = (bf16[128,768]{1,0:T(8,128)(2,1)S(1)}, bf16[128,768]{1,0:T(8,128)(2,1)S(1)}, u32[]{:S(2)}, u32[]{:S(2)}) collective-permute-start(bf16[128,768]{1,0:T(8,128)(2,1)S(1)} %copy-done.41), channel_id=1, source_target_pairs={{0,1},{1,0},{2,3},{3,2},{4,5},{5,4},{6,7},{7,6},{8,9},{9,8},{10,11... | collective-permute-start | bytes 589832 | tf_op jit(solution)/shard_map/ppermute | solution.py:507
  249.1 3.7 %collective-permute-start.57 = (f32[24,128]{1,0:T(8,128)S(1)}, f32[24,128]{1,0:T(8,128)S(1)}, u32[]{:S(2)}, u32[]{:S(2)}) collective-permute-start(f32[24,128]{1,0:T(8,128)S(1)} %add.427), channel_id=1, source_target_pairs={{0,2},{1,3},{2,0},{3,1},{4,6},{5,7},{6,4},{7,5},{8,10},{9,11},{10,... | collective-permute-start | bytes 36872 | tf_op jit(solution)/shard_map/ppermute | solution.py:507
  257.6 4.7 %collective-permute-start.59 = (f32[24,128]{1,0:T(8,128)S(1)}, f32[24,128]{1,0:T(8,128)S(1)}, u32[]{:S(2)}, u32[]{:S(2)}) collective-permute-start(f32[24,128]{1,0:T(8,128)S(1)} %add.428), channel_id=1, source_target_pairs={{0,16},{1,17},{2,18},{3,19},{4,20},{5,21},{6,22},{7,23},{8,24},{9,... | collective-permute-start | bytes 36872 | tf_op jit(solution)/shard_map/ppermute | solution.py:507
  260.1 5.6 %collective-permute-start.60 = (bf16[24,2304]{1,0:T(8,128)(2,1)S(1)}, bf16[24,2304]{1,0:T(8,128)(2,1)S(1)}, u32[]{:S(2)}, u32[]{:S(2)}) collective-permute-start(bf16[24,2304]{1,0:T(8,128)(2,1)S(1)} %add_convert_fusion.12), channel_id=1, source_target_pairs={{0,16},{1,17},{2,18},{3,19},{4,20},{5,21},{6,22},{7,23},{8,24},{9,... | collective-permute-start | bytes 331784 | tf_op jit(solution)/shard_map/ppermute | solution.py:507
  (53 other events, 554.5 us)

commit v2 on v1

--- a/solution.py
+++ b/solution.py
@@ -96,19 +96,6 @@
                 out[t, part] = ref[i, :rows, :]
             else:
                 out[part, t] = ref[i, :rows, :]
-
-
-def fill_rows(where, pattern, refs, out, first):
-    b, s = where[0], where[1]
-    shard = refs[0].shape[0]
-    shards = out.shape[0] // shard
-    quarter = shard // 4
-    out[pl.ds(pl.multiple_of(b * shard, 8), shard), :] = refs[0][...].astype(F32)
-    for ref, (flip, base) in zip(refs[1:], pattern):
-        for i in range(ref.shape[0]):
-            t = b ^ where[2 + (s ^ flip) % 2 * shards + base + i]
-            low = pl.multiple_of(t * shard + (s ^ flip) * quarter, 8)
-            out[pl.ds(low, quarter), :] = ref[i, first : first + quarter, :].astype(F32)
 
 
 def flat(ref):
@@ -235,16 +222,16 @@
 
 
 def out_kernel(pattern, where, x_ref, ctx_a_ref, ctx_b_ref, gains_ref, perm_ref, *refs):
+    width = x_ref.shape[1]
     count = len(pattern) + 1 if pattern else 1
     attn_ref, second_ref, second_t_ref = refs[count : count + 3]
     if pattern:
-        w_ref, hold_ref = refs[count + 3 : count + 5]
-        fill_rows(where, pattern, refs[:count], hold_ref, refs[1].shape[1] - refs[0].shape[0] // 4)
-        w_ref[...] = hold_ref[...].astype(BF16)
+        w_ref = refs[count + 3]
+        fill(where, pattern, refs[:count], w_ref, False)
     else:
         w_ref = refs[0]
     ctx = jnp.concatenate([ctx_a_ref[...], ctx_b_ref[...]], axis=1)
-    attn = nn(ctx, w_ref[...])
+    attn = times_columns(ctx, w_ref, 0, width)
     attn_ref[...] = attn
     middle = x_ref[...].astype(F32) + attn
     r2 = lax.rsqrt(jnp.mean(middle * middle, axis=-1, keepdims=True) + EPS)
@@ -353,7 +340,7 @@
     gmd = r2 * (scaled - normed * jnp.mean(scaled * normed, axis=-1, keepdims=True))
     gmd_ref[...] = gmd
     low = (glow_ref[...].astype(F32) + gmd).astype(BF16)
-    dctx_ref[...] = nt(low, w_ref[...]).astype(BF16)
+    dctx_ref[...] = times_transposed(low, w_ref, 0, low.shape[1]).astype(BF16)
     ctx_t = nt(perm_ref[...], jnp.concatenate([ctx_a_ref[...], ctx_b_ref[...]], axis=1)).astype(BF16)
     dw = nn(ctx_t, low).astype(BF16)
     half = dw.shape[0] // 2
@@ -571,7 +558,7 @@
         name="pack",
         out_shape=row_shapes * 2,
         in_specs=[smem, vmem, vmem],
-        cost_estimate=cost(3),
+        cost_estimate=cost(0.9),
         compiler_params=params(),
     )(where, hidden_in, out_grad)
     row_got = other_y(row_away)
@@ -583,7 +570,7 @@
             shape((width, width), BF16),
         ),
         in_specs=[smem, smem, smem, vmem],
-        cost_estimate=cost(6),
+        cost_estimate=cost(1.8),
         compiler_params=params(),
     )(where, doc_lengths, bias_table, position)
     def tagged(arrays, flip):
@@ -599,11 +586,13 @@
     one.start()
     y_one.append(other_y(one.brought[-2]))
     core_one = [core(array) for array in one.brought[:-1]]
-    two = Gather(jnp.concatenate([piece(after(w_in, one.block), 4), piece(w_out, 4, 0)], axis=1))
+    two = Gather(piece(after(w_in, one.block), 4))
+    four = Gather(piece(after(w_out, one.block), 2))
+    four.start()
     two.start()
     one.brought[-1] = after(one.brought[-1], *y_one, *core_one)
     core_one.append(core(one.brought[-1]))
-    y_one.append(after(other_y(one.brought[-1]), two.brought[0]))
+    y_one.append(after(other_y(one.brought[-1]), two.brought[0], four.brought[0]))
     row_mate, row_far = core(row_mate), core(row_got[1])
     while len(two.brought) < stages - 1:
         two.grow()
@@ -611,6 +600,9 @@
     two.grow()
     y_two = [other_y(after(array, y_one[-1])) for array in two.brought]
     two.start()
+    while len(four.brought) < stages:
+        four.grow()
+        four.start()
     three = Gather(piece(after(w_down, two.block), 2, 0))
     three.start()
     gather1 = tagged(one.brought, 0) + tagged(core_one, 1) + tagged(y_one, 2) + tagged([core(array) for array in y_one], 3)
@@ -627,9 +619,9 @@
             *([w1_shape] if tiled else []),
         ),
         in_specs=[smem] + [vmem] * (5 + len(pieces1)),
-        cost_estimate=cost(9),
+        cost_estimate=cost(2.7),
         compiler_params=params(),
-    )(where, row_keep, row_mate, row_got, row_far, perm, after(pieces1[0], two.block, three.block), *pieces1[1:])
+    )(where, row_keep, row_mate, row_got, row_far, perm, after(pieces1[0], two.block, three.block, *four.brought), *pieces1[1:])
     qkv, first_t, xb, gains = outputs[:4]
     w1 = outputs[4] if tiled else pieces1[0]
     xb = xb.reshape(length, width)
@@ -659,37 +651,36 @@
             ],
             out_specs=(head_block(0, length, length), pair_block(0)),
             scratch_shapes=[pltpu.VMEM((2, length, length), F32)],
-            cost_estimate=cost(10),
+            cost_estimate=cost(3),
             compiler_params=params(),
         )(qkv, qkv, qkv, gated, bias_table, seg_queries, seg_keys)
 
     probs_a, ctx_a = attend(0, after(band, two.brought[-1], three.block, *y_two[:-1]))
     probs_b, ctx_b = attend(1, after(band, ctx_a))
     three.start()
-    three.grow(ctx_b)
+    gather4 = tagged(four.brought, 0) + tagged([core(array) for array in four.brought], 1)
+    wo_shape = (2, nb, shard, width // 2)
+    wo_pieces = [w_out] + [entry[0] for entry in gather4] if tiled else [plain(w_out, gather4)]
+    outputs = pl.pallas_call(
+        functools.partial(out_kernel, [entry[1:] for entry in gather4] if tiled else None),
+        name="out",
+        out_shape=(
+            shape((length, width), F32), shape((length, width), BF16), shape((width, length), BF16),
+            *([shape(wo_shape, BF16)] if tiled else []),
+        ),
+        in_specs=[smem] + [vmem] * (5 + len(wo_pieces)),
+        cost_estimate=cost(1.8),
+        compiler_params=params(),
+    )(where, xb, ctx_a, ctx_b, gains, perm, *wo_pieces)
+    attn, second, second_t = outputs[:3]
+    wo = outputs[3] if tiled else wo_pieces[0]
+    three.grow(second)
+    high3 = three.start()
+    y_two[-1] = after(y_two[-1], second)
     y_two_core = [core(after(array, ctx_b)) for array in y_two]
     gather2 = tagged(two.brought, 0) + tagged([core(array) for array in two.brought], 1) + tagged(y_two, 2) + tagged(y_two_core, 3)
     pattern2 = [entry[1:] for entry in gather2]
     arrays2 = [entry[0] for entry in gather2]
-    if tiled:
-        wo_pieces = [w_out] + arrays2
-    else:
-        wo_pieces = [plain(w_out, gather2, 0, shard).reshape(width, width)]
-    outputs = pl.pallas_call(
-        functools.partial(out_kernel, pattern2 if tiled else None),
-        name="out",
-        out_shape=(
-            shape((length, width), F32), shape((length, width), BF16), shape((width, length), BF16),
-            *([shape((width, width), BF16)] if tiled else []),
-        ),
-        in_specs=[smem] + [vmem] * (5 + len(wo_pieces)),
-        scratch_shapes=[pltpu.VMEM((width, width), F32)] if tiled else [],
-        cost_estimate=cost(6),
-        compiler_params=params(),
-    )(where, xb, after(ctx_a, three.block), ctx_b, gains, perm, *wo_pieces)
-    attn, second, second_t = outputs[:3]
-    wo = outputs[3] if tiled else wo_pieces[0]
-    high3 = three.start()
     grad_got = after(grad_got, second)
     grad_mate, grad_far = core(after(grad_mate, ctx_b)), core(grad_got[1])
     gather3 = tagged(three.brought, 0) + tagged([core(array) for array in three.brought], 1)
@@ -739,7 +730,7 @@
         ),
         cost_estimate=cost(10),
         compiler_params=params(),
-    )(place, where, second, grad_keep, grad_mate, grad_got, grad_far, *pieces2)
+    )(place, where, after(second, three.block), grad_keep, grad_mate, grad_got, grad_far, *pieces2)
     act, slope, wd_keep, wd_send = outputs[:4]
     win = outputs[4] if tiled else pieces2[0]
     glow = outputs[-1].reshape(length, width)

time: 269 us -> 265 us (0.985)
  waiting for transfers between devices: 69.2 us -> 51 us
  starting transfers between devices: 39.1 us -> 56.7 us
    ppermute x63 -> x69, waiting for transfers between devices: 69.2 us -> 51 us  [move(): return lax.ppermute(value, ('batch', 'seq'), pairs)]
    ppermute x63 -> x69, starting transfers between devices: 39.1 us -> 56.7 us  [move(): return lax.ppermute(value, ('batch', 'seq'), pairs)]
  transfers between devices with their start and end apart: 63 -> 69, of which waited for: 26 -> 21; matrix products, arithmetic and copies ran while one was open for 12% -> 12% of each run, Pallas kernels for 42% -> 42%
where the time goes in v2:
time: 265 us; the launch traced here: 264 us
  Pallas kernels  110 us (42%)
  starting transfers between devices  56.7 us (21%)
  waiting for transfers between devices  51 us (19%)
  other arithmetic  34.6 us (13%)
  local copies, waits for them, and re-layouts  9.58 us (4%)
    ppermute x69, starting transfers between devices, move(): return lax.ppermute(value, ('batch', 'seq'), pairs)  56.7 us
    ppermute x69, waiting for transfers between devices, move(): return lax.ppermute(value, ('batch', 'seq'), pairs)  51 us
    pallas_call x1, Pallas kernels, on_device(): pl.pallas_call(functools.partial(down_kernel, [entry[1:] for entry in gat...  20.3 us
    convert_element_type x16, other arithmetic, outgoing(): total(*[value[rows] for value in group]).astype(BF16)  20.2 us
    pallas_call x2, Pallas kernels, back(): pl.pallas_call(back_kernel, name='back', grid=(pairs,), out_shape=(*(shap...  16.3 us
    pallas_call x1, Pallas kernels, on_device(): pl.pallas_call(functools.partial(up_kernel, pattern2 if tiled else None),...  14.8 us
    pallas_call x2, Pallas kernels, attend(): pl.pallas_call(functools.partial(attention_kernel, i * pairs), name='atte...  11.7 us
    pallas_call x1, Pallas kernels, on_device(): pl.pallas_call(functools.partial(qkv_kernel, [entry[1:] for entry in gath...  9.06 us
  transfers between devices with their start and end apart: 69, of which 21 were waited for; matrix products, arithmetic and copies ran while one was open for 12% of the time, Pallas kernels for 42%

profile of v2, /device:TPU:0, one launch (start us, length us, event | category | flops | bytes accessed | tf_op | source)
XLA Modules:
  0.0 263.7 jit_solution(12254120072955515340)
XLA Ops:
  2.7 3.1 %collective-permute-start.3 = (bf16[1,96,640]{2,1,0:T(8,128)(2,1)S(1)}, bf16[1,96,640]{2,1,0:T(8,128)(2,1)S(1)}, u32[]{:S(2)}, u32[]{:S(2)}) collective-permute-start(bf16[1,96,640]{2,1,0:T(8,128)(2,1)S(1)} %dynamic-slice_bitcast_fusion.2), channel_id=1, source_target_pairs={{0,4},{1,17},{2,6},{3,19},{4,0},{5,21},{6,2},{7,23},{8,12},{9,25},... | collective-permute-start | bytes 368648 | tf_op jit(solution)/shard_map/ppermute | solution.py:494
  5.8 1.3 pad_add_fusion.where
  7.1 3.2 %pack.1 = (bf16[128,768]{1,0:T(8,128)(2,1)}, bf16[128,768]{1,0:T(8,128)(2,1)}, bf16[2,128,768]{2,1,0:T(8,128)(2,1)}, bf16[128,768]{1,0:T(8,128)(2,1)}, bf16[128,...) custom-call(s32[18]{0:T(128)} %pad_add_fusion.where, f32[4,128,768]{2,1,0:T(8,128)} %old_ref.2, f32[4,128,768]{2,1,0:T(8,128)} %old_ref.3), custom_call_target="tpu_custom_call" | custom-call | flops 900000000 | bytes 3150000 | tf_op jit(solution)/shard_map/pack/pallas_call | solution.py:556
  10.3 1.5 collective-permute-start.1
  12.6 2.7 %collective-permute-start.4 = (bf16[2,96,640]{2,1,0:T(8,128)(2,1)S(1)}, bf16[2,96,640]{2,1,0:T(8,128)(2,1)S(1)}, u32[]{:S(2)}, u32[]{:S(2)}) collective-permute-start(bf16[2,96,640]{2,1,0:T(8,128)(2,1)S(1)} %pad_maximum_fusion.9), channel_id=1, source_target_pairs={{0,16},{1,9},{2,18},{3,11},{4,20},{5,13},{6,22},{7,15},{8,24},{9,1... | collective-permute-start | bytes 737288 | tf_op jit(solution)/shard_map/ppermute | solution.py:494
  16.4 3.7 %prepare.1 = (f32[12,128,384]{2,1,0:T(8,128)}, bf16[512,128]{1,0:T(8,128)(2,1)}, bf16[512,128]{1,0:T(8,128)(2,1)}, bf16[768,768]{1,0:T(8,128)(2,1)}) custom-call(s32[18]{0:T(128)} %pad_add_fusion.where, s32[4,8]{1,0:T(4,128)} %lengths.1, f32[32,12]{1,0:T(8,128)} %copy.24.table.table_ref, s32[1,768]{1,0:T(1,128)} %fusion.3.position_ref), custom_call_target="tpu_custom_call" | custom-call | flops 1800000000 | bytes 6300000 | tf_op jit(solution)/shard_map/prepare/pallas_call | solution.py:565
  20.1 4.8 %collective-permute-done.5.refs_7_ = bf16[1,96,640]{2,1,0:T(8,128)(2,1)} collective-permute-done((bf16[1,96,640]{2,1,0:T(8,128)(2,1)S(1)}, bf16[1,96,640]{2,1,0:T(8,128)(2,1)}, u32[]{:S(2)}, u32[]{:S(2)}) %collective-permute-start.5) | collective-permute-done | bytes 122912 | tf_op jit(solution)/shard_map/ppermute | solution.py:494
  24.9 1.7 collective-permute-start.11
  26.7 1.5 collective-permute-start.12
  29.7 1.8 collective-permute-start.6
  31.5 3.5 %collective-permute-done.12.refs_8_ = bf16[2,96,640]{2,1,0:T(8,128)(2,1)S(1)} collective-permute-done((bf16[2,96,640]{2,1,0:T(8,128)(2,1)S(1)}, bf16[2,96,640]{2,1,0:T(8,128)(2,1)S(1)}, u32[]{:S(2)}, u32[]{:S(2)}) %collective-permute-start.12) | collective-permute-done | bytes 245792 | tf_op jit(solution)/shard_map/ppermute | solution.py:494
  35.4 2.4 collective-permute-start.16
  38.8 2.6 collective-permute-start.7
  41.5 6.8 %collective-permute-done.16.refs_9_ = bf16[4,96,640]{2,1,0:T(8,128)(2,1)} collective-permute-done((bf16[4,96,640]{2,1,0:T(8,128)(2,1)}, bf16[4,96,640]{2,1,0:T(8,128)(2,1)}, u32[]{:S(2)}, u32[]{:S(2)}) %collective-permute-start.16) | collective-permute-done | bytes 491552 | tf_op jit(solution)/shard_map/ppermute | solution.py:494
  49.0 3.4 %collective-permute-done.7.refs_2_ = bf16[2,96,768]{2,1,0:T(8,128)(2,1)S(1)} collective-permute-done((bf16[2,96,768]{2,1,0:T(8,128)(2,1)S(1)}, bf16[2,96,768]{2,1,0:T(8,128)(2,1)S(1)}, u32[]{:S(2)}, u32[]{:S(2)}) %collective-permute-start.7) | collective-permute-done | bytes 294944 | tf_op jit(solution)/shard_map/ppermute | solution.py:494
  52.6 2.1 collective-permute-start.20
  55.4 3.9 %collective-permute-done.10.refs_3_ = bf16[4,96,384]{2,1,0:T(8,128)(2,1)} collective-permute-done((bf16[4,96,384]{2,1,0:T(8,128)(2,1)S(1)}, bf16[4,96,384]{2,1,0:T(8,128)(2,1)}, u32[]{:S(2)}, u32[]{:S(2)}) %collective-permute-start.10) | collective-permute-done | bytes 294944 | tf_op jit(solution)/shard_map/ppermute | solution.py:494
  59.7 1.9 collective-permute-start.23
  61.6 9.1 %qkv.1 = (bf16[512,2304]{1,0:T(8,128)(2,1)}, bf16[768,512]{1,0:T(8,128)(2,1)}, bf16[4,128,768]{2,1,0:T(8,128)(2,1)}, f32[2,768]{1,0:T(2,128)}, bf16[4,8,96,640]{3,2,1,0:T(8,128)(2,1)}) custom-call(s32[18]{0:T(128)} %pad_add_fusion.where, bf16[128,768]{1,0:T(8,128)(2,1)} %get-tuple-element.116.keep_ref, bf16[128,768]{1,0:T(8,128)(2,1)} %copy-done.42, ...), custom_call_target="tpu_custom_call" | custom-call | flops 2700000000 | bytes 9450000 | tf_op jit(solution)/shard_map/qkv/pallas_call | solution.py:614
  71.4 1.3 collective-permute-start.27
  72.8 5.8 %attention.2 = (bf16[6,512,512]{2,1,0:T(8,128)(2,1)}, bf16[512,384]{1,0:T(8,128)(2,1)}) custom-call(bf16[512,2304]{1,0:T(8,128)(2,1)} %get-tuple-element.129.q_ref.k_ref.v_ref, bf16[512,2304]{1,0:T(8,128)(2,1)} %get-tuple-element.129.q_ref.k_ref.v_ref, bf16[512,2304]{1,0:T(8,128)(2,1)} %get-tuple-element.129.q_ref.k_ref.v_ref, ...), custom_call_target="tpu_custom_call" | custom-call | flops 3000000000 | bytes 10500000 | tf_op jit(solution)/shard_map/attention/pallas_call | solution.py:643
  78.7 2.0 collective-permute-start.29
  80.7 5.8 %attention.3 = (bf16[6,512,512]{2,1,0:T(8,128)(2,1)}, bf16[512,384]{1,0:T(8,128)(2,1)}) custom-call(bf16[512,2304]{1,0:T(8,128)(2,1)} %get-tuple-element.129.q_ref.k_ref.v_ref, bf16[512,2304]{1,0:T(8,128)(2,1)} %get-tuple-element.129.q_ref.k_ref.v_ref, bf16[512,2304]{1,0:T(8,128)(2,1)} %get-tuple-element.129.q_ref.k_ref.v_ref, ...), custom_call_target="tpu_custom_call" | custom-call | flops 3000000000 | bytes 10500000 | tf_op jit(solution)/shard_map/attention/pallas_call | solution.py:643
  87.4 5.3 %out.1 = (f32[512,768]{1,0:T(8,128)}, bf16[512,768]{1,0:T(8,128)(2,1)}, bf16[768,512]{1,0:T(8,128)(2,1)}, bf16[2,8,96,384]{3,2,1,0:T(8,128)(2,1)}) custom-call(s32[18]{0:T(128)} %pad_add_fusion.where, bf16[512,768]{1,0:T(8,128)(2,1)} %bitcast.44, bf16[512,384]{1,0:T(8,128)(2,1)} %get-tuple-element.137.ctx_a_ref.ctx_ref, ...), custom_call_target="tpu_custom_call" | custom-call | flops 1800000000 | bytes 6300000 | tf_op jit(solution)/shard_map/out/pallas_call | solution.py:664
  93.2 2.5 collective-permute-done.29.away_ref
  97.7 1.4 collective-permute-start.38
  101.3 14.8 %up.1 = (bf16[512,3072]{1,0:T(8,128)(2,1)}, bf16[512,3072]{1,0:T(8,128)(2,1)}, bf16[2,2,2,2,96,768]{5,4,3,2,1,0:T(8,128)(2,1)}, bf16[2,2,2,2,96,768]{5,4,3,2,1,0...) custom-call(s32[4]{0:T(128)} %pad_add_fusion.1.place, s32[18]{0:T(128)} %pad_add_fusion.where, ...), custom_call_target="tpu_custom_call" | custom-call | flops 10000000000 | bytes 35000000 | tf_op jit(solution)/shard_map/up/pallas_call | solution.py:716
  117.3 1.3 slice.294
  118.6 2.4 collective-permute-done.39
  121.3 2.0 collective-permute-start.44
  125.0 20.3 %down.1 = (bf16[128,768]{1,0:T(8,128)(2,1)}, bf16[128,768]{1,0:T(8,128)(2,1)}, bf16[2,128,768]{2,1,0:T(8,128)(2,1)}, f32[512,768]{1,0:T(8,128)}, bf16[384,3072]{1,0:T(8,128)(2,1)}, /*index=5*/bf16[384,3072]{1,0:T(8,128)(2,1)}) custom-call(s32[18]{0:T(128)} %pad_add_fusion.where, bf16[768,512]{1,0:T(8,128)(2,1)} %get-tuple-element.141.second_t_ref, ...), custom_call_target="tpu_custom_call" | custom-call | flops 15000000512 | bytes 52500000 | tf_op jit(solution)/shard_map/down/pallas_call | solution.py:790
  145.7 2.5 add_convert_fusion.3
  148.6 7.1 %mid.1 = (f32[512,768]{1,0:T(8,128)}, f32[1,768]{1,0:T(1,128)}, bf16[512,768]{1,0:T(8,128)(2,1)}, bf16[384,768]{1,0:T(8,128)(2,1)}, bf16[384,768]{1,0:T(8,128)(2,1)}) custom-call(bf16[512,768]{1,0:T(8,128)(2,1)} %bitcast.45, f32[512,768]{1,0:T(8,128)} %get-tuple-element.156.attn_ref, f32[2,768]{1,0:T(2,128)} %get-tuple-element.140.gains_ref, ...), custom_call_target="tpu_custom_call" | custom-call | flops 7000000000 | bytes 24500000 | tf_op jit(solution)/shard_map/mid/pallas_call | solution.py:813
  155.7 1.4 collective-permute-start.47
  158.3 2.1 add_convert_fusion.7
  160.4 1.5 collective-permute-start.49
  163.6 1.5 pad_maximum_fusion
  166.1 8.2 %back.2 = (bf16[512,384]{1,0:T(8,128)(2,1)}, bf16[512,384]{1,0:T(8,128)(2,1)}, bf16[512,384]{1,0:T(8,128)(2,1)}, f32[3,8,384]{2,1,0:T(8,128)}) custom-call(bf16[512,2304]{1,0:T(8,128)(2,1)} %get-tuple-element.129.q_ref.k_ref.v_ref, bf16[512,2304]{1,0:T(8,128)(2,1)} %get-tuple-element.129.q_ref.k_ref.v_ref, ...), custom_call_target="tpu_custom_call" | custom-call | flops 10000000000 | bytes 35000000 | tf_op jit(solution)/shard_map/back/pallas_call | solution.py:832
  174.3 1.8 add_convert_fusion.11
  176.1 8.1 %back.3 = (bf16[512,384]{1,0:T(8,128)(2,1)}, bf16[512,384]{1,0:T(8,128)(2,1)}, bf16[512,384]{1,0:T(8,128)(2,1)}, f32[3,8,384]{2,1,0:T(8,128)}) custom-call(bf16[512,2304]{1,0:T(8,128)(2,1)} %get-tuple-element.129.q_ref.k_ref.v_ref, bf16[512,2304]{1,0:T(8,128)(2,1)} %get-tuple-element.129.q_ref.k_ref.v_ref, ...), custom_call_target="tpu_custom_call" | custom-call | flops 10000000000 | bytes 35000000 | tf_op jit(solution)/shard_map/back/pallas_call | solution.py:832
  184.7 1.3 add_convert_fusion.2
  188.2 5.5 %grad.1 = (bf16[384,2304]{1,0:T(8,128)(2,1)}, bf16[384,2304]{1,0:T(8,128)(2,1)}) custom-call(bf16[512,384]{1,0:T(8,128)(2,1)} %get-tuple-element.199.dqa_ref, bf16[512,384]{1,0:T(8,128)(2,1)} %get-tuple-element.184.dqb_ref, bf16[512,384]{1,0:T(8,128)(2,1)} %get-tuple-element.187.dka_ref, bf16[512,384]{1,0:T(8,128)(2,1)} %get-tuple-element.188.dkb_ref, ...), custom_call_target="tpu_custom_call" | custom-call | flops 5000000000 | bytes 17500000 | tf_op jit(solution)/shard_map/grad/pallas_call | solution.py:859
  193.7 5.9 %collective-permute-done.51 = bf16[96,3840]{1,0:T(8,128)(2,1)S(1)} collective-permute-done((bf16[96,3840]{1,0:T(8,128)(2,1)}, bf16[96,3840]{1,0:T(8,128)(2,1)S(1)}, u32[]{:S(2)}, u32[]{:S(2)}) %collective-permute-start.51) | collective-permute-done | bytes 737312 | tf_op jit(solution)/shard_map/ppermute | solution.py:494
  199.6 1.2 add_convert_fusion.13
  202.8 1.3 add_convert_fusion.1
  206.7 1.2 collective-permute-start.53
  207.9 7.5 %first.1 = (bf16[128,768]{1,0:T(8,128)(2,1)}, bf16[128,768]{1,0:T(8,128)(2,1)}, bf16[2,128,768]{2,1,0:T(8,128)(2,1)}, f32[24,128]{1,0:T(8,128)}) custom-call(s32[18]{0:T(128)} %pad_add_fusion.where, bf16[512,768]{1,0:T(8,128)(2,1)} %bitcast.46, f32[2,768]{1,0:T(2,128)} %get-tuple-element.140.gains_ref, bf16[512,384]{1,0:T(8,128)(2,1)} %get-tuple-element.199.dqa_ref, ...), custom_call_target="tpu_custom_call" | custom-call | flops 7000000000 | bytes 24500000 | tf_op jit(solution)/shard_map/first/pallas_call | solution.py:874
  215.4 2.7 %collective-permute-done.53 = bf16[48,3840]{1,0:T(8,128)(2,1)S(1)} collective-permute-done((bf16[48,3840]{1,0:T(8,128)(2,1)}, bf16[48,3840]{1,0:T(8,128)(2,1)S(1)}, u32[]{:S(2)}, u32[]{:S(2)}) %collective-permute-start.53) | collective-permute-done | bytes 368672 | tf_op jit(solution)/shard_map/ppermute | solution.py:494
  218.2 1.3 add_convert_fusion.4
  220.7 1.3 add_convert_fusion.9
  222.0 1.5 collective-permute-start.55
  224.4 1.4 collective-permute-start.59
  225.8 2.4 collective-permute-done.59
  229.3 1.9 collective-permute-start.67
  231.9 3.0 %out_rows.1 = f32[4,128,768]{2,1,0:T(8,128)} custom-call(s32[18]{0:T(128)} %pad_add_fusion.where, f32[4,128,768]{2,1,0:T(8,128)} %old_ref.2, bf16[128,768]{1,0:T(8,128)(2,1)} %get-tuple-element.164.keep_ref, bf16[128,768]{1,0:T(8,128)(2,1)} %copy-done.47, bf16[2,128,768]{2,1,0:T(8,128)(2,1)} %copy-done.22, bf16[128,768]{1,0:T(8,128)(2,1)} %copy-done.46), custom_call_target="tpu_custom_call" | custom-call | flops 3000000000 | bytes 10500000 | tf_op jit(solution)/shard_map/out_rows/pallas_call | solution.py:900
  234.8 1.3 add_convert_fusion.8
  237.0 3.1 %collective-permute-done.67 = bf16[24,3840]{1,0:T(8,128)(2,1)S(1)} collective-permute-done((bf16[24,3840]{1,0:T(8,128)(2,1)S(1)}, bf16[24,3840]{1,0:T(8,128)(2,1)S(1)}, u32[]{:S(2)}, u32[]{:S(2)}) %collective-permute-start.67) | collective-permute-done | bytes 184352 | tf_op jit(solution)/shard_map/ppermute | solution.py:494
  240.1 1.9 convert_add_fusion.2
  242.6 3.1 %collective-permute-done.62 = f32[24,128]{1,0:T(8,128)S(1)} collective-permute-done((f32[24,128]{1,0:T(8,128)S(1)}, f32[24,128]{1,0:T(8,128)S(1)}, u32[]{:S(2)}, u32[]{:S(2)}) %collective-permute-start.62) | collective-permute-done | bytes 12320 | tf_op jit(solution)/shard_map/ppermute | solution.py:494
  246.7 2.0 convert_add_fusion.1
  250.2 3.0 %in_rows.1 = f32[4,128,768]{2,1,0:T(8,128)} custom-call(s32[18]{0:T(128)} %pad_add_fusion.where, f32[4,128,768]{2,1,0:T(8,128)} %old_ref.3, bf16[128,768]{1,0:T(8,128)(2,1)} %get-tuple-element.205.keep_ref, bf16[128,768]{1,0:T(8,128)(2,1)} %copy-done.49, bf16[2,128,768]{2,1,0:T(8,128)(2,1)} %copy-done.23, bf16[128,768]{1,0:T(8,128)(2,1)} %copy-done.48), custom_call_target="tpu_custom_call" | custom-call | flops 3000000000 | bytes 10500000 | tf_op jit(solution)/shard_map/in_rows/pallas_call | solution.py:900
  254.8 1.5 convert_add_fusion.4
  256.2 2.4 collective-permute-start.66
  260.1 1.8 collective-permute-done.66
  (264 shorter events, 42.7 us)
Async XLA Ops:
  2.7 9.8 %collective-permute-start.3 = (bf16[1,96,640]{2,1,0:T(8,128)(2,1)S(1)}, bf16[1,96,640]{2,1,0:T(8,128)(2,1)S(1)}, u32[]{:S(2)}, u32[]{:S(2)}) collective-permute-start(bf16[1,96,640]{2,1,0:T(8,128)(2,1)S(1)} %dynamic-slice_bitcast_fusion.2), channel_id=1, source_target_pairs={{0,4},{1,17},{2,6},{3,19},{4,0},{5,21},{6,2},{7,23},{8,12},{9,25},... | collective-permute-start | bytes 368648 | tf_op jit(solution)/shard_map/ppermute | solution.py:494
  10.3 14.5 %collective-permute-start.1 = (bf16[2,128,768]{2,1,0:T(8,128)(2,1)}, bf16[2,128,768]{2,1,0:T(8,128)(2,1)S(1)}, u32[]{:S(2)}, u32[]{:S(2)}) collective-permute-start(bf16[2,128,768]{2,1,0:T(8,128)(2,1)} %get-tuple-element.118), channel_id=1, source_target_pairs={{0,2},{1,3},{2,0},{3,1},{4,6},{5,7},{6,4},{7,5},{8,10},{9,11},{10,... | collective-permute-start | bytes 1179656 | tf_op jit(solution)/shard_map/ppermute | solution.py:494
  12.6 12.3 %collective-permute-start.4 = (bf16[2,96,640]{2,1,0:T(8,128)(2,1)S(1)}, bf16[2,96,640]{2,1,0:T(8,128)(2,1)S(1)}, u32[]{:S(2)}, u32[]{:S(2)}) collective-permute-start(bf16[2,96,640]{2,1,0:T(8,128)(2,1)S(1)} %pad_maximum_fusion.9), channel_id=1, source_target_pairs={{0,16},{1,9},{2,18},{3,11},{4,20},{5,13},{6,22},{7,15},{8,24},{9,1... | collective-permute-start | bytes 737288 | tf_op jit(solution)/shard_map/ppermute | solution.py:494
  15.9 8.9 %collective-permute-start.5 = (bf16[1,96,640]{2,1,0:T(8,128)(2,1)S(1)}, bf16[1,96,640]{2,1,0:T(8,128)(2,1)}, u32[]{:S(2)}, u32[]{:S(2)}) collective-permute-start(bf16[1,96,640]{2,1,0:T(8,128)(2,1)S(1)} %collective-permute-done.3.refs_1_), channel_id=1, source_target_pairs={{0,2},{1,3},{2,0},{3,1},{4,6},{5,7},{6,4},{7,5},{8,10},{9,11},{10,... | collective-permute-start | bytes 368648 | tf_op jit(solution)/shard_map/ppermute | solution.py:494
  24.9 10.5 %collective-permute-start.11 = (bf16[4,96,640]{2,1,0:T(8,128)(2,1)S(1)}, bf16[4,96,640]{2,1,0:T(8,128)(2,1)}, u32[]{:S(2)}, u32[]{:S(2)}) collective-permute-start(bf16[4,96,640]{2,1,0:T(8,128)(2,1)S(1)} %pad_maximum_fusion.5), channel_id=1, source_target_pairs={{0,8},{1,5},{2,10},{3,7},{4,12},{5,1},{6,14},{7,3},{8,0},{9,13},{1... | collective-permute-start | bytes 1474568 | tf_op jit(solution)/shard_map/ppermute | solution.py:494
  26.7 4.9 %collective-permute-start.14 = (bf16[2,96,640]{2,1,0:T(8,128)(2,1)S(1)}, bf16[2,96,640]{2,1,0:T(8,128)(2,1)S(1)}, u32[]{:S(2)}, u32[]{:S(2)}) collective-permute-start(bf16[2,96,640]{2,1,0:T(8,128)(2,1)S(1)} %collective-permute-done.4.refs_2_), channel_id=1, source_target_pairs={{0,1},{1,0},{2,3},{3,2},{4,5},{5,4},{6,7},{7,6},{8,9},{9,8},{10,11... | collective-permute-start | bytes 737288 | tf_op jit(solution)/shard_map/ppermute | solution.py:494
  26.7 8.4 %collective-permute-start.12 = (bf16[2,96,640]{2,1,0:T(8,128)(2,1)S(1)}, bf16[2,96,640]{2,1,0:T(8,128)(2,1)S(1)}, u32[]{:S(2)}, u32[]{:S(2)}) collective-permute-start(bf16[2,96,640]{2,1,0:T(8,128)(2,1)S(1)} %collective-permute-done.4.refs_2_), channel_id=1, source_target_pairs={{0,2},{1,3},{2,0},{3,1},{4,6},{5,7},{6,4},{7,5},{8,10},{9,11},{10,... | collective-permute-start | bytes 737288 | tf_op jit(solution)/shard_map/ppermute | solution.py:494
  28.4 9.9 %collective-permute-start.8 = (bf16[1,96,384]{2,1,0:T(8,128)(2,1)S(1)}, bf16[1,96,384]{2,1,0:T(8,128)(2,1)S(1)}, u32[]{:S(2)}, u32[]{:S(2)}) collective-permute-start(bf16[1,96,384]{2,1,0:T(8,128)(2,1)S(1)} %dynamic-slice_bitcast_fusion.3), channel_id=1, source_target_pairs={{0,4},{1,17},{2,6},{3,19},{4,0},{5,21},{6,2},{7,23},{8,12},{9,25},... | collective-permute-start | bytes 221192 | tf_op jit(solution)/shard_map/ppermute | solution.py:494
  29.7 9.1 %collective-permute-start.6 = (bf16[1,96,768]{2,1,0:T(8,128)(2,1)S(1)}, bf16[1,96,768]{2,1,0:T(8,128)(2,1)S(1)}, u32[]{:S(2)}, u32[]{:S(2)}) collective-permute-start(bf16[1,96,768]{2,1,0:T(8,128)(2,1)S(1)} %dynamic-slice_bitcast_fusion.1), channel_id=1, source_target_pairs={{0,4},{1,17},{2,6},{3,19},{4,0},{5,21},{6,2},{7,23},{8,12},{9,25},... | collective-permute-start | bytes 442376 | tf_op jit(solution)/shard_map/ppermute | solution.py:494
  35.4 12.9 %collective-permute-start.16 = (bf16[4,96,640]{2,1,0:T(8,128)(2,1)}, bf16[4,96,640]{2,1,0:T(8,128)(2,1)}, u32[]{:S(2)}, u32[]{:S(2)}) collective-permute-start(bf16[4,96,640]{2,1,0:T(8,128)(2,1)} %collective-permute-done.11.refs_3_), channel_id=1, source_target_pairs={{0,2},{1,3},{2,0},{3,1},{4,6},{5,7},{6,4},{7,5},{8,10},{9,11},{10,... | collective-permute-start | bytes 1474568 | tf_op jit(solution)/shard_map/ppermute | solution.py:494
  37.8 11.1 %collective-permute-start = (bf16[128,768]{1,0:T(8,128)(2,1)S(1)}, bf16[128,768]{1,0:T(8,128)(2,1)S(1)}, u32[]{:S(2)}, u32[]{:S(2)}) collective-permute-start(bf16[128,768]{1,0:T(8,128)(2,1)S(1)} %copy-done.40), channel_id=1, source_target_pairs={{0,1},{1,0},{2,3},{3,2},{4,5},{5,4},{6,7},{7,6},{8,9},{9,8},{10,11... | collective-permute-start | bytes 589832 | tf_op jit(solution)/shard_map/ppermute | solution.py:494
  37.8 14.8 %collective-permute-start.17 = (bf16[1,96,640]{2,1,0:T(8,128)(2,1)}, bf16[1,96,640]{2,1,0:T(8,128)(2,1)S(1)}, u32[]{:S(2)}, u32[]{:S(2)}) collective-permute-start(bf16[1,96,640]{2,1,0:T(8,128)(2,1)} %collective-permute-done.5.refs_7_), channel_id=1, source_target_pairs={{0,1},{1,0},{2,3},{3,2},{4,5},{5,4},{6,7},{7,6},{8,9},{9,8},{10,11... | collective-permute-start | bytes 368648 | tf_op jit(solution)/shard_map/ppermute | solution.py:494
  38.4 10.0 %collective-permute-start.9 = (bf16[2,96,384]{2,1,0:T(8,128)(2,1)S(1)}, bf16[2,96,384]{2,1,0:T(8,128)(2,1)S(1)}, u32[]{:S(2)}, u32[]{:S(2)}) collective-permute-start(bf16[2,96,384]{2,1,0:T(8,128)(2,1)S(1)} %pad_maximum_fusion.11), channel_id=1, source_target_pairs={{0,16},{1,9},{2,18},{3,11},{4,20},{5,13},{6,22},{7,15},{8,24},{9,1... | collective-permute-start | bytes 442376 | tf_op jit(solution)/shard_map/ppermute | solution.py:494
  38.8 13.6 %collective-permute-start.7 = (bf16[2,96,768]{2,1,0:T(8,128)(2,1)S(1)}, bf16[2,96,768]{2,1,0:T(8,128)(2,1)S(1)}, u32[]{:S(2)}, u32[]{:S(2)}) collective-permute-start(bf16[2,96,768]{2,1,0:T(8,128)(2,1)S(1)} %pad_maximum_fusion.7), channel_id=1, source_target_pairs={{0,16},{1,9},{2,18},{3,11},{4,20},{5,13},{6,22},{7,15},{8,24},{9,1... | collective-permute-start | bytes 884744 | tf_op jit(solution)/shard_map/ppermute | solution.py:494
  48.3 11.2 %collective-permute-start.15 = (bf16[4,96,640]{2,1,0:T(8,128)(2,1)}, bf16[4,96,640]{2,1,0:T(8,128)(2,1)}, u32[]{:S(2)}, u32[]{:S(2)}) collective-permute-start(bf16[4,96,640]{2,1,0:T(8,128)(2,1)} %collective-permute-done.11.refs_3_), channel_id=1, source_target_pairs={{0,1},{1,0},{2,3},{3,2},{4,5},{5,4},{6,7},{7,6},{8,9},{9,8},{10,11... | collective-permute-start | bytes 1474568 | tf_op jit(solution)/shard_map/ppermute | solution.py:494
  48.3 11.4 %collective-permute-start.19 = (bf16[4,96,640]{2,1,0:T(8,128)(2,1)}, bf16[4,96,640]{2,1,0:T(8,128)(2,1)}, u32[]{:S(2)}, u32[]{:S(2)}) collective-permute-start(bf16[4,96,640]{2,1,0:T(8,128)(2,1)} %collective-permute-done.16.refs_9_), channel_id=1, source_target_pairs={{0,1},{1,0},{2,3},{3,2},{4,5},{5,4},{6,7},{7,6},{8,9},{9,8},{10,11... | collective-permute-start | bytes 1474568 | tf_op jit(solution)/shard_map/ppermute | solution.py:494
  48.9 5.8 %collective-permute-start.2 = (bf16[128,768]{1,0:T(8,128)(2,1)S(1)}, bf16[128,768]{1,0:T(8,128)(2,1)S(1)}, u32[]{:S(2)}, u32[]{:S(2)}) collective-permute-start(bf16[128,768]{1,0:T(8,128)(2,1)S(1)} %slice_bitcast_fusion), channel_id=1, source_target_pairs={{0,1},{1,0},{2,3},{3,2},{4,5},{5,4},{6,7},{7,6},{8,9},{9,8},{10,11... | collective-permute-start | bytes 589832 | tf_op jit(solution)/shard_map/ppermute | solution.py:494
  52.4 6.9 %collective-permute-start.10 = (bf16[4,96,384]{2,1,0:T(8,128)(2,1)S(1)}, bf16[4,96,384]{2,1,0:T(8,128)(2,1)}, u32[]{:S(2)}, u32[]{:S(2)}) collective-permute-start(bf16[4,96,384]{2,1,0:T(8,128)(2,1)S(1)} %pad_maximum_fusion.8), channel_id=1, source_target_pairs={{0,8},{1,5},{2,10},{3,7},{4,12},{5,1},{6,14},{7,3},{8,0},{9,13},{1... | collective-permute-start | bytes 884744 | tf_op jit(solution)/shard_map/ppermute | solution.py:494
  52.6 18.2 %collective-permute-start.20 = (bf16[4,96,768]{2,1,0:T(8,128)(2,1)S(1)}, bf16[4,96,768]{2,1,0:T(8,128)(2,1)}, u32[]{:S(2)}, u32[]{:S(2)}) collective-permute-start(bf16[4,96,768]{2,1,0:T(8,128)(2,1)S(1)} %pad_maximum_fusion.3), channel_id=1, source_target_pairs={{0,8},{1,5},{2,10},{3,7},{4,12},{5,1},{6,14},{7,3},{8,0},{9,13},{1... | collective-permute-start | bytes 1769480 | tf_op jit(solution)/shard_map/ppermute | solution.py:494
  55.4 4.1 %collective-permute-start.18 = (bf16[2,96,640]{2,1,0:T(8,128)(2,1)}, bf16[2,96,640]{2,1,0:T(8,128)(2,1)S(1)}, u32[]{:S(2)}, u32[]{:S(2)}) collective-permute-start(bf16[2,96,640]{2,1,0:T(8,128)(2,1)} %copy-done.36), channel_id=1, source_target_pairs={{0,1},{1,0},{2,3},{3,2},{4,5},{5,4},{6,7},{7,6},{8,9},{9,8},{10,11... | collective-permute-start | bytes 737288 | tf_op jit(solution)/shard_map/ppermute | solution.py:494
  59.3 11.4 %collective-permute-start.21 = (bf16[1,192,768]{2,1,0:T(8,128)(2,1)S(1)}, bf16[1,192,768]{2,1,0:T(8,128)(2,1)S(1)}, u32[]{:S(2)}, u32[]{:S(2)}) collective-permute-start(bf16[1,192,768]{2,1,0:T(8,128)(2,1)S(1)} %dynamic-slice_bitcast_fusion), channel_id=1, source_target_pairs={{0,4},{1,17},{2,6},{3,19},{4,0},{5,21},{6,2},{7,23},{8,12},{9,25},... | collective-permute-start | bytes 884744 | tf_op jit(solution)/shard_map/ppermute | solution.py:494
  59.5 19.2 %collective-permute-start.24 = (bf16[1,96,384]{2,1,0:T(8,128)(2,1)S(1)}, bf16[1,96,384]{2,1,0:T(8,128)(2,1)S(1)}, u32[]{:S(2)}, u32[]{:S(2)}) collective-permute-start(bf16[1,96,384]{2,1,0:T(8,128)(2,1)S(1)} %collective-permute-done.8.refs_1_), channel_id=1, source_target_pairs={{0,1},{1,0},{2,3},{3,2},{4,5},{5,4},{6,7},{7,6},{8,9},{9,8},{10,11... | collective-permute-start | bytes 221192 | tf_op jit(solution)/shard_map/ppermute | solution.py:494
  59.5 11.8 %collective-permute-start.22 = (bf16[1,96,768]{2,1,0:T(8,128)(2,1)S(1)}, bf16[1,96,768]{2,1,0:T(8,128)(2,1)S(1)}, u32[]{:S(2)}, u32[]{:S(2)}) collective-permute-start(bf16[1,96,768]{2,1,0:T(8,128)(2,1)S(1)} %collective-permute-done.6.refs_1_), channel_id=1, source_target_pairs={{0,2},{1,3},{2,0},{3,1},{4,6},{5,7},{6,4},{7,5},{8,10},{9,11},{10,... | collective-permute-start | bytes 442376 | tf_op jit(solution)/shard_map/ppermute | solution.py:494
  59.7 13.0 %collective-permute-start.23 = (bf16[2,96,768]{2,1,0:T(8,128)(2,1)S(1)}, bf16[2,96,768]{2,1,0:T(8,128)(2,1)}, u32[]{:S(2)}, u32[]{:S(2)}) collective-permute-start(bf16[2,96,768]{2,1,0:T(8,128)(2,1)S(1)} %collective-permute-done.7.refs_2_), channel_id=1, source_target_pairs={{0,2},{1,3},{2,0},{3,1},{4,6},{5,7},{6,4},{7,5},{8,10},{9,11},{10,... | collective-permute-start | bytes 884744 | tf_op jit(solution)/shard_map/ppermute | solution.py:494
  70.7 15.8 %collective-permute-start.25 = (bf16[2,96,384]{2,1,0:T(8,128)(2,1)S(1)}, bf16[2,96,384]{2,1,0:T(8,128)(2,1)S(1)}, u32[]{:S(2)}, u32[]{:S(2)}) collective-permute-start(bf16[2,96,384]{2,1,0:T(8,128)(2,1)S(1)} %collective-permute-done.9.refs_2_), channel_id=1, source_target_pairs={{0,1},{1,0},{2,3},{3,2},{4,5},{5,4},{6,7},{7,6},{8,9},{9,8},{10,11... | collective-permute-start | bytes 442376 | tf_op jit(solution)/shard_map/ppermute | solution.py:494
  70.8 15.8 %collective-permute-start.26 = (bf16[4,96,384]{2,1,0:T(8,128)(2,1)}, bf16[4,96,384]{2,1,0:T(8,128)(2,1)S(1)}, u32[]{:S(2)}, u32[]{:S(2)}) collective-permute-start(bf16[4,96,384]{2,1,0:T(8,128)(2,1)} %collective-permute-done.10.refs_3_), channel_id=1, source_target_pairs={{0,1},{1,0},{2,3},{3,2},{4,5},{5,4},{6,7},{7,6},{8,9},{9,8},{10,11... | collective-permute-start | bytes 884744 | tf_op jit(solution)/shard_map/ppermute | solution.py:494
  71.4 24.4 %collective-permute-start.27 = (bf16[2,192,768]{2,1,0:T(8,128)(2,1)S(1)}, bf16[2,192,768]{2,1,0:T(8,128)(2,1)S(1)}, u32[]{:S(2)}, u32[]{:S(2)}) collective-permute-start(bf16[2,192,768]{2,1,0:T(8,128)(2,1)S(1)} %pad_maximum_fusion.4), channel_id=1, source_target_pairs={{0,16},{1,9},{2,18},{3,11},{4,20},{5,13},{6,22},{7,15},{8,24},{9,1... | collective-permute-start | bytes 1769480 | tf_op jit(solution)/shard_map/ppermute | solution.py:494
  72.7 19.9 %collective-permute-start.34 = (bf16[4,96,768]{2,1,0:T(8,128)(2,1)}, bf16[4,96,768]{2,1,0:T(8,128)(2,1)}, u32[]{:S(2)}, u32[]{:S(2)}) collective-permute-start(bf16[4,96,768]{2,1,0:T(8,128)(2,1)} %collective-permute-done.20.refs_3_), channel_id=1, source_target_pairs={{0,2},{1,3},{2,0},{3,1},{4,6},{5,7},{6,4},{7,5},{8,10},{9,11},{10,... | collective-permute-start | bytes 1769480 | tf_op jit(solution)/shard_map/ppermute | solution.py:494
  78.7 17.1 %collective-permute-start.29 = (bf16[2,128,768]{2,1,0:T(8,128)(2,1)S(1)}, bf16[2,128,768]{2,1,0:T(8,128)(2,1)S(1)}, u32[]{:S(2)}, u32[]{:S(2)}) collective-permute-start(bf16[2,128,768]{2,1,0:T(8,128)(2,1)S(1)} %copy-done.29), channel_id=1, source_target_pairs={{0,2},{1,3},{2,0},{3,1},{4,6},{5,7},{6,4},{7,5},{8,10},{9,11},{10,... | collective-permute-start | bytes 1179656 | tf_op jit(solution)/shard_map/ppermute | solution.py:494
  86.6 10.7 %collective-permute-start.32 = (bf16[2,96,768]{2,1,0:T(8,128)(2,1)S(1)}, bf16[2,96,768]{2,1,0:T(8,128)(2,1)S(1)}, u32[]{:S(2)}, u32[]{:S(2)}) collective-permute-start(bf16[2,96,768]{2,1,0:T(8,128)(2,1)S(1)} %collective-permute-done.7.refs_2_), channel_id=1, source_target_pairs={{0,1},{1,0},{2,3},{3,2},{4,5},{5,4},{6,7},{7,6},{8,9},{9,8},{10,11... | collective-permute-start | bytes 884744 | tf_op jit(solution)/shard_map/ppermute | solution.py:494
  86.7 13.5 %collective-permute-start.33 = (bf16[4,96,768]{2,1,0:T(8,128)(2,1)}, bf16[4,96,768]{2,1,0:T(8,128)(2,1)}, u32[]{:S(2)}, u32[]{:S(2)}) collective-permute-start(bf16[4,96,768]{2,1,0:T(8,128)(2,1)} %collective-permute-done.20.refs_3_), channel_id=1, source_target_pairs={{0,1},{1,0},{2,3},{3,2},{4,5},{5,4},{6,7},{7,6},{8,9},{9,8},{10,11... | collective-permute-start | bytes 1769480 | tf_op jit(solution)/shard_map/ppermute | solution.py:494
  92.7 8.0 %collective-permute-start.37 = (bf16[4,96,768]{2,1,0:T(8,128)(2,1)}, bf16[4,96,768]{2,1,0:T(8,128)(2,1)}, u32[]{:S(2)}, u32[]{:S(2)}) collective-permute-start(bf16[4,96,768]{2,1,0:T(8,128)(2,1)} %collective-permute-done.34.refs_9_), channel_id=1, source_target_pairs={{0,1},{1,0},{2,3},{3,2},{4,5},{5,4},{6,7},{7,6},{8,9},{9,8},{10,11... | collective-permute-start | bytes 1769480 | tf_op jit(solution)/shard_map/ppermute | solution.py:494
  97.3 2.9 %collective-permute-start.36 = (bf16[2,96,768]{2,1,0:T(8,128)(2,1)}, bf16[2,96,768]{2,1,0:T(8,128)(2,1)S(1)}, u32[]{:S(2)}, u32[]{:S(2)}) collective-permute-start(bf16[2,96,768]{2,1,0:T(8,128)(2,1)} %collective-permute-done.23.refs_8_), channel_id=1, source_target_pairs={{0,1},{1,0},{2,3},{3,2},{4,5},{5,4},{6,7},{7,6},{8,9},{9,8},{10,11... | collective-permute-start | bytes 884744 | tf_op jit(solution)/shard_map/ppermute | solution.py:494
  97.7 18.5 %collective-permute-start.38 = (bf16[4,192,768]{2,1,0:T(8,128)(2,1)S(1)}, bf16[4,192,768]{2,1,0:T(8,128)(2,1)}, u32[]{:S(2)}, u32[]{:S(2)}) collective-permute-start(bf16[4,192,768]{2,1,0:T(8,128)(2,1)S(1)} %pad_maximum_fusion.1), channel_id=1, source_target_pairs={{0,8},{1,5},{2,10},{3,7},{4,12},{5,1},{6,14},{7,3},{8,0},{9,13},{1... | collective-permute-start | bytes 3538952 | tf_op jit(solution)/shard_map/ppermute | solution.py:494
  116.2 4.8 %collective-permute-start.39 = (bf16[1536,768]{1,0:T(8,128)(2,1)}, bf16[1536,768]{1,0:T(8,128)(2,1)S(1)}, u32[]{:S(2)}, u32[]{:S(2)}) collective-permute-start(bf16[1536,768]{1,0:T(8,128)(2,1)} %bitcast.41), channel_id=1, source_target_pairs={{0,1},{1,0},{2,3},{3,2},{4,5},{5,4},{6,7},{7,6},{8,9},{9,8},{10,11... | collective-permute-start | bytes 7077896 | tf_op jit(solution)/shard_map/ppermute | solution.py:494
  116.6 7.4 %collective-permute-start.42 = (bf16[4,192,768]{2,1,0:T(8,128)(2,1)}, bf16[4,192,768]{2,1,0:T(8,128)(2,1)S(1)}, u32[]{:S(2)}, u32[]{:S(2)}) collective-permute-start(bf16[4,192,768]{2,1,0:T(8,128)(2,1)} %collective-permute-done.38.refs_3_), channel_id=1, source_target_pairs={{0,1},{1,0},{2,3},{3,2},{4,5},{5,4},{6,7},{7,6},{8,9},{9,8},{10,11... | collective-permute-start | bytes 3538952 | tf_op jit(solution)/shard_map/ppermute | solution.py:494
  116.7 6.6 %collective-permute-start.41 = (bf16[2,192,768]{2,1,0:T(8,128)(2,1)S(1)}, bf16[2,192,768]{2,1,0:T(8,128)(2,1)S(1)}, u32[]{:S(2)}, u32[]{:S(2)}) collective-permute-start(bf16[2,192,768]{2,1,0:T(8,128)(2,1)S(1)} %collective-permute-done.27.refs_2_), channel_id=1, source_target_pairs={{0,1},{1,0},{2,3},{3,2},{4,5},{5,4},{6,7},{7,6},{8,9},{9,8},{10,11... | collective-permute-start | bytes 1769480 | tf_op jit(solution)/shard_map/ppermute | solution.py:494
  117.1 6.2 %collective-permute-start.40 = (bf16[1,192,768]{2,1,0:T(8,128)(2,1)S(1)}, bf16[1,192,768]{2,1,0:T(8,128)(2,1)S(1)}, u32[]{:S(2)}, u32[]{:S(2)}) collective-permute-start(bf16[1,192,768]{2,1,0:T(8,128)(2,1)S(1)} %collective-permute-done.21.refs_1_), channel_id=1, source_target_pairs={{0,1},{1,0},{2,3},{3,2},{4,5},{5,4},{6,7},{7,6},{8,9},{9,8},{10,11... | collective-permute-start | bytes 884744 | tf_op jit(solution)/shard_map/ppermute | solution.py:494
  121.3 24.4 %collective-permute-start.44 = (bf16[768,768]{1,0:T(8,128)(2,1)S(1)}, bf16[768,768]{1,0:T(8,128)(2,1)S(1)}, u32[]{:S(2)}, u32[]{:S(2)}) collective-permute-start(bf16[768,768]{1,0:T(8,128)(2,1)S(1)} %fusion), channel_id=1, source_target_pairs={{0,4},{1,3},{2,6},{3,1},{4,0},{5,7},{6,2},{7,5},{8,12},{9,11},{10,... | collective-permute-start | bytes 3538952 | tf_op jit(solution)/shard_map/ppermute | solution.py:494
  145.3 17.8 %collective-permute-start.46 = (bf16[384,3072]{1,0:T(8,128)(2,1)}, bf16[384,3072]{1,0:T(8,128)(2,1)S(1)}, u32[]{:S(2)}, u32[]{:S(2)}) collective-permute-start(bf16[384,3072]{1,0:T(8,128)(2,1)} %get-tuple-element.174), channel_id=1, source_target_pairs={{0,1},{1,0},{2,3},{3,2},{4,5},{5,4},{6,7},{7,6},{8,9},{9,8},{10,11... | collective-permute-start | bytes 7077896 | tf_op jit(solution)/shard_map/ppermute | solution.py:494
  148.2 10.1 %collective-permute-start.45 = (bf16[384,768]{1,0:T(8,128)(2,1)}, bf16[384,768]{1,0:T(8,128)(2,1)S(1)}, u32[]{:S(2)}, u32[]{:S(2)}) collective-permute-start(bf16[384,768]{1,0:T(8,128)(2,1)} %add_convert_fusion.3), channel_id=1, source_target_pairs={{0,2},{1,5},{2,0},{3,7},{4,6},{5,1},{6,4},{7,3},{8,10},{9,13},{10,... | collective-permute-start | bytes 1769480 | tf_op jit(solution)/shard_map/ppermute | solution.py:494
  155.7 6.2 %collective-permute-start.47 = (bf16[384,768]{1,0:T(8,128)(2,1)}, bf16[384,768]{1,0:T(8,128)(2,1)S(1)}, u32[]{:S(2)}, u32[]{:S(2)}) collective-permute-start(bf16[384,768]{1,0:T(8,128)(2,1)} %get-tuple-element.177), channel_id=1, source_target_pairs={{0,1},{1,0},{2,3},{3,2},{4,5},{5,4},{6,7},{7,6},{8,9},{9,8},{10,11... | collective-permute-start | bytes 1769480 | tf_op jit(solution)/shard_map/ppermute | solution.py:494
  160.4 13.8 %collective-permute-start.49 = (bf16[192,768]{1,0:T(8,128)(2,1)}, bf16[192,768]{1,0:T(8,128)(2,1)}, u32[]{:S(2)}, u32[]{:S(2)}) collective-permute-start(bf16[192,768]{1,0:T(8,128)(2,1)} %add_convert_fusion.7), channel_id=1, source_target_pairs={{0,8},{1,9},{2,10},{3,11},{4,12},{5,13},{6,14},{7,15},{8,0},{9,1},... | collective-permute-start | bytes 884744 | tf_op jit(solution)/shard_map/ppermute | solution.py:494
  165.0 19.7 %collective-permute-start.48 = (bf16[192,3840]{1,0:T(8,128)(2,1)}, bf16[192,3840]{1,0:T(8,128)(2,1)}, u32[]{:S(2)}, u32[]{:S(2)}) collective-permute-start(bf16[192,3840]{1,0:T(8,128)(2,1)} %pad_maximum_fusion), channel_id=1, source_target_pairs={{0,4},{1,3},{2,6},{3,1},{4,0},{5,7},{6,2},{7,5},{8,12},{9,11},{10,... | collective-permute-start | bytes 4423688 | tf_op jit(solution)/shard_map/ppermute | solution.py:494
  188.0 11.7 %collective-permute-start.51 = (bf16[96,3840]{1,0:T(8,128)(2,1)}, bf16[96,3840]{1,0:T(8,128)(2,1)S(1)}, u32[]{:S(2)}, u32[]{:S(2)}) collective-permute-start(bf16[96,3840]{1,0:T(8,128)(2,1)} %pad_maximum_fusion.2), channel_id=1, source_target_pairs={{0,2},{1,5},{2,0},{3,7},{4,6},{5,1},{6,4},{7,3},{8,10},{9,13},{10,... | collective-permute-start | bytes 2211848 | tf_op jit(solution)/shard_map/ppermute | solution.py:494
  193.7 9.1 %collective-permute-start.50 = (bf16[384,2304]{1,0:T(8,128)(2,1)}, bf16[384,2304]{1,0:T(8,128)(2,1)S(1)}, u32[]{:S(2)}, u32[]{:S(2)}) collective-permute-start(bf16[384,2304]{1,0:T(8,128)(2,1)} %get-tuple-element.193), channel_id=1, source_target_pairs={{0,1},{1,0},{2,3},{3,2},{4,5},{5,4},{6,7},{7,6},{8,9},{9,8},{10,11... | collective-permute-start | bytes 5308424 | tf_op jit(solution)/shard_map/ppermute | solution.py:494
  204.3 13.8 %collective-permute-start.52 = (bf16[192,2304]{1,0:T(8,128)(2,1)}, bf16[192,2304]{1,0:T(8,128)(2,1)S(1)}, u32[]{:S(2)}, u32[]{:S(2)}) collective-permute-start(bf16[192,2304]{1,0:T(8,128)(2,1)} %add_convert_fusion.1), channel_id=1, source_target_pairs={{0,4},{1,3},{2,6},{3,1},{4,0},{5,7},{6,2},{7,5},{8,12},{9,11},{10,... | collective-permute-start | bytes 2654216 | tf_op jit(solution)/shard_map/ppermute | solution.py:494
  205.3 15.3 %collective-permute-start.43 = (bf16[2,128,768]{2,1,0:T(8,128)(2,1)}, bf16[2,128,768]{2,1,0:T(8,128)(2,1)S(1)}, u32[]{:S(2)}, u32[]{:S(2)}) collective-permute-start(bf16[2,128,768]{2,1,0:T(8,128)(2,1)} %get-tuple-element.166), channel_id=1, source_target_pairs={{0,2},{1,3},{2,0},{3,1},{4,6},{5,7},{6,4},{7,5},{8,10},{9,11},{10,... | collective-permute-start | bytes 1179656 | tf_op jit(solution)/shard_map/ppermute | solution.py:494
  205.6 36.4 %collective-permute-start.68 = (bf16[96,768]{1,0:T(8,128)(2,1)}, bf16[96,768]{1,0:T(8,128)(2,1)S(1)}, u32[]{:S(2)}, u32[]{:S(2)}) collective-permute-start(bf16[96,768]{1,0:T(8,128)(2,1)} %add_convert_fusion.11), channel_id=1, source_target_pairs={{0,16},{1,17},{2,18},{3,19},{4,20},{5,21},{6,22},{7,23},{8,24},{9,... | collective-permute-start | bytes 442376 | tf_op jit(solution)/shard_map/ppermute | solution.py:494
  206.7 11.4 %collective-permute-start.53 = (bf16[48,3840]{1,0:T(8,128)(2,1)}, bf16[48,3840]{1,0:T(8,128)(2,1)S(1)}, u32[]{:S(2)}, u32[]{:S(2)}) collective-permute-start(bf16[48,3840]{1,0:T(8,128)(2,1)} %pad_maximum_fusion.6), channel_id=1, source_target_pairs={{0,8},{1,9},{2,10},{3,11},{4,12},{5,13},{6,14},{7,15},{8,0},{9,1},... | collective-permute-start | bytes 1105928 | tf_op jit(solution)/shard_map/ppermute | solution.py:494
  218.1 6.3 %collective-permute-start.58 = (f32[24,128]{1,0:T(8,128)}, f32[24,128]{1,0:T(8,128)S(1)}, u32[]{:S(2)}, u32[]{:S(2)}) collective-permute-start(f32[24,128]{1,0:T(8,128)} %get-tuple-element.210), channel_id=1, source_target_pairs={{0,1},{1,0},{2,3},{3,2},{4,5},{5,4},{6,7},{7,6},{8,9},{9,8},{10,11... | collective-permute-start | bytes 36872 | tf_op jit(solution)/shard_map/ppermute | solution.py:494
  219.5 15.3 %collective-permute-start.57 = (bf16[96,2304]{1,0:T(8,128)(2,1)S(1)}, bf16[96,2304]{1,0:T(8,128)(2,1)S(1)}, u32[]{:S(2)}, u32[]{:S(2)}) collective-permute-start(bf16[96,2304]{1,0:T(8,128)(2,1)S(1)} %add_convert_fusion.4), channel_id=1, source_target_pairs={{0,2},{1,5},{2,0},{3,7},{4,6},{5,1},{6,4},{7,3},{8,10},{9,13},{10,... | collective-permute-start | bytes 1327112 | tf_op jit(solution)/shard_map/ppermute | solution.py:494
  222.0 7.3 %collective-permute-start.55 = (bf16[128,768]{1,0:T(8,128)(2,1)S(1)}, bf16[128,768]{1,0:T(8,128)(2,1)S(1)}, u32[]{:S(2)}, u32[]{:S(2)}) collective-permute-start(bf16[128,768]{1,0:T(8,128)(2,1)S(1)} %slice_bitcast_fusion.2), channel_id=1, source_target_pairs={{0,1},{1,0},{2,3},{3,2},{4,5},{5,4},{6,7},{7,6},{8,9},{9,8},{10,11... | collective-permute-start | bytes 589832 | tf_op jit(solution)/shard_map/ppermute | solution.py:494
  223.5 7.7 %collective-permute-start.54 = (bf16[128,768]{1,0:T(8,128)(2,1)S(1)}, bf16[128,768]{1,0:T(8,128)(2,1)S(1)}, u32[]{:S(2)}, u32[]{:S(2)}) collective-permute-start(bf16[128,768]{1,0:T(8,128)(2,1)S(1)} %copy-done.39), channel_id=1, source_target_pairs={{0,1},{1,0},{2,3},{3,2},{4,5},{5,4},{6,7},{7,6},{8,9},{9,8},{10,11... | collective-permute-start | bytes 589832 | tf_op jit(solution)/shard_map/ppermute | solution.py:494
  224.4 3.8 %collective-permute-start.59 = (f32[24,128]{1,0:T(8,128)S(1)}, f32[24,128]{1,0:T(8,128)S(1)}, u32[]{:S(2)}, u32[]{:S(2)}) collective-permute-start(f32[24,128]{1,0:T(8,128)S(1)} %add.424), channel_id=1, source_target_pairs={{0,4},{1,5},{2,6},{3,7},{4,0},{5,1},{6,2},{7,3},{8,12},{9,13},{10,... | collective-permute-start | bytes 36872 | tf_op jit(solution)/shard_map/ppermute | solution.py:494
  228.2 13.8 %collective-permute-start.56 = (bf16[2,128,768]{2,1,0:T(8,128)(2,1)S(1)}, bf16[2,128,768]{2,1,0:T(8,128)(2,1)S(1)}, u32[]{:S(2)}, u32[]{:S(2)}) collective-permute-start(bf16[2,128,768]{2,1,0:T(8,128)(2,1)S(1)} %copy-done.30), channel_id=1, source_target_pairs={{0,2},{1,3},{2,0},{3,1},{4,6},{5,7},{6,4},{7,5},{8,10},{9,11},{10,... | collective-permute-start | bytes 1179656 | tf_op jit(solution)/shard_map/ppermute | solution.py:494
  229.3 10.9 %collective-permute-start.67 = (bf16[24,3840]{1,0:T(8,128)(2,1)S(1)}, bf16[24,3840]{1,0:T(8,128)(2,1)S(1)}, u32[]{:S(2)}, u32[]{:S(2)}) collective-permute-start(bf16[24,3840]{1,0:T(8,128)(2,1)S(1)} %pad_maximum_fusion.10), channel_id=1, source_target_pairs={{0,16},{1,17},{2,18},{3,19},{4,20},{5,21},{6,22},{7,23},{8,24},{9,... | collective-permute-start | bytes 552968 | tf_op jit(solution)/shard_map/ppermute | solution.py:494
  236.2 17.0 %collective-permute-start.64 = (bf16[48,2304]{1,0:T(8,128)(2,1)S(1)}, bf16[48,2304]{1,0:T(8,128)(2,1)S(1)}, u32[]{:S(2)}, u32[]{:S(2)}) collective-permute-start(bf16[48,2304]{1,0:T(8,128)(2,1)S(1)} %add_convert_fusion.8), channel_id=1, source_target_pairs={{0,8},{1,9},{2,10},{3,11},{4,12},{5,13},{6,14},{7,15},{8,0},{9,1},... | collective-permute-start | bytes 663560 | tf_op jit(solution)/shard_map/ppermute | solution.py:494
  242.0 3.7 %collective-permute-start.62 = (f32[24,128]{1,0:T(8,128)S(1)}, f32[24,128]{1,0:T(8,128)S(1)}, u32[]{:S(2)}, u32[]{:S(2)}) collective-permute-start(f32[24,128]{1,0:T(8,128)S(1)} %add.425), channel_id=1, source_target_pairs={{0,8},{1,9},{2,10},{3,11},{4,12},{5,13},{6,14},{7,15},{8,0},{9,1},... | collective-permute-start | bytes 36872 | tf_op jit(solution)/shard_map/ppermute | solution.py:494
  242.1 7.4 %collective-permute-start.61 = (bf16[128,768]{1,0:T(8,128)(2,1)S(1)}, bf16[128,768]{1,0:T(8,128)(2,1)S(1)}, u32[]{:S(2)}, u32[]{:S(2)}) collective-permute-start(bf16[128,768]{1,0:T(8,128)(2,1)S(1)} %slice_bitcast_fusion.1), channel_id=1, source_target_pairs={{0,1},{1,0},{2,3},{3,2},{4,5},{5,4},{6,7},{7,6},{8,9},{9,8},{10,11... | collective-permute-start | bytes 589832 | tf_op jit(solution)/shard_map/ppermute | solution.py:494
  242.1 7.3 %collective-permute-start.60 = (bf16[128,768]{1,0:T(8,128)(2,1)S(1)}, bf16[128,768]{1,0:T(8,128)(2,1)S(1)}, u32[]{:S(2)}, u32[]{:S(2)}) collective-permute-start(bf16[128,768]{1,0:T(8,128)(2,1)S(1)} %copy-done.41), channel_id=1, source_target_pairs={{0,1},{1,0},{2,3},{3,2},{4,5},{5,4},{6,7},{7,6},{8,9},{9,8},{10,11... | collective-permute-start | bytes 589832 | tf_op jit(solution)/shard_map/ppermute | solution.py:494
  245.7 3.7 %collective-permute-start.63 = (f32[24,128]{1,0:T(8,128)S(1)}, f32[24,128]{1,0:T(8,128)S(1)}, u32[]{:S(2)}, u32[]{:S(2)}) collective-permute-start(f32[24,128]{1,0:T(8,128)S(1)} %add.427), channel_id=1, source_target_pairs={{0,2},{1,3},{2,0},{3,1},{4,6},{5,7},{6,4},{7,5},{8,10},{9,11},{10,... | collective-permute-start | bytes 36872 | tf_op jit(solution)/shard_map/ppermute | solution.py:494
  254.2 4.7 %collective-permute-start.65 = (f32[24,128]{1,0:T(8,128)S(1)}, f32[24,128]{1,0:T(8,128)S(1)}, u32[]{:S(2)}, u32[]{:S(2)}) collective-permute-start(f32[24,128]{1,0:T(8,128)S(1)} %add.428), channel_id=1, source_target_pairs={{0,16},{1,17},{2,18},{3,19},{4,20},{5,21},{6,22},{7,23},{8,24},{9,... | collective-permute-start | bytes 36872 | tf_op jit(solution)/shard_map/ppermute | solution.py:494
  256.2 5.6 %collective-permute-start.66 = (bf16[24,2304]{1,0:T(8,128)(2,1)S(1)}, bf16[24,2304]{1,0:T(8,128)(2,1)S(1)}, u32[]{:S(2)}, u32[]{:S(2)}) collective-permute-start(bf16[24,2304]{1,0:T(8,128)(2,1)S(1)} %add_convert_fusion.12), channel_id=1, source_target_pairs={{0,16},{1,17},{2,18},{3,19},{4,20},{5,21},{6,22},{7,23},{8,24},{9,... | collective-permute-start | bytes 331784 | tf_op jit(solution)/shard_map/ppermute | solution.py:494
  (62 other events, 665.4 us)
